TPU v7x, 32 devices: a whole 2x2x4 slice. The times are simulated.
32 devices in a mesh: gz: 2 (over x), pr: 4 (over y, core), pc: 4 (over z).
Axes of the slice: x: 2, y: 2, z: 4, core: 2. Of those that a mesh axis runs over, the one named last changes fastest.
Arguments:
- sep_rhs: bfloat16 [4, 3, 128, 128], P('pr'), may hold values from -6 to 6
- diag_inverse: bfloat16 [4, 3, 128, 128], P('pr'), may hold values from -0.5 to 0.5
- off_blocks: bfloat16 [4, 3, 3, 4, 128, 128], P('pr', None, None, 'pc'), may hold values from -0.21875 to 0.21875
- pattern: int32 [12, 12], replicated, may hold values 0 or 1
- sub_solution: bfloat16 [2, 4, 4, 1024, 128], P('gz', 'pr', 'pc'), may hold values from -6 to 6
- couple_low: bfloat16 [2, 4, 4, 384, 1024], P('gz', 'pr', 'pc'), may hold values from -0.0625 to 0.0625
- couple_up: bfloat16 [2, 4, 4, 1024, 384], P('gz', 'pr', 'pc'), may hold values from -0.3125 to 0.3125
Outputs:
- sep_solution: bfloat16 [4, 3, 128, 128], P('pr')
- sub_result: bfloat16 [2, 4, 4, 1024, 128], P('gz', 'pr', 'pc')
Inputs may be any that keep to these rules, and one draw needn't show every extreme that they name: `pattern`: only entries [i, j] with i // 4 > j // 4 are read; 1 marks a nonzero block.
All inputs are finite; a program needn't handle non-finite values.
Results may differ from a plain program's by a relative error of at most 0.02.
Values may be sent and summed in bfloat16 or wider, within the bound.
No kernel may reach another device: no remote copies, remote signals or barrier semaphores. Data moves between devices by JAX's collectives and lax.ppermute only.
A program may use at most 64 MiB of HBM per device.

v0:
```python
import jax
import jax.numpy as jnp
from jax import lax
from jax.sharding import PartitionSpec as P


def per_device(sep_rhs, diag_inverse, off_blocks, pattern, sub_solution, couple_low, couple_up):
    row_index = lax.axis_index("pr")
    col_index = lax.axis_index("pc")
    row_count = lax.axis_size("pr")
    col_count = lax.axis_size("pc")
    inverse = diag_inverse[0]
    blocks = off_blocks[0, :, :, 0]
    levels = inverse.shape[0]
    block_width = inverse.shape[1]
    col_blocks = blocks.shape[1]
    block_count = levels * row_count
    own_sub = sub_solution[0, 0, 0]
    partial_value = jnp.dot(couple_low[0, 0, 0], own_sub, preferred_element_type=jnp.float32)
    rhs_local = sep_rhs[0].astype(jnp.float32)
    layers = lax.axis_size("gz")
    layer_index = lax.axis_index("gz")
    rhs_cols = own_sub.shape[1] // layers
    summed = lax.psum_scatter(
        partial_value.astype(jnp.bfloat16), "gz", scatter_dimension=1, tiled=True
    ).astype(jnp.float32)
    summed = lax.psum(summed, "pc")
    rhs_local = lax.dynamic_slice_in_dim(rhs_local, layer_index * rhs_cols, rhs_cols, 2)
    fed_rhs = rhs_local - summed.reshape(rhs_local.shape)
    rows_pattern = lax.dynamic_index_in_dim(
        pattern.reshape(levels, row_count, block_count), row_index, 1, keepdims=False
    )
    marks_forward = lax.dynamic_index_in_dim(
        rows_pattern.reshape(levels, col_blocks, col_count), col_index, 2, keepdims=False
    )
    cols_pattern = lax.dynamic_index_in_dim(
        jnp.transpose(pattern).reshape(levels, row_count, block_count), row_index, 1, keepdims=False
    )
    marks_backward = lax.dynamic_index_in_dim(
        cols_pattern.reshape(levels, col_blocks, col_count), col_index, 2, keepdims=False
    )
    col_levels = (jnp.arange(col_blocks, dtype=jnp.int32) * col_count + col_index) // row_count
    empty_cols = jnp.zeros((col_blocks, block_width, rhs_cols), jnp.bfloat16)

    def own_columns(level_blocks):
        flat = level_blocks.reshape(col_blocks, col_count, block_width, rhs_cols)
        return lax.dynamic_index_in_dim(flat, col_index, 1, keepdims=False)

    y_levels = jnp.zeros((levels, row_count, block_width, rhs_cols), jnp.bfloat16)
    for level in range(levels):
        if level == 0:
            residual = fed_rhs[level].astype(jnp.bfloat16)
        else:
            keep = (marks_forward[level] == 1) & (col_levels < level)
            masked = jnp.where(keep[:, None, None], own_columns(y_levels), empty_cols)
            part = jnp.einsum(
                "bst,btc->sc", blocks[level], masked, preferred_element_type=jnp.float32
            )
            total = lax.psum(part.astype(jnp.bfloat16), "pc").astype(jnp.float32)
            residual = (fed_rhs[level] - total).astype(jnp.bfloat16)
        solved = jnp.dot(inverse[level], residual, preferred_element_type=jnp.float32).astype(
            jnp.bfloat16
        )
        level_rows = lax.all_gather(solved[None], "pr", axis=0, tiled=True)
        y_levels = y_levels.at[level].set(level_rows)
    y_own = lax.dynamic_index_in_dim(y_levels, row_index, 1, keepdims=False)
    x_levels = jnp.zeros((levels, row_count, block_width, rhs_cols), jnp.bfloat16)
    for level in range(levels - 1, -1, -1):
        if level == levels - 1:
            x_levels = x_levels.at[level].set(y_levels[level])
        else:
            keep = (marks_backward[level] == 1) & (col_levels > level)
            masked = jnp.where(keep[:, None, None], own_columns(x_levels), empty_cols)
            part = jnp.einsum(
                "bst,btc->sc", blocks[level], masked, preferred_element_type=jnp.float32
            )
            total = lax.psum(part.astype(jnp.bfloat16), "pc").astype(jnp.float32)
            solved = (y_own[level].astype(jnp.float32) - total).astype(jnp.bfloat16)
            level_rows = lax.all_gather(solved[None], "pr", axis=0, tiled=True)
            x_levels = x_levels.at[level].set(level_rows)
    own_solution = lax.dynamic_index_in_dim(x_levels, row_index, 1, keepdims=False)
    own_solution = lax.all_gather(own_solution, "gz", axis=2, tiled=True)
    full_cols = own_solution.shape[2]
    removed = jnp.dot(
        couple_up[0, 0, 0],
        own_solution.reshape(levels * block_width, full_cols),
        preferred_element_type=jnp.float32,
    )
    sub_result = (own_sub.astype(jnp.float32) - removed).astype(jnp.bfloat16)
    return (own_solution[None], sub_result[None, None, None])


def solution(mesh):
    return jax.shard_map(
        per_device,
        mesh=mesh,
        in_specs=(
            P("pr", None, None, None),
            P("pr", None, None, None),
            P("pr", None, None, "pc", None, None),
            P(),
            P("gz", "pr", "pc", None, None),
            P("gz", "pr", "pc", None, None),
            P("gz", "pr", "pc", None, None),
        ),
        out_specs=(P("pr", None, None, None), P("gz", "pr", "pc", None, None)),
        check_vma=False,
    )
```

profile of v0, /device:TPU:0, one launch (start us, length us, event | category | flops | bytes accessed | tf_op | source)
XLA Modules:
  0.0 168.1 jit_solution(17526800513178852559)
XLA Ops:
  7.2 0.0 copy-start
  7.2 0.0 reduce-scatter.2.cloned.1.call-start
  7.2 0.0 copy-start.1
  7.2 2.3 %convolution_convert_fusion = bf16[384,128]{0,1:T(8,128)(2,1)} fusion(bf16[1,1,1,384,1024]{4,3,2,1,0:T(8,128)(2,1)} %param.24, bf16[1,1,1,1024,128]{4,3,2,1,0:T(8,128)(2,1)} %param.23), kind=kOutput, calls=%fused_computation.4 | convolution fusion | flops 100712448 | bytes 1146880 | tf_op jit(solution)/shard_map/dot_general | solution.py:19
  9.5 0.0 reduce-scatter.2.cloned.1.call-update
  9.5 0.0 all-reduce.4.cloned.1.call-start
  9.6 0.0 copy-done.1
  9.6 0.1 copy.23
  9.8 0.0 copy-start.4
  9.8 0.7 copy-done.4
  10.5 0.1 copy.31
  10.6 0.1 reshape.328
  10.7 0.2 fusion.66
  11.0 0.1 reshape.332
  11.0 0.2 fusion.67
  11.3 0.0 copy-start.2
  11.3 12.2 %reduce-scatter.2.cloned.1.call-done = bf16[384,64]{0,1:T(8,128)(2,1)} async-done(((bf16[384,128]{0,1:T(8,128)(2,1)}), bf16[384,64]{0,1:T(8,128)(2,1)}) %reduce-scatter.2.cloned.1.call-update) | async-done | bytes 49168 | tf_op jit(solution)/shard_map/reduce_scatter | solution.py:24
  23.5 1.4 copy_bitcast_fusion
  25.0 0.0 all-reduce.4.cloned.1.call-update
  25.0 0.0 copy-done.2
  25.0 0.1 constant_dynamic-slice_fusion.7
  25.1 0.1 copy.39
  25.2 0.0 copy-start.3
  25.2 0.0 copy-start.5
  25.2 35.5 %all-reduce.4.cloned.1.call-done = f32[3,128,64]{1,2,0:T(8,128)} async-done(((f32[3,128,64]{1,2,0:T(8,128)}), f32[3,128,64]{1,2,0:T(8,128)}) %all-reduce.4.cloned.1.call-update) | async-done | bytes 98320 | tf_op jit(solution)/shard_map/psum | solution.py:27
  60.7 0.9 bitcast_subtract_fusion
  61.6 0.0 copy-done.3
  61.6 0.1 fusion.7
  61.7 5.3 %all-gather = bf16[512,64]{0,1:T(8,128)(2,1)S(1)} all-gather(bf16[128,64]{0,1:T(8,128)(2,1)S(1)} %fusion.7), channel_id=2, replica_groups=mesh['gz'=2,'pr'=4,'pc'=4] {'pr'}, dimensions={0}, use_global_device_ids=true | all-gather | bytes 81920 | tf_op jit(solution)/shard_map/all_gather | solution.py:64
  67.1 0.0 copy-done.5
  67.1 0.2 fusion.13
  67.3 17.5 %psum.36 = bf16[128,64]{0,1:T(8,128)(2,1)S(1)} all-reduce(bf16[128,64]{0,1:T(8,128)(2,1)S(1)} %fusion.13), channel_id=1, replica_groups=mesh['gz'=2,'pr'=4,'pc'=4] {'pc'}, use_global_device_ids=true, to_apply=%region_2.3 | all-reduce | flops 8192 | bytes 32768 | tf_op jit(solution)/shard_map/psum | solution.py:59
  84.8 0.1 fusion.8
  84.9 5.3 %all-gather.1 = bf16[512,64]{0,1:T(8,128)(2,1)S(1)} all-gather(bf16[128,64]{0,1:T(8,128)(2,1)S(1)} %fusion.8), channel_id=3, replica_groups=mesh['gz'=2,'pr'=4,'pc'=4] {'pr'}, dimensions={0}, use_global_device_ids=true | all-gather | bytes 81920 | tf_op jit(solution)/shard_map/all_gather | solution.py:64
  90.3 0.2 fusion.12
  90.5 15.5 %psum.37 = bf16[128,64]{0,1:T(8,128)(2,1)S(1)} all-reduce(bf16[128,64]{0,1:T(8,128)(2,1)S(1)} %fusion.12), channel_id=1, replica_groups=mesh['gz'=2,'pr'=4,'pc'=4] {'pc'}, use_global_device_ids=true, to_apply=%region_3.4 | all-reduce | flops 8192 | bytes 32768 | tf_op jit(solution)/shard_map/psum | solution.py:59
  106.0 0.1 fusion.9
  106.1 5.3 %all-gather.2 = bf16[512,64]{0,1:T(8,128)(2,1)S(1)} all-gather(bf16[128,64]{0,1:T(8,128)(2,1)S(1)} %fusion.9), channel_id=4, replica_groups=mesh['gz'=2,'pr'=4,'pc'=4] {'pr'}, dimensions={0}, use_global_device_ids=true | all-gather | bytes 81920 | tf_op jit(solution)/shard_map/all_gather | solution.py:64
  111.5 0.2 fusion.11
  111.7 16.3 %psum.38 = bf16[128,64]{0,1:T(8,128)(2,1)S(1)} all-reduce(bf16[128,64]{0,1:T(8,128)(2,1)S(1)} %fusion.11), channel_id=1, replica_groups=mesh['gz'=2,'pr'=4,'pc'=4] {'pc'}, use_global_device_ids=true, to_apply=%region_4.5 | all-reduce | flops 8192 | bytes 32768 | tf_op jit(solution)/shard_map/psum | solution.py:77
  128.0 5.3 %all-gather.3 = bf16[512,64]{0,1:T(8,128)(2,1)S(1)} all-gather(bf16[128,64]{0,1:T(8,128)(2,1)S(1)} %fusion.42), channel_id=5, replica_groups=mesh['gz'=2,'pr'=4,'pc'=4] {'pr'}, dimensions={0}, use_global_device_ids=true | all-gather | bytes 81920 | tf_op jit(solution)/shard_map/all_gather | solution.py:79
  133.3 0.2 fusion.10
  133.5 15.5 %psum.39 = bf16[128,64]{0,1:T(8,128)(2,1)S(1)} all-reduce(bf16[128,64]{0,1:T(8,128)(2,1)S(1)} %fusion.10), channel_id=1, replica_groups=mesh['gz'=2,'pr'=4,'pc'=4] {'pc'}, use_global_device_ids=true, to_apply=%region_5.6 | all-reduce | flops 8192 | bytes 32768 | tf_op jit(solution)/shard_map/psum | solution.py:77
  149.1 5.3 %all-gather.4 = bf16[512,64]{0,1:T(8,128)(2,1)S(1)} all-gather(bf16[128,64]{0,1:T(8,128)(2,1)S(1)} %fusion.41), channel_id=6, replica_groups=mesh['gz'=2,'pr'=4,'pc'=4] {'pr'}, dimensions={0}, use_global_device_ids=true | all-gather | bytes 81920 | tf_op jit(solution)/shard_map/all_gather | solution.py:79
  154.4 4.8 %all-gather.5 = bf16[3,1,128,128]{2,3,1,0:T(8,128)(2,1)S(1)} all-gather(bf16[3,1,128,64]{2,3,1,0:T(8,128)(2,1)S(1)} %constant_dynamic-slice_fusion.2), channel_id=7, replica_groups=mesh['gz'=2,'pr'=4,'pc'=4] {'gz'}, dimensions={3}, use_global_device_ids=true | all-gather | bytes 147456 | tf_op jit(solution)/shard_map/all_gather | solution.py:82
  159.2 0.1 copy.35
  159.3 0.8 copy.36
  160.1 0.0 copy-done
  160.1 0.4 fusion.2
  160.5 0.8 copy.37
  (23 shorter events, 0.4 us)
Async XLA Ops:
  7.2 152.9 %copy-start = (bf16[1,1,1,1024,384]{4,3,2,1,0:T(8,128)(2,1)S(1)}, bf16[1,1,1,1024,384]{4,3,2,1,0:T(8,128)(2,1)}, u32[]{:S(2)}) copy-start(bf16[1,1,1,1024,384]{4,3,2,1,0:T(8,128)(2,1)} %param.25) | copy-start | bytes 2359300
  7.2 16.3 %reduce-scatter.2.cloned.1.call-start = ((), (), s32[]{:S(2)}) async-start(), calls=%async_computation.1 | async-start | bytes 147456 | tf_op jit(solution)/shard_map/reduce_scatter | solution.py:24
  7.2 2.4 %copy-start.1 = (bf16[1,1,1,1024,128]{4,3,2,1,0:T(8,128)(2,1)S(1)}, bf16[1,1,1,1024,128]{4,3,2,1,0:T(8,128)(2,1)}, u32[]{:S(2)}) copy-start(bf16[1,1,1,1024,128]{4,3,2,1,0:T(8,128)(2,1)} %param.23) | copy-start | bytes 786436
  9.5 51.2 %all-reduce.4.cloned.1.call-start = ((), (), s32[]{:S(2)}) async-start(), calls=%async_computation.2 | async-start | bytes 196608 | tf_op jit(solution)/shard_map/psum | solution.py:27
  9.8 0.7 copy-start.4
  11.3 13.7 %copy-start.2 = (bf16[1,3,128,128]{3,2,1,0:T(8,128)(2,1)S(1)}, bf16[1,3,128,128]{3,2,1,0:T(8,128)(2,1)}, u32[]{:S(2)}) copy-start(bf16[1,3,128,128]{3,2,1,0:T(8,128)(2,1)} %param.19) | copy-start | bytes 294916
  25.2 36.4 %copy-start.3 = (bf16[1,3,128,128]{3,2,1,0:T(8,128)(2,1)S(1)}, bf16[1,3,128,128]{3,2,1,0:T(8,128)(2,1)}, u32[]{:S(2)}) copy-start(bf16[1,3,128,128]{3,2,1,0:T(8,128)(2,1)} %param.20) | copy-start | bytes 294916
  25.2 41.8 %copy-start.5 = (bf16[1,3,3,1,128,128]{5,4,3,2,1,0:T(8,128)(2,1)S(1)}, bf16[1,3,3,1,128,128]{5,4,3,2,1,0:T(8,128)(2,1)}, u32[]{:S(2)}) copy-start(bf16[1,3,3,1,128,128]{5,4,3,2,1,0:T(8,128)(2,1)} %param.21) | copy-start | bytes 884740
Sparse Core Ops, SparseCore 0:
  10.8 12.6 reduce-scatter.1
  26.4 34.2 all-reduce.3
where the time goes:
time: 169 us; the launch traced here: 168 us
  blocking collectives  96 us (57%)
  waiting for transfers between devices  47.7 us (28%)
  between operations  14.3 us (8%)
  matrix products  3.84 us (2%)
  local copies, waits for them, and re-layouts  3.37 us (2%)
  other arithmetic  2.87 us (2%)
    psum x4, blocking collectives, per_device(): total = lax.psum(part.astype(jnp.bfloat16), 'pc').astype(jnp.float32)  64.9 us
    psum x1, waiting for transfers between devices, per_device(): summed = lax.psum(summed, 'pc')  35.5 us
    all_gather x5, blocking collectives, per_device(): level_rows = lax.all_gather(solved[None], 'pr', axis=0, tiled=True)  26.4 us
    reduce_scatter x1, waiting for transfers between devices, per_device(): lax.psum_scatter(partial_value.astype(jnp.bfloat16), 'gz', scatter_dimens...  12.2 us
    all_gather x1, blocking collectives, per_device(): own_solution = lax.all_gather(own_solution, 'gz', axis=2, tiled=True)  4.77 us
  transfers between devices with their start and end apart: 2, of which 2 were waited for; matrix products, arithmetic and copies ran while one was open for 1% of the time, Pallas kernels for 0%

commit v1 on v0

v1 whole, which is shorter than its diff:
```python
import jax
import jax.numpy as jnp
from jax import lax
from jax.experimental import pallas as pl
from jax.experimental.pallas import tpu as pltpu
from jax.sharding import PartitionSpec as P

FIRST, MIDDLE, LAST = range(3)
VMEM = pl.BlockSpec(memory_space=pltpu.VMEM)
SMEM = pl.BlockSpec(memory_space=pltpu.SMEM)


def dot(a, b):
    return jnp.dot(a, b, preferred_element_type=jnp.float32)


def hop(x, axis, offset):
    size = lax.axis_size(axis)
    return lax.ppermute(x, axis, [(i, i ^ offset) for i in range(size)])


def spread(x, axis):
    held = {0: x}
    bit = lax.axis_size(axis) // 2
    while bit:
        held.update({k ^ bit: hop(value, axis, bit) for k, value in list(held.items())})
        bit //= 2
    return [held[k] for k in range(len(held))]


def spread_direct(x, axis):
    return [x] + [hop(x, axis, k) for k in range(1, lax.axis_size(axis))]


def call(kernel, outs, args, scratch=(), in_specs=None):
    return pl.pallas_call(
        kernel,
        out_shape=outs,
        in_specs=in_specs or [VMEM] * len(args),
        out_specs=[VMEM] * len(outs),
        scratch_shapes=list(scratch),
        compiler_params=pltpu.CompilerParams(vmem_limit_bytes=48 * 1024 * 1024),
    )(*args)


def per_device(sep_rhs, diag_inverse, off_blocks, pattern, sub_solution, couple_low, couple_up):
    rows, cols = lax.axis_size("pr"), lax.axis_size("pc")
    rhs, inverse, blocks = sep_rhs[0], diag_inverse[0], off_blocks[0, :, :, 0]
    sub, low, up = sub_solution[0, 0, 0], couple_low[0, 0, 0], couple_up[0, 0, 0]
    levels, width, count = rhs.shape
    per = blocks.shape[1] // levels
    assert levels == 3 and per * cols == rows
    bf16, f32 = jnp.bfloat16, jnp.float32

    def shaped(*shape):
        return jax.ShapeDtypeStruct(shape, bf16)

    def start_kernel(pattern_ref, low_ref, sub_ref, blocks_ref, part_ref, mid_a_ref, mid_b_ref, last_ref, first_ref):
        row, col = lax.axis_index("pr"), lax.axis_index("pc")

        def masked(level, b):
            i, j = level * rows + row, b * cols + col
            mark = pattern_ref[i, j] if b // per < level else pattern_ref[j, i]
            return jnp.where(mark == 1, blocks_ref[level, b], jnp.zeros((width, width), bf16))

        part_ref[...] = dot(low_ref[...], sub_ref[...]).astype(bf16).reshape(levels, width, count)
        for m in range(per):
            mid_a_ref[m] = masked(MIDDLE, m)
            mid_b_ref[m] = masked(MIDDLE, LAST * per + m)
        for m in range(2 * per):
            last_ref[m] = masked(LAST, m)
            first_ref[m] = masked(FIRST, per + m)

    part, mid_a, mid_b, last, first = call(
        start_kernel,
        [shaped(levels, width, count), shaped(per, width, width), shaped(per, width, width),
         shaped(2 * per, width, width), shaped(2 * per, width, width)],
        [pattern, low, sub, blocks],
        in_specs=[SMEM, VMEM, VMEM, VMEM],
    )

    bit = 1
    while bit < lax.axis_size("gz"):
        part = part + hop(part, "gz", bit)
        bit *= 2
    parts = spread_direct(part, "pc")
    mid_a = jnp.concatenate(spread_direct(mid_a, "pc") + [inverse[MIDDLE][None]])
    mid_a = spread(mid_a, "pr")
    mid_b = spread(jnp.concatenate(spread_direct(mid_b, "pc")), "pr")
    last = spread_direct(last, "pc")
    first = spread_direct(first, "pc")

    def solve_first(rhs_ref, inverse_ref, *refs):
        out_ref, resid_ref = refs[cols:]
        for level in range(levels):
            total = sum(ref[level].astype(f32) for ref in refs[:cols])
            resid = (rhs_ref[level].astype(f32) - total).astype(bf16)
            if level == FIRST:
                out_ref[0] = dot(inverse_ref[...], resid).astype(bf16)
            elif level == MIDDLE:
                out_ref[1] = resid
            else:
                resid_ref[...] = resid

    solved, resid_last = call(
        solve_first, [shaped(2, width, count), shaped(width, count)], [rhs, inverse[FIRST], *parts]
    )
    gathered = spread(solved, "pr")

    def columns(refs_by_col, indices):
        return jnp.concatenate([ref[m] for ref in refs_by_col for m in indices], axis=1)

    def solve_forward(inverse_ref, resid_ref, *refs):
        solved_refs, mid_refs, last_refs = refs[:rows], refs[rows:2 * rows], refs[2 * rows:2 * rows + cols]
        x_last_ref, y_mid_ref, y_first_ref = refs[2 * rows + cols:]
        row, col = lax.axis_index("pr"), lax.axis_index("pc")
        for k in range(rows):
            y_first_ref[row ^ k] = solved_refs[k][0]
        y_first = [y_first_ref[m * cols + (col ^ k)] for k in range(cols) for m in range(per)]
        stacked = jnp.concatenate(y_first, axis=0)
        for k in range(rows):
            factor = jnp.concatenate([mid_refs[k][j] for j in range(cols * per)], axis=1)
            resid = (solved_refs[k][1].astype(f32) - dot(factor, stacked)).astype(bf16)
            y_mid_ref[row ^ k] = dot(mid_refs[k][cols * per], resid).astype(bf16)
        total = dot(columns(last_refs, range(per)), stacked)
        y_mid = [y_mid_ref[m * cols + (col ^ k)] for k in range(cols) for m in range(per)]
        total += dot(columns(last_refs, range(per, 2 * per)), jnp.concatenate(y_mid, axis=0))
        resid = (resid_ref[...].astype(f32) - total).astype(bf16)
        x_last_ref[...] = dot(inverse_ref[...], resid).astype(bf16)

    x_last, y_mid = call(
        solve_forward,
        [shaped(width, count), shaped(rows, width, count)],
        [inverse[LAST], resid_last, *gathered, *mid_a, *last],
        scratch=[pltpu.VMEM((rows, width, count), bf16)],
    )
    x_lasts = spread(x_last, "pr")

    def solve_backward(solved_ref, y_mid_ref, up_ref, sub_ref, *refs):
        x_last_refs, mid_refs, first_refs = refs[:rows], refs[rows:2 * rows], refs[2 * rows:2 * rows + cols]
        solution_ref, result_ref, x_last_all, x_mid_all = refs[2 * rows + cols:]
        row, col = lax.axis_index("pr"), lax.axis_index("pc")
        for k in range(rows):
            x_last_all[row ^ k] = x_last_refs[k][...]
        stacked = jnp.concatenate([x_last_all[m * cols + (col ^ k)] for k in range(cols) for m in range(per)], axis=0)
        for k in range(rows):
            factor = jnp.concatenate([mid_refs[k][j] for j in range(cols * per)], axis=1)
            x_mid_all[row ^ k] = (y_mid_ref[row ^ k].astype(f32) - dot(factor, stacked)).astype(bf16)
        x_mid = [x_mid_all[m * cols + (col ^ k)] for k in range(cols) for m in range(per)]
        total = dot(columns(first_refs, range(per, 2 * per)), stacked)
        total += dot(columns(first_refs, range(per)), jnp.concatenate(x_mid, axis=0))
        x_first = (solved_ref[0].astype(f32) - total).astype(bf16)
        solution_ref[FIRST] = x_first
        solution_ref[MIDDLE] = x_mid_all[row]
        solution_ref[LAST] = x_last_refs[0][...]
        own = solution_ref[...].reshape(levels * width, count)
        result_ref[...] = (sub_ref[...].astype(f32) - dot(up_ref[...], own)).astype(bf16)

    own_solution, result = call(
        solve_backward,
        [shaped(levels, width, count), shaped(*sub.shape)],
        [solved, y_mid, up, sub, *x_lasts, *mid_b, *first],
        scratch=[pltpu.VMEM((rows, width, count), bf16)] * 2,
    )
    return own_solution[None], result[None, None, None]


def solution(mesh):
    return jax.shard_map(
        per_device,
        mesh=mesh,
        in_specs=(
            P("pr", None, None, None),
            P("pr", None, None, None),
            P("pr", None, None, "pc", None, None),
            P(),
            P("gz", "pr", "pc", None, None),
            P("gz", "pr", "pc", None, None),
            P("gz", "pr", "pc", None, None),
        ),
        out_specs=(P("pr", None, None, None), P("gz", "pr", "pc", None, None)),
        check_vma=False,
    )
```

time: 169 us -> 54.9 us (0.32)
  blocking collectives: 96 us -> 0 us
  waiting for transfers between devices: 47.7 us -> 13.7 us
  starting transfers between devices: 0.08 us -> 32.3 us
  between operations: 14.3 us -> 0.77 us
  Pallas kernels: 0 us -> 3.96 us
  matrix products: 3.84 us -> 0 us
  other arithmetic: 2.87 us -> 0.03 us
    psum x4 -> x0, blocking collectives: 64.9 us -> none  [per_device(): total = lax.psum(part.astype(jnp.bfloat16), 'pc').astype(jnp.float32)]
    psum x1 -> x0, waiting for transfers between devices: 35.5 us -> none  [per_device(): summed = lax.psum(summed, 'pc')]
    ppermute x0 -> x28, starting transfers between devices: none -> 32.3 us  [hop(): return lax.ppermute(x, axis, [(i, i ^ offset) for i in range(size)])]
    all_gather x6 -> x0, blocking collectives: 31.1 us -> none  [the longest x5 26.4 us: per_device(): level_rows = lax.all_gather(solved[None], 'pr', axis=0, tiled=True)]
    ppermute x0 -> x28, waiting for transfers between devices: none -> 13.7 us  [hop(): return lax.ppermute(x, axis, [(i, i ^ offset) for i in range(size)])]
    reduce_scatter x1 -> x0, waiting for transfers between devices: 12.2 us -> none  [per_device(): lax.psum_scatter(partial_value.astype(jnp.bfloat16), 'gz', scatter_dimens...]
    pallas_call x0 -> x4, Pallas kernels: none -> 3.96 us  [call(): pl.pallas_call(kernel, out_shape=outs, in_specs=in_specs or [VMEM] * len(...]
    dot_general x9 -> x0, matrix products: 3.84 us -> none  [the longest x1 2.28 us: per_device(): jnp.dot(couple_low[0, 0, 0], own_sub, preferred_element_type=jnp.float32)]
  transfers between devices with their start and end apart: 2 -> 28, of which waited for: 2 -> 10; matrix products, arithmetic and copies ran while one was open for 1% -> 0% of each run, Pallas kernels for 0% -> 2%
where the time goes in v1:
time: 54.9 us; the launch traced here: 54.6 us
  starting transfers between devices  32.3 us (59%)
  waiting for transfers between devices  13.7 us (25%)
  Pallas kernels  3.96 us (7%)
  local copies, waits for them, and re-layouts  3.83 us (7%)
  between operations  0.77 us (1%)
    ppermute x28, starting transfers between devices, hop(): return lax.ppermute(x, axis, [(i, i ^ offset) for i in range(size)])  32.3 us
    ppermute x28, waiting for transfers between devices, hop(): return lax.ppermute(x, axis, [(i, i ^ offset) for i in range(size)])  13.7 us
    pallas_call x4, Pallas kernels, call(): pl.pallas_call(kernel, out_shape=outs, in_specs=in_specs or [VMEM] * len(...  3.96 us
    unnamed x23, local copies, waits for them, and re-layouts  3.81 us
  transfers between devices with their start and end apart: 28, of which 10 were waited for; matrix products, arithmetic and copies ran while one was open for 0% of the time, Pallas kernels for 2%

profile of v1, /device:TPU:0, one launch (start us, length us, event | category | flops | bytes accessed | tf_op | source)
XLA Modules:
  0.0 54.6 jit_solution(18114017207015464116)
XLA Ops:
  0.6 0.0 copy-start
  0.6 0.9 %copy-done = bf16[1,1,1,1024,128]{4,3,2,1,0:T(8,128)(2,1)S(1)} copy-done((bf16[1,1,1,1024,128]{4,3,2,1,0:T(8,128)(2,1)S(1)}, bf16[1,1,1,1024,128]{4,3,2,1,0:T(8,128)(2,1)}, u32[]{:S(2)}) %copy-start) | copy-done | bytes 262168
  1.6 1.1 %copy-done.3 = bf16[1,1,1,384,1024]{4,3,2,1,0:T(8,128)(2,1)S(1)} copy-done((bf16[1,1,1,384,1024]{4,3,2,1,0:T(8,128)(2,1)S(1)}, bf16[1,1,1,384,1024]{4,3,2,1,0:T(8,128)(2,1)}, u32[]{:S(2)}) %copy-start.3) | copy-done | bytes 786456
  2.7 1.0 %copy-done.4 = bf16[1,3,3,1,128,128]{5,4,3,2,1,0:T(8,128)(2,1)S(1)} copy-done((bf16[1,3,3,1,128,128]{5,4,3,2,1,0:T(8,128)(2,1)S(1)}, bf16[1,3,3,1,128,128]{5,4,3,2,1,0:T(8,128)(2,1)}, u32[]{:S(2)}) %copy-start.4) | copy-done | bytes 294936
  3.7 0.7 %copy-done.6 = s32[12,12]{1,0:T(8,128)S(1)} copy-done((s32[12,12]{1,0:T(8,128)S(1)}, s32[12,12]{1,0:T(8,128)}, u32[]{:S(2)}) %copy-start.6) | copy-done | bytes 600
  4.4 1.0 %shard_map.86 = (bf16[3,128,128]{2,1,0:T(8,128)(2,1)S(1)}, bf16[1,128,128]{2,1,0:T(8,128)(2,1)S(1)}, bf16[1,128,128]{2,1,0:T(8,128)(2,1)S(1)}, bf16[2,128,128]{2,1,0:T(8,128)(2,1)S(1)}, bf16[2,128,128]{2,1,0:T(8,128)(2,1)S(1)}) custom-call(s32[12,12]{1,0:T(8,128)S(1)} %copy-done.6, bf16[384,1024]{1,0:T(8,128)(2,1)S(1)} %bitcast.16, ...), custom_call_target="tpu_custom_call" | custom-call | tf_op jit(solution)/shard_map/pallas_call | solution.py:36
  5.4 3.1 %collective-permute-start.7 = (bf16[1,128,128]{2,1,0:T(8,128)(2,1)S(1)}, bf16[1,128,128]{2,1,0:T(8,128)(2,1)S(1)}, u32[]{:S(2)}, u32[]{:S(2)}) collective-permute-start(bf16[1,128,128]{2,1,0:T(8,128)(2,1)S(1)} %get-tuple-element.16), channel_id=1, source_target_pairs={{0,1},{1,0},{2,3},{3,2},{4,5},{5,4},{6,7},{7,6},{8,9},{9,8},{10,11... | collective-permute-start | bytes 98312 | tf_op jit(solution)/shard_map/ppermute | solution.py:19
  8.5 2.6 %collective-permute-start.8 = (bf16[1,128,128]{2,1,0:T(8,128)(2,1)S(1)}, bf16[1,128,128]{2,1,0:T(8,128)(2,1)S(1)}, u32[]{:S(2)}, u32[]{:S(2)}) collective-permute-start(bf16[1,128,128]{2,1,0:T(8,128)(2,1)S(1)} %get-tuple-element.16), channel_id=1, source_target_pairs={{0,2},{1,3},{2,0},{3,1},{4,6},{5,7},{6,4},{7,5},{8,10},{9,11},{10,... | collective-permute-start | bytes 98312 | tf_op jit(solution)/shard_map/ppermute | solution.py:19
  11.1 0.0 collective-permute-start.9
  11.1 0.9 %collective-permute-start.13 = (bf16[2,128,128]{2,1,0:T(8,128)(2,1)S(1)}, bf16[2,128,128]{2,1,0:T(8,128)(2,1)S(1)}, u32[]{:S(2)}, u32[]{:S(2)}) collective-permute-start(bf16[2,128,128]{2,1,0:T(8,128)(2,1)S(1)} %get-tuple-element.17.refs_8_), channel_id=1, source_target_pairs={{0,1},{1,0},{2,3},{3,2},{4,5},{5,4},{6,7},{7,6},{8,9},{9,8},{10,11... | collective-permute-start | bytes 196616 | tf_op jit(solution)/shard_map/ppermute | solution.py:19
  12.0 3.5 %collective-permute-start.14 = (bf16[2,128,128]{2,1,0:T(8,128)(2,1)S(1)}, bf16[2,128,128]{2,1,0:T(8,128)(2,1)S(1)}, u32[]{:S(2)}, u32[]{:S(2)}) collective-permute-start(bf16[2,128,128]{2,1,0:T(8,128)(2,1)S(1)} %get-tuple-element.17.refs_8_), channel_id=1, source_target_pairs={{0,2},{1,3},{2,0},{3,1},{4,6},{5,7},{6,4},{7,5},{8,10},{9,11},{10,... | collective-permute-start | bytes 196616 | tf_op jit(solution)/shard_map/ppermute | solution.py:19
  15.5 0.0 collective-permute-done.7
  15.5 0.1 collective-permute-start.19
  15.6 0.0 collective-permute-done.8
  15.6 0.6 %collective-permute-start.20 = (bf16[1,128,128]{2,1,0:T(8,128)(2,1)S(1)}, bf16[1,128,128]{2,1,0:T(8,128)(2,1)S(1)}, u32[]{:S(2)}, u32[]{:S(2)}) collective-permute-start(bf16[1,128,128]{2,1,0:T(8,128)(2,1)S(1)} %get-tuple-element.20), channel_id=1, source_target_pairs={{0,2},{1,3},{2,0},{3,1},{4,6},{5,7},{6,4},{7,5},{8,10},{9,11},{10,... | collective-permute-start | bytes 98312 | tf_op jit(solution)/shard_map/ppermute | solution.py:19
  16.2 1.0 %collective-permute-done.9 = bf16[1,128,128]{2,1,0:T(8,128)(2,1)S(1)} collective-permute-done((bf16[1,128,128]{2,1,0:T(8,128)(2,1)S(1)}, bf16[1,128,128]{2,1,0:T(8,128)(2,1)S(1)}, u32[]{:S(2)}, u32[]{:S(2)}) %collective-permute-start.9) | collective-permute-done | bytes 32800 | tf_op jit(solution)/shard_map/ppermute | solution.py:19
  17.2 2.9 %collective-permute-start.21 = (bf16[1,128,128]{2,1,0:T(8,128)(2,1)S(1)}, bf16[1,128,128]{2,1,0:T(8,128)(2,1)S(1)}, u32[]{:S(2)}, u32[]{:S(2)}) collective-permute-start(bf16[1,128,128]{2,1,0:T(8,128)(2,1)S(1)} %get-tuple-element.20), channel_id=1, source_target_pairs={{0,3},{1,2},{2,1},{3,0},{4,7},{5,6},{6,5},{7,4},{8,11},{9,10},{10,... | collective-permute-start | bytes 98312 | tf_op jit(solution)/shard_map/ppermute | solution.py:19
  20.1 0.0 collective-permute-done.19
  20.2 1.6 %collective-permute-start = (bf16[3,128,128]{2,1,0:T(8,128)(2,1)S(1)}, bf16[3,128,128]{2,1,0:T(8,128)(2,1)S(1)}, u32[]{:S(2)}, u32[]{:S(2)}) collective-permute-start(bf16[3,128,128]{2,1,0:T(8,128)(2,1)S(1)} %get-tuple-element.13), channel_id=1, source_target_pairs={{0,16},{16,0},{1,17},{17,1},{2,18},{18,2},{3,19},{19,3},{4,20},{20... | collective-permute-start | bytes 294920 | tf_op jit(solution)/shard_map/ppermute | solution.py:19
  21.7 0.0 collective-permute-done.20
  21.7 3.1 %collective-permute-done = bf16[3,128,128]{2,1,0:T(8,128)(2,1)S(1)} collective-permute-done((bf16[3,128,128]{2,1,0:T(8,128)(2,1)S(1)}, bf16[3,128,128]{2,1,0:T(8,128)(2,1)S(1)}, u32[]{:S(2)}, u32[]{:S(2)}) %collective-permute-start) | collective-permute-done | bytes 98336 | tf_op jit(solution)/shard_map/ppermute | solution.py:19
  24.9 0.0 copy-start.5
  24.9 0.1 collective-permute-start.1
  25.0 1.5 %collective-permute-start.2 = (bf16[3,128,128]{2,1,0:T(8,128)(2,1)S(1)}, bf16[3,128,128]{2,1,0:T(8,128)(2,1)S(1)}, u32[]{:S(2)}, u32[]{:S(2)}) collective-permute-start(bf16[3,128,128]{2,1,0:T(8,128)(2,1)S(1)} %add.3.refs_0_), channel_id=1, source_target_pairs={{0,2},{1,3},{2,0},{3,1},{4,6},{5,7},{6,4},{7,5},{8,10},{9,11},{10,... | collective-permute-start | bytes 294920 | tf_op jit(solution)/shard_map/ppermute | solution.py:19
  26.5 0.0 collective-permute-done.21
  26.5 2.9 %collective-permute-start.3 = (bf16[3,128,128]{2,1,0:T(8,128)(2,1)S(1)}, bf16[3,128,128]{2,1,0:T(8,128)(2,1)S(1)}, u32[]{:S(2)}, u32[]{:S(2)}) collective-permute-start(bf16[3,128,128]{2,1,0:T(8,128)(2,1)S(1)} %add.3.refs_0_), channel_id=1, source_target_pairs={{0,3},{1,2},{2,1},{3,0},{4,7},{5,6},{6,5},{7,4},{8,11},{9,10},{10,... | collective-permute-start | bytes 294920 | tf_op jit(solution)/shard_map/ppermute | solution.py:19
  29.3 0.0 collective-permute-done.13.refs_9_
  29.4 1.0 %collective-permute-start.15 = (bf16[2,128,128]{2,1,0:T(8,128)(2,1)S(1)}, bf16[2,128,128]{2,1,0:T(8,128)(2,1)S(1)}, u32[]{:S(2)}, u32[]{:S(2)}) collective-permute-start(bf16[2,128,128]{2,1,0:T(8,128)(2,1)S(1)} %get-tuple-element.17.refs_8_), channel_id=1, source_target_pairs={{0,3},{1,2},{2,1},{3,0},{4,7},{5,6},{6,5},{7,4},{8,11},{9,10},{10,... | collective-permute-start | bytes 196616 | tf_op jit(solution)/shard_map/ppermute | solution.py:19
  30.4 0.8 %collective-permute-done.1.refs_1_ = bf16[3,128,128]{2,1,0:T(8,128)(2,1)S(1)} collective-permute-done((bf16[3,128,128]{2,1,0:T(8,128)(2,1)S(1)}, bf16[3,128,128]{2,1,0:T(8,128)(2,1)S(1)}, u32[]{:S(2)}, u32[]{:S(2)}) %collective-permute-start.1) | collective-permute-done | bytes 98336 | tf_op jit(solution)/shard_map/ppermute | solution.py:19
  31.2 1.5 %collective-permute-start.11 = (bf16[5,128,128]{2,1,0:T(8,128)(2,1)S(1)}, bf16[5,128,128]{2,1,0:T(8,128)(2,1)S(1)}, u32[]{:S(2)}, u32[]{:S(2)}) collective-permute-start(bf16[5,128,128]{2,1,0:T(8,128)(2,1)S(1)} %bitcast_dynamic-update-slice_fusion.refs_4_), channel_id=1, source_target_pairs={{0,8},{4,12},{8,0},{12,4},{1,9},{5,13},{9,1},{13,5},{2,10},{6,14},... | collective-permute-start | bytes 491528 | tf_op jit(solution)/shard_map/ppermute | solution.py:19
  32.7 1.6 %collective-permute-done.2.refs_2_ = bf16[3,128,128]{2,1,0:T(8,128)(2,1)S(1)} collective-permute-done((bf16[3,128,128]{2,1,0:T(8,128)(2,1)S(1)}, bf16[3,128,128]{2,1,0:T(8,128)(2,1)S(1)}, u32[]{:S(2)}, u32[]{:S(2)}) %collective-permute-start.2) | collective-permute-done | bytes 98336 | tf_op jit(solution)/shard_map/ppermute | solution.py:19
  34.3 0.0 collective-permute-start.10
  34.3 0.0 collective-permute-done.3.refs_3_
  34.3 1.5 %collective-permute-start.23 = (bf16[4,128,128]{2,1,0:T(8,128)(2,1)S(1)}, bf16[4,128,128]{2,1,0:T(8,128)(2,1)S(1)}, u32[]{:S(2)}, u32[]{:S(2)}) collective-permute-start(bf16[4,128,128]{2,1,0:T(8,128)(2,1)S(1)} %constant_dynamic-update-slice_fusion.4.refs_4_), channel_id=1, source_target_pairs={{0,8},{4,12},{8,0},{12,4},{1,9},{5,13},{9,1},{13,5},{2,10},{6,14},... | collective-permute-start | bytes 393224 | tf_op jit(solution)/shard_map/ppermute | solution.py:19
  35.8 0.0 copy-start.2
  35.8 0.2 shard_map.87
  36.0 0.5 collective-permute-done.11.refs_6_
  36.5 0.0 collective-permute-start.12
  36.5 0.0 collective-permute-done.14.refs_10_
  36.5 1.5 %collective-permute-start.5 = (bf16[2,128,128]{2,1,0:T(8,128)(2,1)S(1)}, bf16[2,128,128]{2,1,0:T(8,128)(2,1)S(1)}, u32[]{:S(2)}, u32[]{:S(2)}) collective-permute-start(bf16[2,128,128]{2,1,0:T(8,128)(2,1)S(1)} %get-tuple-element.14.refs_0_.solved_ref), channel_id=1, source_target_pairs={{0,8},{4,12},{8,0},{12,4},{1,9},{5,13},{9,1},{13,5},{2,10},{6,14},... | collective-permute-start | bytes 196616 | tf_op jit(solution)/shard_map/ppermute | solution.py:19
  38.0 0.0 collective-permute-done.15.refs_11_
  38.0 0.2 collective-permute-start.4
  38.3 3.3 %collective-permute-done.5.refs_2_ = bf16[2,128,128]{2,1,0:T(8,128)(2,1)S(1)} collective-permute-done((bf16[2,128,128]{2,1,0:T(8,128)(2,1)S(1)}, bf16[2,128,128]{2,1,0:T(8,128)(2,1)S(1)}, u32[]{:S(2)}, u32[]{:S(2)}) %collective-permute-start.5) | collective-permute-done | bytes 65568 | tf_op jit(solution)/shard_map/ppermute | solution.py:19
  41.6 0.0 collective-permute-start.6
  41.6 0.0 collective-permute-done.23.refs_6_
  41.6 1.4 %collective-permute-start.25 = (bf16[2,128,128]{2,1,0:T(8,128)(2,1)S(1)}, bf16[2,128,128]{2,1,0:T(8,128)(2,1)S(1)}, u32[]{:S(2)}, u32[]{:S(2)}) collective-permute-start(bf16[2,128,128]{2,1,0:T(8,128)(2,1)S(1)} %get-tuple-element.21.refs_8_), channel_id=1, source_target_pairs={{0,1},{1,0},{2,3},{3,2},{4,5},{5,4},{6,7},{7,6},{8,9},{9,8},{10,11... | collective-permute-start | bytes 196616 | tf_op jit(solution)/shard_map/ppermute | solution.py:19
  43.0 0.0 collective-permute-done.10.refs_5_
  43.0 0.2 collective-permute-start.22
  43.2 0.0 collective-permute-done.4.refs_1_
  43.2 0.3 collective-permute-start.24
  43.5 0.0 collective-permute-done.6.refs_3_
  43.5 1.3 %collective-permute-start.26 = (bf16[2,128,128]{2,1,0:T(8,128)(2,1)S(1)}, bf16[2,128,128]{2,1,0:T(8,128)(2,1)S(1)}, u32[]{:S(2)}, u32[]{:S(2)}) collective-permute-start(bf16[2,128,128]{2,1,0:T(8,128)(2,1)S(1)} %get-tuple-element.21.refs_8_), channel_id=1, source_target_pairs={{0,2},{1,3},{2,0},{3,1},{4,6},{5,7},{6,4},{7,5},{8,10},{9,11},{10,... | collective-permute-start | bytes 196616 | tf_op jit(solution)/shard_map/ppermute | solution.py:19
  44.9 0.0 collective-permute-done.12.refs_7_
  44.9 1.8 %collective-permute-start.27 = (bf16[2,128,128]{2,1,0:T(8,128)(2,1)S(1)}, bf16[2,128,128]{2,1,0:T(8,128)(2,1)S(1)}, u32[]{:S(2)}, u32[]{:S(2)}) collective-permute-start(bf16[2,128,128]{2,1,0:T(8,128)(2,1)S(1)} %get-tuple-element.21.refs_8_), channel_id=1, source_target_pairs={{0,3},{1,2},{2,1},{3,0},{4,7},{5,6},{6,5},{7,4},{8,11},{9,10},{10,... | collective-permute-start | bytes 196616 | tf_op jit(solution)/shard_map/ppermute | solution.py:19
  46.6 1.2 %shard_map.88 = (bf16[128,128]{1,0:T(8,128)(2,1)S(1)}, bf16[4,128,128]{2,1,0:T(8,128)(2,1)S(1)}) custom-call(bf16[128,128]{1,0:T(8,128)(2,1)S(1)} %get-tuple-element.24.inverse_ref, bf16[128,128]{1,0:T(8,128)(2,1)S(1)} %get-tuple-element.15.resid_ref, bf16[2,128,128]{2,1,0:T(8,128)(2,1)S(1)} %get-tuple-element.14.refs_0_.solved_ref, ...), custom_call_target="tpu_custom_call" | custom-call | tf_op jit(solution)/shard_map/pallas_call | solution.py:36
  47.8 0.0 collective-permute-done.25.refs_9_
  47.8 1.6 %collective-permute-start.17 = (bf16[128,128]{1,0:T(8,128)(2,1)S(1)}, bf16[128,128]{1,0:T(8,128)(2,1)S(1)}, u32[]{:S(2)}, u32[]{:S(2)}) collective-permute-start(bf16[128,128]{1,0:T(8,128)(2,1)S(1)} %get-tuple-element.19.refs_0_), channel_id=1, source_target_pairs={{0,8},{4,12},{8,0},{12,4},{1,9},{5,13},{9,1},{13,5},{2,10},{6,14},... | collective-permute-start | bytes 98312 | tf_op jit(solution)/shard_map/ppermute | solution.py:19
  49.4 2.3 %collective-permute-done.26.refs_10_ = bf16[2,128,128]{2,1,0:T(8,128)(2,1)S(1)} collective-permute-done((bf16[2,128,128]{2,1,0:T(8,128)(2,1)S(1)}, bf16[2,128,128]{2,1,0:T(8,128)(2,1)S(1)}, u32[]{:S(2)}, u32[]{:S(2)}) %collective-permute-start.26) | collective-permute-done | bytes 65568 | tf_op jit(solution)/shard_map/ppermute | solution.py:19
  51.6 0.1 collective-permute-done.17.refs_2_
  51.8 0.4 collective-permute-start.18
  52.2 0.0 collective-permute-done.24.refs_7_
  52.2 0.7 %collective-permute-done.16.refs_1_ = bf16[128,128]{1,0:T(8,128)(2,1)S(1)} collective-permute-done((bf16[128,128]{1,0:T(8,128)(2,1)S(1)}, bf16[128,128]{1,0:T(8,128)(2,1)S(1)}, u32[]{:S(2)}, u32[]{:S(2)}) %collective-permute-start.16) | collective-permute-done | bytes 32800 | tf_op jit(solution)/shard_map/ppermute | solution.py:19
  52.8 0.2 collective-permute-done.18.refs_3_
  53.0 1.6 %shard_map.89 = (bf16[3,128,128]{2,1,0:T(8,128)(2,1)}, bf16[1024,128]{1,0:T(8,128)(2,1)}) custom-call(bf16[2,128,128]{2,1,0:T(8,128)(2,1)S(1)} %get-tuple-element.14.refs_0_.solved_ref, bf16[4,128,128]{2,1,0:T(8,128)(2,1)S(1)} %get-tuple-element.18.y_mid_ref, bf16[1024,384]{1,0:T(8,128)(2,1)S(1)} %bitcast.15, bf16[1024,128]{1,0:T(8,128)(2,1)S(1)} %bitcast.14, ...), custom_call_target="tpu_custom_call" | custom-call | tf_op jit(solution)/shard_map/pallas_call | solution.py:36
  (23 shorter events, 0.1 us)
Async XLA Ops:
  0.6 1.0 %copy-start = (bf16[1,1,1,1024,128]{4,3,2,1,0:T(8,128)(2,1)S(1)}, bf16[1,1,1,1024,128]{4,3,2,1,0:T(8,128)(2,1)}, u32[]{:S(2)}) copy-start(bf16[1,1,1,1024,128]{4,3,2,1,0:T(8,128)(2,1)} %param.11) | copy-start | bytes 786436
  1.6 1.1 %copy-start.3 = (bf16[1,1,1,384,1024]{4,3,2,1,0:T(8,128)(2,1)S(1)}, bf16[1,1,1,384,1024]{4,3,2,1,0:T(8,128)(2,1)}, u32[]{:S(2)}) copy-start(bf16[1,1,1,384,1024]{4,3,2,1,0:T(8,128)(2,1)} %param.12) | copy-start | bytes 2359300
  2.7 1.0 %copy-start.4 = (bf16[1,3,3,1,128,128]{5,4,3,2,1,0:T(8,128)(2,1)S(1)}, bf16[1,3,3,1,128,128]{5,4,3,2,1,0:T(8,128)(2,1)}, u32[]{:S(2)}) copy-start(bf16[1,3,3,1,128,128]{5,4,3,2,1,0:T(8,128)(2,1)} %param.9) | copy-start | bytes 884740
  3.7 0.7 %copy-start.6 = (s32[12,12]{1,0:T(8,128)S(1)}, s32[12,12]{1,0:T(8,128)}, u32[]{:S(2)}) copy-start(s32[12,12]{1,0:T(8,128)} %pattern_ref.1) | copy-start | bytes 1732
  5.4 10.1 %collective-permute-start.7 = (bf16[1,128,128]{2,1,0:T(8,128)(2,1)S(1)}, bf16[1,128,128]{2,1,0:T(8,128)(2,1)S(1)}, u32[]{:S(2)}, u32[]{:S(2)}) collective-permute-start(bf16[1,128,128]{2,1,0:T(8,128)(2,1)S(1)} %get-tuple-element.16), channel_id=1, source_target_pairs={{0,1},{1,0},{2,3},{3,2},{4,5},{5,4},{6,7},{7,6},{8,9},{9,8},{10,11... | collective-permute-start | bytes 98312 | tf_op jit(solution)/shard_map/ppermute | solution.py:19
  8.5 7.1 %collective-permute-start.8 = (bf16[1,128,128]{2,1,0:T(8,128)(2,1)S(1)}, bf16[1,128,128]{2,1,0:T(8,128)(2,1)S(1)}, u32[]{:S(2)}, u32[]{:S(2)}) collective-permute-start(bf16[1,128,128]{2,1,0:T(8,128)(2,1)S(1)} %get-tuple-element.16), channel_id=1, source_target_pairs={{0,2},{1,3},{2,0},{3,1},{4,6},{5,7},{6,4},{7,5},{8,10},{9,11},{10,... | collective-permute-start | bytes 98312 | tf_op jit(solution)/shard_map/ppermute | solution.py:19
  11.1 6.2 %collective-permute-start.9 = (bf16[1,128,128]{2,1,0:T(8,128)(2,1)S(1)}, bf16[1,128,128]{2,1,0:T(8,128)(2,1)S(1)}, u32[]{:S(2)}, u32[]{:S(2)}) collective-permute-start(bf16[1,128,128]{2,1,0:T(8,128)(2,1)S(1)} %get-tuple-element.16), channel_id=1, source_target_pairs={{0,3},{1,2},{2,1},{3,0},{4,7},{5,6},{6,5},{7,4},{8,11},{9,10},{10,... | collective-permute-start | bytes 98312 | tf_op jit(solution)/shard_map/ppermute | solution.py:19
  11.1 18.3 %collective-permute-start.13 = (bf16[2,128,128]{2,1,0:T(8,128)(2,1)S(1)}, bf16[2,128,128]{2,1,0:T(8,128)(2,1)S(1)}, u32[]{:S(2)}, u32[]{:S(2)}) collective-permute-start(bf16[2,128,128]{2,1,0:T(8,128)(2,1)S(1)} %get-tuple-element.17.refs_8_), channel_id=1, source_target_pairs={{0,1},{1,0},{2,3},{3,2},{4,5},{5,4},{6,7},{7,6},{8,9},{9,8},{10,11... | collective-permute-start | bytes 196616 | tf_op jit(solution)/shard_map/ppermute | solution.py:19
  12.0 24.5 %collective-permute-start.14 = (bf16[2,128,128]{2,1,0:T(8,128)(2,1)S(1)}, bf16[2,128,128]{2,1,0:T(8,128)(2,1)S(1)}, u32[]{:S(2)}, u32[]{:S(2)}) collective-permute-start(bf16[2,128,128]{2,1,0:T(8,128)(2,1)S(1)} %get-tuple-element.17.refs_8_), channel_id=1, source_target_pairs={{0,2},{1,3},{2,0},{3,1},{4,6},{5,7},{6,4},{7,5},{8,10},{9,11},{10,... | collective-permute-start | bytes 196616 | tf_op jit(solution)/shard_map/ppermute | solution.py:19
  15.5 4.6 %copy-start.7 = (bf16[1,3,128,128]{3,2,1,0:T(8,128)(2,1)S(1)}, bf16[1,3,128,128]{3,2,1,0:T(8,128)(2,1)}, u32[]{:S(2)}) copy-start(bf16[1,3,128,128]{3,2,1,0:T(8,128)(2,1)} %param.8) | copy-start | bytes 294916
  15.5 4.6 %collective-permute-start.19 = (bf16[1,128,128]{2,1,0:T(8,128)(2,1)S(1)}, bf16[1,128,128]{2,1,0:T(8,128)(2,1)S(1)}, u32[]{:S(2)}, u32[]{:S(2)}) collective-permute-start(bf16[1,128,128]{2,1,0:T(8,128)(2,1)S(1)} %get-tuple-element.20), channel_id=1, source_target_pairs={{0,1},{1,0},{2,3},{3,2},{4,5},{5,4},{6,7},{7,6},{8,9},{9,8},{10,11... | collective-permute-start | bytes 98312 | tf_op jit(solution)/shard_map/ppermute | solution.py:19
  15.6 6.1 %collective-permute-start.20 = (bf16[1,128,128]{2,1,0:T(8,128)(2,1)S(1)}, bf16[1,128,128]{2,1,0:T(8,128)(2,1)S(1)}, u32[]{:S(2)}, u32[]{:S(2)}) collective-permute-start(bf16[1,128,128]{2,1,0:T(8,128)(2,1)S(1)} %get-tuple-element.20), channel_id=1, source_target_pairs={{0,2},{1,3},{2,0},{3,1},{4,6},{5,7},{6,4},{7,5},{8,10},{9,11},{10,... | collective-permute-start | bytes 98312 | tf_op jit(solution)/shard_map/ppermute | solution.py:19
  17.2 9.2 %collective-permute-start.21 = (bf16[1,128,128]{2,1,0:T(8,128)(2,1)S(1)}, bf16[1,128,128]{2,1,0:T(8,128)(2,1)S(1)}, u32[]{:S(2)}, u32[]{:S(2)}) collective-permute-start(bf16[1,128,128]{2,1,0:T(8,128)(2,1)S(1)} %get-tuple-element.20), channel_id=1, source_target_pairs={{0,3},{1,2},{2,1},{3,0},{4,7},{5,6},{6,5},{7,4},{8,11},{9,10},{10,... | collective-permute-start | bytes 98312 | tf_op jit(solution)/shard_map/ppermute | solution.py:19
  20.2 4.7 %collective-permute-start = (bf16[3,128,128]{2,1,0:T(8,128)(2,1)S(1)}, bf16[3,128,128]{2,1,0:T(8,128)(2,1)S(1)}, u32[]{:S(2)}, u32[]{:S(2)}) collective-permute-start(bf16[3,128,128]{2,1,0:T(8,128)(2,1)S(1)} %get-tuple-element.13), channel_id=1, source_target_pairs={{0,16},{16,0},{1,17},{17,1},{2,18},{18,2},{3,19},{19,3},{4,20},{20... | collective-permute-start | bytes 294920 | tf_op jit(solution)/shard_map/ppermute | solution.py:19
  24.9 11.0 %copy-start.5 = (bf16[1,3,128,128]{3,2,1,0:T(8,128)(2,1)S(1)}, bf16[1,3,128,128]{3,2,1,0:T(8,128)(2,1)}, u32[]{:S(2)}) copy-start(bf16[1,3,128,128]{3,2,1,0:T(8,128)(2,1)} %param.7) | copy-start | bytes 294916
  24.9 6.3 %collective-permute-start.1 = (bf16[3,128,128]{2,1,0:T(8,128)(2,1)S(1)}, bf16[3,128,128]{2,1,0:T(8,128)(2,1)S(1)}, u32[]{:S(2)}, u32[]{:S(2)}) collective-permute-start(bf16[3,128,128]{2,1,0:T(8,128)(2,1)S(1)} %add.3.refs_0_), channel_id=1, source_target_pairs={{0,1},{1,0},{2,3},{3,2},{4,5},{5,4},{6,7},{7,6},{8,9},{9,8},{10,11... | collective-permute-start | bytes 294920 | tf_op jit(solution)/shard_map/ppermute | solution.py:19
  25.0 9.3 %collective-permute-start.2 = (bf16[3,128,128]{2,1,0:T(8,128)(2,1)S(1)}, bf16[3,128,128]{2,1,0:T(8,128)(2,1)S(1)}, u32[]{:S(2)}, u32[]{:S(2)}) collective-permute-start(bf16[3,128,128]{2,1,0:T(8,128)(2,1)S(1)} %add.3.refs_0_), channel_id=1, source_target_pairs={{0,2},{1,3},{2,0},{3,1},{4,6},{5,7},{6,4},{7,5},{8,10},{9,11},{10,... | collective-permute-start | bytes 294920 | tf_op jit(solution)/shard_map/ppermute | solution.py:19
  26.5 7.8 %collective-permute-start.3 = (bf16[3,128,128]{2,1,0:T(8,128)(2,1)S(1)}, bf16[3,128,128]{2,1,0:T(8,128)(2,1)S(1)}, u32[]{:S(2)}, u32[]{:S(2)}) collective-permute-start(bf16[3,128,128]{2,1,0:T(8,128)(2,1)S(1)} %add.3.refs_0_), channel_id=1, source_target_pairs={{0,3},{1,2},{2,1},{3,0},{4,7},{5,6},{6,5},{7,4},{8,11},{9,10},{10,... | collective-permute-start | bytes 294920 | tf_op jit(solution)/shard_map/ppermute | solution.py:19
  29.4 8.7 %collective-permute-start.15 = (bf16[2,128,128]{2,1,0:T(8,128)(2,1)S(1)}, bf16[2,128,128]{2,1,0:T(8,128)(2,1)S(1)}, u32[]{:S(2)}, u32[]{:S(2)}) collective-permute-start(bf16[2,128,128]{2,1,0:T(8,128)(2,1)S(1)} %get-tuple-element.17.refs_8_), channel_id=1, source_target_pairs={{0,3},{1,2},{2,1},{3,0},{4,7},{5,6},{6,5},{7,4},{8,11},{9,10},{10,... | collective-permute-start | bytes 196616 | tf_op jit(solution)/shard_map/ppermute | solution.py:19
  31.2 5.3 %collective-permute-start.11 = (bf16[5,128,128]{2,1,0:T(8,128)(2,1)S(1)}, bf16[5,128,128]{2,1,0:T(8,128)(2,1)S(1)}, u32[]{:S(2)}, u32[]{:S(2)}) collective-permute-start(bf16[5,128,128]{2,1,0:T(8,128)(2,1)S(1)} %bitcast_dynamic-update-slice_fusion.refs_4_), channel_id=1, source_target_pairs={{0,8},{4,12},{8,0},{12,4},{1,9},{5,13},{9,1},{13,5},{2,10},{6,14},... | collective-permute-start | bytes 491528 | tf_op jit(solution)/shard_map/ppermute | solution.py:19
  34.3 8.7 %collective-permute-start.10 = (bf16[5,128,128]{2,1,0:T(8,128)(2,1)S(1)}, bf16[5,128,128]{2,1,0:T(8,128)(2,1)S(1)}, u32[]{:S(2)}, u32[]{:S(2)}) collective-permute-start(bf16[5,128,128]{2,1,0:T(8,128)(2,1)S(1)} %bitcast_dynamic-update-slice_fusion.refs_4_), channel_id=1, source_target_pairs={{0,4},{4,0},{8,12},{12,8},{1,5},{5,1},{9,13},{13,9},{2,6},{6,2},{1... | collective-permute-start | bytes 491528 | tf_op jit(solution)/shard_map/ppermute | solution.py:19
  34.3 7.3 %collective-permute-start.23 = (bf16[4,128,128]{2,1,0:T(8,128)(2,1)S(1)}, bf16[4,128,128]{2,1,0:T(8,128)(2,1)S(1)}, u32[]{:S(2)}, u32[]{:S(2)}) collective-permute-start(bf16[4,128,128]{2,1,0:T(8,128)(2,1)S(1)} %constant_dynamic-update-slice_fusion.4.refs_4_), channel_id=1, source_target_pairs={{0,8},{4,12},{8,0},{12,4},{1,9},{5,13},{9,1},{13,5},{2,10},{6,14},... | collective-permute-start | bytes 393224 | tf_op jit(solution)/shard_map/ppermute | solution.py:19
  35.8 17.2 %copy-start.2 = (bf16[1,1,1,1024,384]{4,3,2,1,0:T(8,128)(2,1)S(1)}, bf16[1,1,1,1024,384]{4,3,2,1,0:T(8,128)(2,1)}, u32[]{:S(2)}) copy-start(bf16[1,1,1,1024,384]{4,3,2,1,0:T(8,128)(2,1)} %param.13) | copy-start | bytes 2359300
  36.5 8.3 %collective-permute-start.12 = (bf16[5,128,128]{2,1,0:T(8,128)(2,1)S(1)}, bf16[5,128,128]{2,1,0:T(8,128)(2,1)S(1)}, u32[]{:S(2)}, u32[]{:S(2)}) collective-permute-start(bf16[5,128,128]{2,1,0:T(8,128)(2,1)S(1)} %collective-permute-done.11.refs_6_), channel_id=1, source_target_pairs={{0,4},{4,0},{8,12},{12,8},{1,5},{5,1},{9,13},{13,9},{2,6},{6,2},{1... | collective-permute-start | bytes 491528 | tf_op jit(solution)/shard_map/ppermute | solution.py:19
  36.5 5.1 %collective-permute-start.5 = (bf16[2,128,128]{2,1,0:T(8,128)(2,1)S(1)}, bf16[2,128,128]{2,1,0:T(8,128)(2,1)S(1)}, u32[]{:S(2)}, u32[]{:S(2)}) collective-permute-start(bf16[2,128,128]{2,1,0:T(8,128)(2,1)S(1)} %get-tuple-element.14.refs_0_.solved_ref), channel_id=1, source_target_pairs={{0,8},{4,12},{8,0},{12,4},{1,9},{5,13},{9,1},{13,5},{2,10},{6,14},... | collective-permute-start | bytes 196616 | tf_op jit(solution)/shard_map/ppermute | solution.py:19
  38.0 5.2 %collective-permute-start.4 = (bf16[2,128,128]{2,1,0:T(8,128)(2,1)S(1)}, bf16[2,128,128]{2,1,0:T(8,128)(2,1)S(1)}, u32[]{:S(2)}, u32[]{:S(2)}) collective-permute-start(bf16[2,128,128]{2,1,0:T(8,128)(2,1)S(1)} %get-tuple-element.14.refs_0_.solved_ref), channel_id=1, source_target_pairs={{0,4},{4,0},{8,12},{12,8},{1,5},{5,1},{9,13},{13,9},{2,6},{6,2},{1... | collective-permute-start | bytes 196616 | tf_op jit(solution)/shard_map/ppermute | solution.py:19
  41.6 1.9 %collective-permute-start.6 = (bf16[2,128,128]{2,1,0:T(8,128)(2,1)S(1)}, bf16[2,128,128]{2,1,0:T(8,128)(2,1)S(1)}, u32[]{:S(2)}, u32[]{:S(2)}) collective-permute-start(bf16[2,128,128]{2,1,0:T(8,128)(2,1)S(1)} %collective-permute-done.5.refs_2_), channel_id=1, source_target_pairs={{0,4},{4,0},{8,12},{12,8},{1,5},{5,1},{9,13},{13,9},{2,6},{6,2},{1... | collective-permute-start | bytes 196616 | tf_op jit(solution)/shard_map/ppermute | solution.py:19
  41.6 6.2 %collective-permute-start.25 = (bf16[2,128,128]{2,1,0:T(8,128)(2,1)S(1)}, bf16[2,128,128]{2,1,0:T(8,128)(2,1)S(1)}, u32[]{:S(2)}, u32[]{:S(2)}) collective-permute-start(bf16[2,128,128]{2,1,0:T(8,128)(2,1)S(1)} %get-tuple-element.21.refs_8_), channel_id=1, source_target_pairs={{0,1},{1,0},{2,3},{3,2},{4,5},{5,4},{6,7},{7,6},{8,9},{9,8},{10,11... | collective-permute-start | bytes 196616 | tf_op jit(solution)/shard_map/ppermute | solution.py:19
  43.0 9.2 %collective-permute-start.22 = (bf16[4,128,128]{2,1,0:T(8,128)(2,1)S(1)}, bf16[4,128,128]{2,1,0:T(8,128)(2,1)S(1)}, u32[]{:S(2)}, u32[]{:S(2)}) collective-permute-start(bf16[4,128,128]{2,1,0:T(8,128)(2,1)S(1)} %constant_dynamic-update-slice_fusion.4.refs_4_), channel_id=1, source_target_pairs={{0,4},{4,0},{8,12},{12,8},{1,5},{5,1},{9,13},{13,9},{2,6},{6,2},{1... | collective-permute-start | bytes 393224 | tf_op jit(solution)/shard_map/ppermute | solution.py:19
  43.2 8.9 %collective-permute-start.24 = (bf16[4,128,128]{2,1,0:T(8,128)(2,1)S(1)}, bf16[4,128,128]{2,1,0:T(8,128)(2,1)S(1)}, u32[]{:S(2)}, u32[]{:S(2)}) collective-permute-start(bf16[4,128,128]{2,1,0:T(8,128)(2,1)S(1)} %collective-permute-done.23.refs_6_), channel_id=1, source_target_pairs={{0,4},{4,0},{8,12},{12,8},{1,5},{5,1},{9,13},{13,9},{2,6},{6,2},{1... | collective-permute-start | bytes 393224 | tf_op jit(solution)/shard_map/ppermute | solution.py:19
  43.5 8.1 %collective-permute-start.26 = (bf16[2,128,128]{2,1,0:T(8,128)(2,1)S(1)}, bf16[2,128,128]{2,1,0:T(8,128)(2,1)S(1)}, u32[]{:S(2)}, u32[]{:S(2)}) collective-permute-start(bf16[2,128,128]{2,1,0:T(8,128)(2,1)S(1)} %get-tuple-element.21.refs_8_), channel_id=1, source_target_pairs={{0,2},{1,3},{2,0},{3,1},{4,6},{5,7},{6,4},{7,5},{8,10},{9,11},{10,... | collective-permute-start | bytes 196616 | tf_op jit(solution)/shard_map/ppermute | solution.py:19
  44.9 7.3 %collective-permute-start.27 = (bf16[2,128,128]{2,1,0:T(8,128)(2,1)S(1)}, bf16[2,128,128]{2,1,0:T(8,128)(2,1)S(1)}, u32[]{:S(2)}, u32[]{:S(2)}) collective-permute-start(bf16[2,128,128]{2,1,0:T(8,128)(2,1)S(1)} %get-tuple-element.21.refs_8_), channel_id=1, source_target_pairs={{0,3},{1,2},{2,1},{3,0},{4,7},{5,6},{6,5},{7,4},{8,11},{9,10},{10,... | collective-permute-start | bytes 196616 | tf_op jit(solution)/shard_map/ppermute | solution.py:19
  46.6 6.4 %copy-start.1 = (bf16[1,1,1,1024,128]{4,3,2,1,0:T(8,128)(2,1)S(1)}, bf16[1,1,1,1024,128]{4,3,2,1,0:T(8,128)(2,1)}, u32[]{:S(2)}) copy-start(bf16[1,1,1,1024,128]{4,3,2,1,0:T(8,128)(2,1)} %param.11) | copy-start | bytes 786436
  47.8 4.0 %collective-permute-start.17 = (bf16[128,128]{1,0:T(8,128)(2,1)S(1)}, bf16[128,128]{1,0:T(8,128)(2,1)S(1)}, u32[]{:S(2)}, u32[]{:S(2)}) collective-permute-start(bf16[128,128]{1,0:T(8,128)(2,1)S(1)} %get-tuple-element.19.refs_0_), channel_id=1, source_target_pairs={{0,8},{4,12},{8,0},{12,4},{1,9},{5,13},{9,1},{13,5},{2,10},{6,14},... | collective-permute-start | bytes 98312 | tf_op jit(solution)/shard_map/ppermute | solution.py:19
  51.6 1.2 %collective-permute-start.16 = (bf16[128,128]{1,0:T(8,128)(2,1)S(1)}, bf16[128,128]{1,0:T(8,128)(2,1)S(1)}, u32[]{:S(2)}, u32[]{:S(2)}) collective-permute-start(bf16[128,128]{1,0:T(8,128)(2,1)S(1)} %get-tuple-element.19.refs_0_), channel_id=1, source_target_pairs={{0,4},{4,0},{8,12},{12,8},{1,5},{5,1},{9,13},{13,9},{2,6},{6,2},{1... | collective-permute-start | bytes 98312 | tf_op jit(solution)/shard_map/ppermute | solution.py:19
  51.8 1.2 %collective-permute-start.18 = (bf16[128,128]{1,0:T(8,128)(2,1)S(1)}, bf16[128,128]{1,0:T(8,128)(2,1)S(1)}, u32[]{:S(2)}, u32[]{:S(2)}) collective-permute-start(bf16[128,128]{1,0:T(8,128)(2,1)S(1)} %collective-permute-done.17.refs_2_), channel_id=1, source_target_pairs={{0,4},{4,0},{8,12},{12,8},{1,5},{5,1},{9,13},{13,9},{2,6},{6,2},{1... | collective-permute-start | bytes 98312 | tf_op jit(solution)/shard_map/ppermute | solution.py:19

commit v2 on v1

v2 whole, which is shorter than its diff:
```python
import jax
import jax.numpy as jnp
from jax import lax
from jax.experimental import pallas as pl
from jax.experimental.pallas import tpu as pltpu
from jax.sharding import PartitionSpec as P

FIRST, MIDDLE, LAST = range(3)
VMEM = pl.BlockSpec(memory_space=pltpu.VMEM)
SMEM = pl.BlockSpec(memory_space=pltpu.SMEM)


def dot(a, b):
    return jnp.dot(a, b, preferred_element_type=jnp.float32)


def hop(x, axis, offset):
    size = lax.axis_size(axis)
    return lax.ppermute(x, axis, [(i, i ^ offset) for i in range(size)])


def offsets(axis):
    order, bit = [0], lax.axis_size(axis) // 2
    while bit:
        order += [k ^ bit for k in order]
        bit //= 2
    return order


def gather(x, axis):
    bit = lax.axis_size(axis) // 2
    while bit:
        x = jnp.concatenate([x, hop(x, axis, bit)])
        bit //= 2
    return x


def after(x, *others):
    return lax.optimization_barrier((x, *others))[0]


def spread_direct(x, axis):
    return [x] + [hop(x, axis, k) for k in range(1, lax.axis_size(axis))]


def call(kernel, outs, args, scratch=(), in_specs=None):
    return pl.pallas_call(
        kernel,
        out_shape=outs,
        in_specs=in_specs or [VMEM] * len(args),
        out_specs=[VMEM] * len(outs),
        scratch_shapes=list(scratch),
        compiler_params=pltpu.CompilerParams(vmem_limit_bytes=48 * 1024 * 1024),
    )(*args)


def per_device(sep_rhs, diag_inverse, off_blocks, pattern, sub_solution, couple_low, couple_up):
    rows, cols = lax.axis_size("pr"), lax.axis_size("pc")
    rhs, inverse, blocks = sep_rhs[0], diag_inverse[0], off_blocks[0, :, :, 0]
    sub, low, up = sub_solution[0, 0, 0], couple_low[0, 0, 0], couple_up[0, 0, 0]
    levels, width, count = rhs.shape
    per = blocks.shape[1] // levels
    assert levels == 3 and per * cols == rows
    bf16, f32 = jnp.bfloat16, jnp.float32

    def shaped(*shape):
        return jax.ShapeDtypeStruct(shape, bf16)

    mid_size, row_order, col_order = 2 * per, offsets("pr"), offsets("pc")

    def couple_kernel(low_ref, sub_ref, part_ref):
        part_ref[...] = dot(low_ref[...], sub_ref[...]).astype(bf16).reshape(levels, width, count)

    (part,) = call(couple_kernel, [shaped(levels, width, count)], [low, sub])

    def mask_kernel(pattern_ref, blocks_ref, mid_ref, rest_ref):
        row, col = lax.axis_index("pr"), lax.axis_index("pc")

        def masked(level, b):
            i, j = level * rows + row, b * cols + col
            mark = pattern_ref[i, j] if b // per < level else pattern_ref[j, i]
            return jnp.where(mark == 1, blocks_ref[level, b], jnp.zeros((width, width), bf16))

        for m in range(per):
            mid_ref[m] = masked(MIDDLE, m)
            mid_ref[per + m] = masked(MIDDLE, LAST * per + m)
        for m in range(2 * per):
            rest_ref[m] = masked(LAST, m)
            rest_ref[2 * per + m] = masked(FIRST, per + m)

    mid, rest = call(
        mask_kernel,
        [shaped(2 * per, width, width), shaped(4 * per, width, width)],
        [pattern, blocks],
        in_specs=[SMEM, VMEM],
    )

    bit = 1
    while bit < lax.axis_size("gz"):
        part = part + hop(part, "gz", bit)
        bit *= 2
    parts = [part] + [hop(part, "pc", k) for k in range(cols - 1, 0, -1)]
    mid = jnp.concatenate([mid, hop(mid, "pc", 2)])
    mid = after(mid, part)
    mid = jnp.concatenate([mid, hop(mid, "pc", 1)])
    mid = gather(jnp.concatenate([mid, inverse[MIDDLE][None]]), "pr")
    rest = jnp.concatenate([rest, hop(rest, "pc", 2)])
    rest = after(rest, part)
    rest = jnp.concatenate([rest, hop(rest, "pc", 1)])

    def solve_first(rhs_ref, inverse_ref, *refs):
        out_ref, resid_ref = refs[cols:]
        for level in range(levels):
            total = sum(ref[level].astype(f32) for ref in refs[:cols])
            resid = (rhs_ref[level].astype(f32) - total).astype(bf16)
            if level == FIRST:
                out_ref[0] = dot(inverse_ref[...], resid).astype(bf16)
            elif level == MIDDLE:
                out_ref[1] = resid
            else:
                resid_ref[...] = resid

    solved, resid_last = call(
        solve_first, [shaped(2, width, count), shaped(width, count)], [rhs, inverse[FIRST], *parts]
    )
    gathered = gather(solved, "pr")

    mid_stride = cols * mid_size + 1

    def mid_factor(mid_ref, n, upper):
        picks = [n * mid_stride + c * mid_size + upper * per + m for c in range(cols) for m in range(per)]
        return jnp.concatenate([mid_ref[pick] for pick in picks], axis=1)

    def row_factor(ref, half):
        picks = [c * 4 * per + half * per + m for c in range(cols) for m in range(per)]
        return jnp.concatenate([ref[pick] for pick in picks], axis=1)

    def stack(ref, col):
        return jnp.concatenate([ref[m * cols + (col ^ k)] for k in col_order for m in range(per)], axis=0)

    def solve_forward(inverse_ref, resid_ref, gathered_ref, mid_ref, last_ref, x_last_ref, y_mid_ref, y_first_ref):
        row, col = lax.axis_index("pr"), lax.axis_index("pc")
        for n, k in enumerate(row_order):
            y_first_ref[row ^ k] = gathered_ref[2 * n]
        y_first = stack(y_first_ref, col)
        for n, k in enumerate(row_order):
            resid = (gathered_ref[2 * n + 1].astype(f32) - dot(mid_factor(mid_ref, n, 0), y_first)).astype(bf16)
            y_mid_ref[row ^ k] = dot(mid_ref[n * mid_stride + cols * mid_size], resid).astype(bf16)
        total = dot(row_factor(last_ref, 0), y_first) + dot(row_factor(last_ref, 1), stack(y_mid_ref, col))
        resid = (resid_ref[...].astype(f32) - total).astype(bf16)
        x_last_ref[0] = dot(inverse_ref[...], resid).astype(bf16)

    x_last, y_mid = call(
        solve_forward,
        [shaped(1, width, count), shaped(rows, width, count)],
        [inverse[LAST], resid_last, gathered, mid, rest],
        scratch=[pltpu.VMEM((rows, width, count), bf16)],
    )
    x_lasts = gather(x_last, "pr")

    def solve_backward(solved_ref, y_mid_ref, up_ref, sub_ref, x_lasts_ref, mid_ref, first_ref,
                       solution_ref, result_ref, x_last_all, x_mid_all):
        row, col = lax.axis_index("pr"), lax.axis_index("pc")
        for n, k in enumerate(row_order):
            x_last_all[row ^ k] = x_lasts_ref[n]
        x_last = stack(x_last_all, col)
        for n, k in enumerate(row_order):
            total = dot(mid_factor(mid_ref, n, 1), x_last)
            x_mid_all[row ^ k] = (y_mid_ref[row ^ k].astype(f32) - total).astype(bf16)
        total = dot(row_factor(first_ref, 3), x_last) + dot(row_factor(first_ref, 2), stack(x_mid_all, col))
        solution_ref[FIRST] = (solved_ref[0].astype(f32) - total).astype(bf16)
        solution_ref[MIDDLE] = x_mid_all[row]
        solution_ref[LAST] = x_lasts_ref[0]
        own = solution_ref[...].reshape(levels * width, count)
        result_ref[...] = (sub_ref[...].astype(f32) - dot(up_ref[...], own)).astype(bf16)

    own_solution, result = call(
        solve_backward,
        [shaped(levels, width, count), shaped(*sub.shape)],
        [solved, y_mid, up, sub, x_lasts, mid, rest],
        scratch=[pltpu.VMEM((rows, width, count), bf16)] * 2,
    )
    return own_solution[None], result[None, None, None]


def solution(mesh):
    return jax.shard_map(
        per_device,
        mesh=mesh,
        in_specs=(
            P("pr", None, None, None),
            P("pr", None, None, None),
            P("pr", None, None, "pc", None, None),
            P(),
            P("gz", "pr", "pc", None, None),
            P("gz", "pr", "pc", None, None),
            P("gz", "pr", "pc", None, None),
        ),
        out_specs=(P("pr", None, None, None), P("gz", "pr", "pc", None, None)),
        check_vma=False,
    )
```

time: 54.9 us -> 42.5 us (0.77)
  starting transfers between devices: 32.3 us -> 17.4 us
  waiting for transfers between devices: 13.7 us -> 15.7 us
    ppermute x28 -> x14, starting transfers between devices: 32.3 us -> 17.4 us  [hop(): return lax.ppermute(x, axis, [(i, i ^ offset) for i in range(size)])]
    ppermute x28 -> x14, waiting for transfers between devices: 13.7 us -> 15.7 us  [hop(): return lax.ppermute(x, axis, [(i, i ^ offset) for i in range(size)])]
    pallas_call x4 -> x5, Pallas kernels: 3.96 us -> 4.03 us  [call(): pl.pallas_call(kernel, out_shape=outs, in_specs=in_specs or [VMEM] * len(...]
    unnamed x23 -> x21, local copies, waits for them, and re-layouts: 3.81 us -> 3.85 us
  transfers between devices with their start and end apart: 28 -> 14, of which waited for: 10 -> 8; matrix products, arithmetic and copies ran while one was open for 0% -> 1% of each run, Pallas kernels for 2% -> 1%
where the time goes in v2:
time: 42.5 us; the launch traced here: 42.2 us
  starting transfers between devices  17.4 us (41%)
  waiting for transfers between devices  15.7 us (37%)
  Pallas kernels  4.03 us (9%)
  local copies, waits for them, and re-layouts  3.98 us (9%)
  between operations  0.85 us (2%)
    ppermute x14, starting transfers between devices, hop(): return lax.ppermute(x, axis, [(i, i ^ offset) for i in range(size)])  17.4 us
    ppermute x14, waiting for transfers between devices, hop(): return lax.ppermute(x, axis, [(i, i ^ offset) for i in range(size)])  15.7 us
    pallas_call x5, Pallas kernels, call(): pl.pallas_call(kernel, out_shape=outs, in_specs=in_specs or [VMEM] * len(...  4.03 us
    unnamed x21, local copies, waits for them, and re-layouts  3.85 us
  transfers between devices with their start and end apart: 14, of which 8 were waited for; matrix products, arithmetic and copies ran while one was open for 1% of the time, Pallas kernels for 1%

profile of v2, /device:TPU:0, one launch (start us, length us, event | category | flops | bytes accessed | tf_op | source)
XLA Modules:
  0.0 42.2 jit_solution(1403798999313739385)
XLA Ops:
  0.6 0.0 copy-start.4
  0.6 1.0 %copy-done.4 = bf16[1,3,3,1,128,128]{5,4,3,2,1,0:T(8,128)(2,1)S(1)} copy-done((bf16[1,3,3,1,128,128]{5,4,3,2,1,0:T(8,128)(2,1)S(1)}, bf16[1,3,3,1,128,128]{5,4,3,2,1,0:T(8,128)(2,1)}, u32[]{:S(2)}) %copy-start.4) | copy-done | bytes 294936
  1.6 0.0 copy-start.6
  1.6 0.7 %copy-done.6 = s32[12,12]{1,0:T(8,128)S(1)} copy-done((s32[12,12]{1,0:T(8,128)S(1)}, s32[12,12]{1,0:T(8,128)}, u32[]{:S(2)}) %copy-start.6) | copy-done | bytes 600
  2.3 0.0 copy-start.7
  2.3 0.7 %shard_map.88 = (bf16[2,128,128]{2,1,0:T(8,128)(2,1)S(1)}, bf16[4,128,128]{2,1,0:T(8,128)(2,1)S(1)}) custom-call(s32[12,12]{1,0:T(8,128)S(1)} %copy-done.6, bf16[3,3,128,128]{3,2,1,0:T(8,128)(2,1)S(1)} %bitcast.19), custom_call_target="tpu_custom_call" | custom-call | tf_op jit(solution)/shard_map/pallas_call | solution.py:47
  3.0 4.1 %collective-permute-start.6 = (bf16[2,128,128]{2,1,0:T(8,128)(2,1)S(1)}, bf16[2,128,128]{2,1,0:T(8,128)(2,1)S(1)}, u32[]{:S(2)}, u32[]{:S(2)}) collective-permute-start(bf16[2,128,128]{2,1,0:T(8,128)(2,1)S(1)} %get-tuple-element.14), channel_id=1, source_target_pairs={{0,2},{1,3},{2,0},{3,1},{4,6},{5,7},{6,4},{7,5},{8,10},{9,11},{10,... | collective-permute-start | bytes 196616 | tf_op jit(solution)/shard_map/ppermute | solution.py:19
  7.1 0.0 copy-start
  7.1 0.9 %copy-done = bf16[1,1,1,1024,128]{4,3,2,1,0:T(8,128)(2,1)S(1)} copy-done((bf16[1,1,1,1024,128]{4,3,2,1,0:T(8,128)(2,1)S(1)}, bf16[1,1,1,1024,128]{4,3,2,1,0:T(8,128)(2,1)}, u32[]{:S(2)}) %copy-start) | copy-done | bytes 262168
  8.1 0.0 copy-start.2
  8.1 1.1 %copy-done.2 = bf16[1,1,1,384,1024]{4,3,2,1,0:T(8,128)(2,1)S(1)} copy-done((bf16[1,1,1,384,1024]{4,3,2,1,0:T(8,128)(2,1)S(1)}, bf16[1,1,1,384,1024]{4,3,2,1,0:T(8,128)(2,1)}, u32[]{:S(2)}) %copy-start.2) | copy-done | bytes 786456
  9.2 0.4 shard_map.86
  9.6 1.6 %collective-permute-start = (bf16[3,128,128]{2,1,0:T(8,128)(2,1)S(1)}, bf16[3,128,128]{2,1,0:T(8,128)(2,1)S(1)}, u32[]{:S(2)}, u32[]{:S(2)}) collective-permute-start(bf16[3,128,128]{2,1,0:T(8,128)(2,1)S(1)} %shard_map.86), channel_id=1, source_target_pairs={{0,16},{16,0},{1,17},{17,1},{2,18},{18,2},{3,19},{19,3},{4,20},{20... | collective-permute-start | bytes 294920 | tf_op jit(solution)/shard_map/ppermute | solution.py:19
  11.1 0.3 collective-permute-start.10
  11.5 0.0 collective-permute-done.6
  11.5 0.0 copy-start.5
  11.5 2.8 %collective-permute-done = bf16[3,128,128]{2,1,0:T(8,128)(2,1)S(1)} collective-permute-done((bf16[3,128,128]{2,1,0:T(8,128)(2,1)S(1)}, bf16[3,128,128]{2,1,0:T(8,128)(2,1)S(1)}, u32[]{:S(2)}, u32[]{:S(2)}) %collective-permute-start) | collective-permute-done | bytes 98336 | tf_op jit(solution)/shard_map/ppermute | solution.py:19
  14.3 1.6 %collective-permute-start.7 = (bf16[4,128,128]{2,1,0:T(8,128)(2,1)S(1)}, bf16[4,128,128]{2,1,0:T(8,128)(2,1)S(1)}, u32[]{:S(2)}, u32[]{:S(2)}) collective-permute-start(bf16[4,128,128]{2,1,0:T(8,128)(2,1)S(1)} %pad_maximum_fusion.5), channel_id=1, source_target_pairs={{0,1},{1,0},{2,3},{3,2},{4,5},{5,4},{6,7},{7,6},{8,9},{9,8},{10,11... | collective-permute-start | bytes 393224 | tf_op jit(solution)/shard_map/ppermute | solution.py:19
  15.9 0.0 copy-done.7
  16.0 0.1 collective-permute-start.1
  16.0 1.9 %collective-permute-start.2 = (bf16[3,128,128]{2,1,0:T(8,128)(2,1)S(1)}, bf16[3,128,128]{2,1,0:T(8,128)(2,1)S(1)}, u32[]{:S(2)}, u32[]{:S(2)}) collective-permute-start(bf16[3,128,128]{2,1,0:T(8,128)(2,1)S(1)} %add.3.refs_0_), channel_id=1, source_target_pairs={{0,2},{1,3},{2,0},{3,1},{4,6},{5,7},{6,4},{7,5},{8,10},{9,11},{10,... | collective-permute-start | bytes 294920 | tf_op jit(solution)/shard_map/ppermute | solution.py:19
  17.9 2.5 %collective-permute-start.3 = (bf16[3,128,128]{2,1,0:T(8,128)(2,1)S(1)}, bf16[3,128,128]{2,1,0:T(8,128)(2,1)S(1)}, u32[]{:S(2)}, u32[]{:S(2)}) collective-permute-start(bf16[3,128,128]{2,1,0:T(8,128)(2,1)S(1)} %add.3.refs_0_), channel_id=1, source_target_pairs={{0,1},{1,0},{2,3},{3,2},{4,5},{5,4},{6,7},{7,6},{8,9},{9,8},{10,11... | collective-permute-start | bytes 294920 | tf_op jit(solution)/shard_map/ppermute | solution.py:19
  20.4 1.6 %collective-permute-done.7 = bf16[4,128,128]{2,1,0:T(8,128)(2,1)S(1)} collective-permute-done((bf16[4,128,128]{2,1,0:T(8,128)(2,1)S(1)}, bf16[4,128,128]{2,1,0:T(8,128)(2,1)S(1)}, u32[]{:S(2)}, u32[]{:S(2)}) %collective-permute-start.7) | collective-permute-done | bytes 131104 | tf_op jit(solution)/shard_map/ppermute | solution.py:19
  22.0 1.6 %collective-permute-start.8 = (bf16[9,128,128]{2,1,0:T(8,128)(2,1)S(1)}, bf16[9,128,128]{2,1,0:T(8,128)(2,1)S(1)}, u32[]{:S(2)}, u32[]{:S(2)}) collective-permute-start(bf16[9,128,128]{2,1,0:T(8,128)(2,1)S(1)} %pad_maximum_fusion.1), channel_id=1, source_target_pairs={{0,8},{4,12},{8,0},{12,4},{1,9},{5,13},{9,1},{13,5},{2,10},{6,14},... | collective-permute-start | bytes 884744 | tf_op jit(solution)/shard_map/ppermute | solution.py:19
  23.6 0.0 collective-permute-done.10
  23.6 0.5 %collective-permute-start.11 = (bf16[8,128,128]{2,1,0:T(8,128)(2,1)S(1)}, bf16[8,128,128]{2,1,0:T(8,128)(2,1)S(1)}, u32[]{:S(2)}, u32[]{:S(2)}) collective-permute-start(bf16[8,128,128]{2,1,0:T(8,128)(2,1)S(1)} %pad_maximum_fusion.3), channel_id=1, source_target_pairs={{0,1},{1,0},{2,3},{3,2},{4,5},{5,4},{6,7},{7,6},{8,9},{9,8},{10,11... | collective-permute-start | bytes 786440 | tf_op jit(solution)/shard_map/ppermute | solution.py:19
  24.1 0.3 collective-permute-done.1.refs_1_
  24.4 3.6 %collective-permute-done.2.refs_2_ = bf16[3,128,128]{2,1,0:T(8,128)(2,1)S(1)} collective-permute-done((bf16[3,128,128]{2,1,0:T(8,128)(2,1)S(1)}, bf16[3,128,128]{2,1,0:T(8,128)(2,1)S(1)}, u32[]{:S(2)}, u32[]{:S(2)}) %collective-permute-start.2) | collective-permute-done | bytes 98336 | tf_op jit(solution)/shard_map/ppermute | solution.py:19
  28.0 0.0 collective-permute-done.3.refs_3_
  28.0 0.0 copy-done.5
  28.0 0.2 shard_map.87
  28.2 1.5 %collective-permute-start.4 = (bf16[2,128,128]{2,1,0:T(8,128)(2,1)S(1)}, bf16[2,128,128]{2,1,0:T(8,128)(2,1)S(1)}, u32[]{:S(2)}, u32[]{:S(2)}) collective-permute-start(bf16[2,128,128]{2,1,0:T(8,128)(2,1)S(1)} %get-tuple-element.12.solved_ref), channel_id=1, source_target_pairs={{0,8},{4,12},{8,0},{12,4},{1,9},{5,13},{9,1},{13,5},{2,10},{6,14},... | collective-permute-start | bytes 196616 | tf_op jit(solution)/shard_map/ppermute | solution.py:19
  29.7 0.0 collective-permute-done.8
  29.7 0.1 pad_maximum_fusion
  29.8 0.1 collective-permute-start.9
  29.9 2.6 %collective-permute-done.4 = bf16[2,128,128]{2,1,0:T(8,128)(2,1)S(1)} collective-permute-done((bf16[2,128,128]{2,1,0:T(8,128)(2,1)S(1)}, bf16[2,128,128]{2,1,0:T(8,128)(2,1)S(1)}, u32[]{:S(2)}, u32[]{:S(2)}) %collective-permute-start.4) | collective-permute-done | bytes 65568 | tf_op jit(solution)/shard_map/ppermute | solution.py:19
  32.5 0.1 collective-permute-start.5
  32.6 1.3 %collective-permute-done.5 = bf16[4,128,128]{2,1,0:T(8,128)(2,1)S(1)} collective-permute-done((bf16[4,128,128]{2,1,0:T(8,128)(2,1)S(1)}, bf16[4,128,128]{2,1,0:T(8,128)(2,1)S(1)}, u32[]{:S(2)}, u32[]{:S(2)}) %collective-permute-start.5) | collective-permute-done | bytes 131104 | tf_op jit(solution)/shard_map/ppermute | solution.py:19
  33.9 0.0 collective-permute-done.11
  34.0 0.0 collective-permute-done.9
  34.0 0.1 constant_dynamic-update-slice_fusion.mid_ref
  34.1 0.0 copy-start.1
  34.1 0.0 copy-start.3
  34.1 1.2 %shard_map.89 = (bf16[1,128,128]{2,1,0:T(8,128)(2,1)S(1)}, bf16[4,128,128]{2,1,0:T(8,128)(2,1)S(1)}) custom-call(bf16[128,128]{1,0:T(8,128)(2,1)S(1)} %get-tuple-element.24.inverse_ref, bf16[128,128]{1,0:T(8,128)(2,1)S(1)} %get-tuple-element.13.resid_ref, bf16[8,128,128]{2,1,0:T(8,128)(2,1)S(1)} %pad_maximum_fusion.2.gathered_ref, ...), custom_call_target="tpu_custom_call" | custom-call | tf_op jit(solution)/shard_map/pallas_call | solution.py:47
  35.3 1.5 %collective-permute-start.12 = (bf16[1,128,128]{2,1,0:T(8,128)(2,1)S(1)}, bf16[1,128,128]{2,1,0:T(8,128)(2,1)S(1)}, u32[]{:S(2)}, u32[]{:S(2)}) collective-permute-start(bf16[1,128,128]{2,1,0:T(8,128)(2,1)S(1)} %get-tuple-element.19), channel_id=1, source_target_pairs={{0,8},{4,12},{8,0},{12,4},{1,9},{5,13},{9,1},{13,5},{2,10},{6,14},... | collective-permute-start | bytes 98312 | tf_op jit(solution)/shard_map/ppermute | solution.py:19
  36.9 2.4 %collective-permute-done.12 = bf16[1,128,128]{2,1,0:T(8,128)(2,1)S(1)} collective-permute-done((bf16[1,128,128]{2,1,0:T(8,128)(2,1)S(1)}, bf16[1,128,128]{2,1,0:T(8,128)(2,1)S(1)}, u32[]{:S(2)}, u32[]{:S(2)}) %collective-permute-start.12) | collective-permute-done | bytes 32800 | tf_op jit(solution)/shard_map/ppermute | solution.py:19
  39.3 0.1 collective-permute-start.13
  39.3 1.2 %collective-permute-done.13 = bf16[2,128,128]{2,1,0:T(8,128)(2,1)S(1)} collective-permute-done((bf16[2,128,128]{2,1,0:T(8,128)(2,1)S(1)}, bf16[2,128,128]{2,1,0:T(8,128)(2,1)S(1)}, u32[]{:S(2)}, u32[]{:S(2)}) %collective-permute-start.13) | collective-permute-done | bytes 65568 | tf_op jit(solution)/shard_map/ppermute | solution.py:19
  40.6 0.0 copy-done.1
  40.6 0.0 copy-done.3
  40.6 1.6 %shard_map.90 = (bf16[3,128,128]{2,1,0:T(8,128)(2,1)}, bf16[1024,128]{1,0:T(8,128)(2,1)}) custom-call(bf16[2,128,128]{2,1,0:T(8,128)(2,1)S(1)} %get-tuple-element.12.solved_ref, bf16[4,128,128]{2,1,0:T(8,128)(2,1)S(1)} %get-tuple-element.18.y_mid_ref, bf16[1024,384]{1,0:T(8,128)(2,1)S(1)} %bitcast.18, bf16[1024,128]{1,0:T(8,128)(2,1)S(1)} %bitcast.16, ...), custom_call_target="tpu_custom_call" | custom-call | tf_op jit(solution)/shard_map/pallas_call | solution.py:47
  (15 shorter events, 0.3 us)
Async XLA Ops:
  0.6 1.0 %copy-start.4 = (bf16[1,3,3,1,128,128]{5,4,3,2,1,0:T(8,128)(2,1)S(1)}, bf16[1,3,3,1,128,128]{5,4,3,2,1,0:T(8,128)(2,1)}, u32[]{:S(2)}) copy-start(bf16[1,3,3,1,128,128]{5,4,3,2,1,0:T(8,128)(2,1)} %param.9) | copy-start | bytes 884740
  1.6 0.7 %copy-start.6 = (s32[12,12]{1,0:T(8,128)S(1)}, s32[12,12]{1,0:T(8,128)}, u32[]{:S(2)}) copy-start(s32[12,12]{1,0:T(8,128)} %pattern_ref.1) | copy-start | bytes 1732
  2.3 13.6 %copy-start.7 = (bf16[1,3,128,128]{3,2,1,0:T(8,128)(2,1)S(1)}, bf16[1,3,128,128]{3,2,1,0:T(8,128)(2,1)}, u32[]{:S(2)}) copy-start(bf16[1,3,128,128]{3,2,1,0:T(8,128)(2,1)} %param.8) | copy-start | bytes 294916
  3.0 8.5 %collective-permute-start.6 = (bf16[2,128,128]{2,1,0:T(8,128)(2,1)S(1)}, bf16[2,128,128]{2,1,0:T(8,128)(2,1)S(1)}, u32[]{:S(2)}, u32[]{:S(2)}) collective-permute-start(bf16[2,128,128]{2,1,0:T(8,128)(2,1)S(1)} %get-tuple-element.14), channel_id=1, source_target_pairs={{0,2},{1,3},{2,0},{3,1},{4,6},{5,7},{6,4},{7,5},{8,10},{9,11},{10,... | collective-permute-start | bytes 196616 | tf_op jit(solution)/shard_map/ppermute | solution.py:19
  7.1 0.9 %copy-start = (bf16[1,1,1,1024,128]{4,3,2,1,0:T(8,128)(2,1)S(1)}, bf16[1,1,1,1024,128]{4,3,2,1,0:T(8,128)(2,1)}, u32[]{:S(2)}) copy-start(bf16[1,1,1,1024,128]{4,3,2,1,0:T(8,128)(2,1)} %param.11) | copy-start | bytes 786436
  8.1 1.1 %copy-start.2 = (bf16[1,1,1,384,1024]{4,3,2,1,0:T(8,128)(2,1)S(1)}, bf16[1,1,1,384,1024]{4,3,2,1,0:T(8,128)(2,1)}, u32[]{:S(2)}) copy-start(bf16[1,1,1,384,1024]{4,3,2,1,0:T(8,128)(2,1)} %param.12) | copy-start | bytes 2359300
  9.6 4.7 %collective-permute-start = (bf16[3,128,128]{2,1,0:T(8,128)(2,1)S(1)}, bf16[3,128,128]{2,1,0:T(8,128)(2,1)S(1)}, u32[]{:S(2)}, u32[]{:S(2)}) collective-permute-start(bf16[3,128,128]{2,1,0:T(8,128)(2,1)S(1)} %shard_map.86), channel_id=1, source_target_pairs={{0,16},{16,0},{1,17},{17,1},{2,18},{18,2},{3,19},{19,3},{4,20},{20... | collective-permute-start | bytes 294920 | tf_op jit(solution)/shard_map/ppermute | solution.py:19
  11.1 12.5 %collective-permute-start.10 = (bf16[4,128,128]{2,1,0:T(8,128)(2,1)S(1)}, bf16[4,128,128]{2,1,0:T(8,128)(2,1)S(1)}, u32[]{:S(2)}, u32[]{:S(2)}) collective-permute-start(bf16[4,128,128]{2,1,0:T(8,128)(2,1)S(1)} %get-tuple-element.16), channel_id=1, source_target_pairs={{0,2},{1,3},{2,0},{3,1},{4,6},{5,7},{6,4},{7,5},{8,10},{9,11},{10,... | collective-permute-start | bytes 393224 | tf_op jit(solution)/shard_map/ppermute | solution.py:19
  11.5 16.5 %copy-start.5 = (bf16[1,3,128,128]{3,2,1,0:T(8,128)(2,1)S(1)}, bf16[1,3,128,128]{3,2,1,0:T(8,128)(2,1)}, u32[]{:S(2)}) copy-start(bf16[1,3,128,128]{3,2,1,0:T(8,128)(2,1)} %param.7) | copy-start | bytes 294916
  14.3 7.7 %collective-permute-start.7 = (bf16[4,128,128]{2,1,0:T(8,128)(2,1)S(1)}, bf16[4,128,128]{2,1,0:T(8,128)(2,1)S(1)}, u32[]{:S(2)}, u32[]{:S(2)}) collective-permute-start(bf16[4,128,128]{2,1,0:T(8,128)(2,1)S(1)} %pad_maximum_fusion.5), channel_id=1, source_target_pairs={{0,1},{1,0},{2,3},{3,2},{4,5},{5,4},{6,7},{7,6},{8,9},{9,8},{10,11... | collective-permute-start | bytes 393224 | tf_op jit(solution)/shard_map/ppermute | solution.py:19
  16.0 8.5 %collective-permute-start.1 = (bf16[3,128,128]{2,1,0:T(8,128)(2,1)S(1)}, bf16[3,128,128]{2,1,0:T(8,128)(2,1)S(1)}, u32[]{:S(2)}, u32[]{:S(2)}) collective-permute-start(bf16[3,128,128]{2,1,0:T(8,128)(2,1)S(1)} %add.3.refs_0_), channel_id=1, source_target_pairs={{0,3},{1,2},{2,1},{3,0},{4,7},{5,6},{6,5},{7,4},{8,11},{9,10},{10,... | collective-permute-start | bytes 294920 | tf_op jit(solution)/shard_map/ppermute | solution.py:19
  16.0 12.0 %collective-permute-start.2 = (bf16[3,128,128]{2,1,0:T(8,128)(2,1)S(1)}, bf16[3,128,128]{2,1,0:T(8,128)(2,1)S(1)}, u32[]{:S(2)}, u32[]{:S(2)}) collective-permute-start(bf16[3,128,128]{2,1,0:T(8,128)(2,1)S(1)} %add.3.refs_0_), channel_id=1, source_target_pairs={{0,2},{1,3},{2,0},{3,1},{4,6},{5,7},{6,4},{7,5},{8,10},{9,11},{10,... | collective-permute-start | bytes 294920 | tf_op jit(solution)/shard_map/ppermute | solution.py:19
  17.9 10.1 %collective-permute-start.3 = (bf16[3,128,128]{2,1,0:T(8,128)(2,1)S(1)}, bf16[3,128,128]{2,1,0:T(8,128)(2,1)S(1)}, u32[]{:S(2)}, u32[]{:S(2)}) collective-permute-start(bf16[3,128,128]{2,1,0:T(8,128)(2,1)S(1)} %add.3.refs_0_), channel_id=1, source_target_pairs={{0,1},{1,0},{2,3},{3,2},{4,5},{5,4},{6,7},{7,6},{8,9},{9,8},{10,11... | collective-permute-start | bytes 294920 | tf_op jit(solution)/shard_map/ppermute | solution.py:19
  22.0 7.7 %collective-permute-start.8 = (bf16[9,128,128]{2,1,0:T(8,128)(2,1)S(1)}, bf16[9,128,128]{2,1,0:T(8,128)(2,1)S(1)}, u32[]{:S(2)}, u32[]{:S(2)}) collective-permute-start(bf16[9,128,128]{2,1,0:T(8,128)(2,1)S(1)} %pad_maximum_fusion.1), channel_id=1, source_target_pairs={{0,8},{4,12},{8,0},{12,4},{1,9},{5,13},{9,1},{13,5},{2,10},{6,14},... | collective-permute-start | bytes 884744 | tf_op jit(solution)/shard_map/ppermute | solution.py:19
  23.6 10.3 %collective-permute-start.11 = (bf16[8,128,128]{2,1,0:T(8,128)(2,1)S(1)}, bf16[8,128,128]{2,1,0:T(8,128)(2,1)S(1)}, u32[]{:S(2)}, u32[]{:S(2)}) collective-permute-start(bf16[8,128,128]{2,1,0:T(8,128)(2,1)S(1)} %pad_maximum_fusion.3), channel_id=1, source_target_pairs={{0,1},{1,0},{2,3},{3,2},{4,5},{5,4},{6,7},{7,6},{8,9},{9,8},{10,11... | collective-permute-start | bytes 786440 | tf_op jit(solution)/shard_map/ppermute | solution.py:19
  28.2 4.3 %collective-permute-start.4 = (bf16[2,128,128]{2,1,0:T(8,128)(2,1)S(1)}, bf16[2,128,128]{2,1,0:T(8,128)(2,1)S(1)}, u32[]{:S(2)}, u32[]{:S(2)}) collective-permute-start(bf16[2,128,128]{2,1,0:T(8,128)(2,1)S(1)} %get-tuple-element.12.solved_ref), channel_id=1, source_target_pairs={{0,8},{4,12},{8,0},{12,4},{1,9},{5,13},{9,1},{13,5},{2,10},{6,14},... | collective-permute-start | bytes 196616 | tf_op jit(solution)/shard_map/ppermute | solution.py:19
  29.8 4.2 %collective-permute-start.9 = (bf16[18,128,128]{2,1,0:T(8,128)(2,1)S(1)}, bf16[18,128,128]{2,1,0:T(8,128)(2,1)S(1)}, u32[]{:S(2)}, u32[]{:S(2)}) collective-permute-start(bf16[18,128,128]{2,1,0:T(8,128)(2,1)S(1)} %pad_maximum_fusion), channel_id=1, source_target_pairs={{0,4},{4,0},{8,12},{12,8},{1,5},{5,1},{9,13},{13,9},{2,6},{6,2},{1... | collective-permute-start | bytes 1769480 | tf_op jit(solution)/shard_map/ppermute | solution.py:19
  32.5 1.4 %collective-permute-start.5 = (bf16[4,128,128]{2,1,0:T(8,128)(2,1)S(1)}, bf16[4,128,128]{2,1,0:T(8,128)(2,1)S(1)}, u32[]{:S(2)}, u32[]{:S(2)}) collective-permute-start(bf16[4,128,128]{2,1,0:T(8,128)(2,1)S(1)} %pad_maximum_fusion.4), channel_id=1, source_target_pairs={{0,4},{4,0},{8,12},{12,8},{1,5},{5,1},{9,13},{13,9},{2,6},{6,2},{1... | collective-permute-start | bytes 393224 | tf_op jit(solution)/shard_map/ppermute | solution.py:19
  34.1 6.5 %copy-start.1 = (bf16[1,1,1,1024,128]{4,3,2,1,0:T(8,128)(2,1)S(1)}, bf16[1,1,1,1024,128]{4,3,2,1,0:T(8,128)(2,1)}, u32[]{:S(2)}) copy-start(bf16[1,1,1,1024,128]{4,3,2,1,0:T(8,128)(2,1)} %param.11) | copy-start | bytes 786436
  34.1 6.5 %copy-start.3 = (bf16[1,1,1,1024,384]{4,3,2,1,0:T(8,128)(2,1)S(1)}, bf16[1,1,1,1024,384]{4,3,2,1,0:T(8,128)(2,1)}, u32[]{:S(2)}) copy-start(bf16[1,1,1,1024,384]{4,3,2,1,0:T(8,128)(2,1)} %param.13) | copy-start | bytes 2359300
  35.3 3.9 %collective-permute-start.12 = (bf16[1,128,128]{2,1,0:T(8,128)(2,1)S(1)}, bf16[1,128,128]{2,1,0:T(8,128)(2,1)S(1)}, u32[]{:S(2)}, u32[]{:S(2)}) collective-permute-start(bf16[1,128,128]{2,1,0:T(8,128)(2,1)S(1)} %get-tuple-element.19), channel_id=1, source_target_pairs={{0,8},{4,12},{8,0},{12,4},{1,9},{5,13},{9,1},{13,5},{2,10},{6,14},... | collective-permute-start | bytes 98312 | tf_op jit(solution)/shard_map/ppermute | solution.py:19
  39.3 1.3 %collective-permute-start.13 = (bf16[2,128,128]{2,1,0:T(8,128)(2,1)S(1)}, bf16[2,128,128]{2,1,0:T(8,128)(2,1)S(1)}, u32[]{:S(2)}, u32[]{:S(2)}) collective-permute-start(bf16[2,128,128]{2,1,0:T(8,128)(2,1)S(1)} %pad_maximum_fusion.7), channel_id=1, source_target_pairs={{0,4},{4,0},{8,12},{12,8},{1,5},{5,1},{9,13},{13,9},{2,6},{6,2},{1... | collective-permute-start | bytes 196616 | tf_op jit(solution)/shard_map/ppermute | solution.py:19

commit v3 on v2

v3 whole, which is shorter than its diff:
```python
import jax
import jax.numpy as jnp
from jax import lax
from jax.experimental import pallas as pl
from jax.experimental.pallas import tpu as pltpu
from jax.sharding import PartitionSpec as P

FIRST, MIDDLE, LAST = range(3)
VMEM = pl.BlockSpec(memory_space=pltpu.VMEM)
SMEM = pl.BlockSpec(memory_space=pltpu.SMEM)


def dot(a, b):
    return jnp.dot(a, b, preferred_element_type=jnp.float32)


def hop(x, axis, offset):
    size = lax.axis_size(axis)
    return lax.ppermute(x, axis, [(i, i ^ offset) for i in range(size)])


def far_to_near(axis):
    bit = lax.axis_size(axis) // 2
    while bit:
        yield bit
        bit //= 2


def offsets(axis):
    order = [0]
    for bit in far_to_near(axis):
        order += [k ^ bit for k in order]
    return order


def far_half(x, axis):
    return jnp.concatenate([x, hop(x, axis, lax.axis_size(axis) // 2)])


def near_half(x, axis):
    for bit in list(far_to_near(axis))[1:]:
        x = jnp.concatenate([x, hop(x, axis, bit)])
    return x


def gather(x, axis):
    return near_half(far_half(x, axis), axis)


def gather_direct(x, axis):
    got = {k: hop(x, axis, k) for k in range(lax.axis_size(axis) - 1, 0, -1)}
    return jnp.concatenate([x] + [got[k] for k in offsets(axis)[1:]])


def after(x, *others):
    return lax.optimization_barrier((x, *others))[0]


def call(kernel, outs, args, scratch=(), in_specs=None):
    return pl.pallas_call(
        kernel,
        out_shape=outs,
        in_specs=in_specs or [VMEM] * len(args),
        out_specs=[VMEM] * len(outs),
        scratch_shapes=list(scratch),
        compiler_params=pltpu.CompilerParams(vmem_limit_bytes=48 * 1024 * 1024),
    )(*args)


def per_device(sep_rhs, diag_inverse, off_blocks, pattern, sub_solution, couple_low, couple_up):
    rows, cols = lax.axis_size("pr"), lax.axis_size("pc")
    rhs, inverse, blocks = sep_rhs[0], diag_inverse[0], off_blocks[0, :, :, 0]
    sub, low, up = sub_solution[0, 0, 0], couple_low[0, 0, 0], couple_up[0, 0, 0]
    levels, width, count = rhs.shape
    per = blocks.shape[1] // levels
    assert levels == 3 and per * cols == rows
    bf16, f32 = jnp.bfloat16, jnp.float32

    def shaped(*shape):
        return jax.ShapeDtypeStruct(shape, bf16)

    row_order, col_order = offsets("pr"), offsets("pc")


    def couple_kernel(low_ref, sub_ref, part_ref, kept_ref):
        kept_ref[...] = sub_ref[...]
        part_ref[...] = dot(low_ref[...], sub_ref[...]).astype(bf16).reshape(levels, width, count)

    part, kept = call(couple_kernel, [shaped(levels, width, count), shaped(*sub.shape)], [low, sub])

    def mask_kernel(pattern_ref, inverse_ref, blocks_ref, early_ref, late_ref, column_ref):
        row, col = lax.axis_index("pr"), lax.axis_index("pc")

        def masked(level, b):
            i, j = level * rows + row, b * cols + col
            mark = pattern_ref[i, j] if b // per < level else pattern_ref[j, i]
            return jnp.where(mark == 1, blocks_ref[level, b], jnp.zeros((width, width), bf16))

        for m in range(per):
            to_first, to_last = masked(MIDDLE, m), masked(MIDDLE, LAST * per + m)
            early_ref[m] = masked(LAST, MIDDLE * per + m)
            early_ref[per + m] = masked(FIRST, MIDDLE * per + m)
            late_ref[m] = masked(LAST, m)
            late_ref[per + m] = masked(FIRST, LAST * per + m)
            late_ref[2 * per + m] = to_last
            late_ref[3 * per + m] = to_first
            column_ref[m] = dot(inverse_ref[...], to_first).astype(bf16)
            column_ref[per + m] = to_last

    early, late, column = call(
        mask_kernel,
        [shaped(2 * per, width, width), shaped(4 * per, width, width), shaped(2 * per, width, width)],
        [pattern, inverse[MIDDLE], after(blocks, part)],
        in_specs=[SMEM, VMEM, VMEM],
    )

    def row_factor(ref, start):
        share = ref.shape[0] // cols
        return jnp.concatenate([ref[c * share + start + m] for c in range(cols) for m in range(per)], axis=1)

    def stack(ref, col):
        return jnp.concatenate([ref[m * cols + (col ^ k)] for k in col_order for m in range(per)], axis=0)

    def fill_kernel(early_ref, late_ref, columns_ref, forward_ref, backward_ref, held_ref):
        row, col = lax.axis_index("pr"), lax.axis_index("pc")
        for start, source, out_ref in ((0, 0, forward_ref), (per, 1, backward_ref)):
            factor = row_factor(early_ref, start)
            for m in range(per):
                for n, k in enumerate(row_order):
                    held_ref[row ^ k] = columns_ref[n * 2 * per + source * per + m]
                fill = dot(factor, stack(held_ref, col))
                out_ref[m] = (late_ref[start + m].astype(f32) - fill).astype(bf16)
        for m in range(per):
            backward_ref[per + m] = late_ref[2 * per + m]
            forward_ref[per + m] = late_ref[3 * per + m]

    def solve_first(rhs_ref, first_inverse_ref, middle_inverse_ref, total_ref, out_ref, resid_ref):
        resid = (rhs_ref[FIRST].astype(f32) - total_ref[FIRST].astype(f32)).astype(bf16)
        out_ref[0] = dot(first_inverse_ref[...], resid).astype(bf16)
        resid = (rhs_ref[MIDDLE].astype(f32) - total_ref[MIDDLE].astype(f32)).astype(bf16)
        out_ref[1] = dot(middle_inverse_ref[...], resid).astype(bf16)
        resid_ref[...] = resid

    early = far_half(early, "pc")
    bit = 1
    while bit < lax.axis_size("gz"):
        part = part + hop(part, "gz", bit)
        bit *= 2
    total = part
    for bit in far_to_near("pc"):
        total = total + hop(total, "pc", bit)
    early = near_half(after(early, part), "pc")
    columns = gather(after(column, part), "pr")
    forward, backward = call(
        fill_kernel,
        [shaped(2 * per, width, width), shaped(2 * per, width, width)],
        [early, late, columns],
        scratch=[pltpu.VMEM((rows, width, width), bf16)],
    )
    solved, resid = call(
        solve_first,
        [shaped(2, width, count), shaped(width, count)],
        [rhs, inverse[FIRST], inverse[MIDDLE], total],
    )
    gathered = gather(solved, "pr")
    forward = gather_direct(forward, "pc")
    backward = far_half(after(backward, solved), "pc")
    backward = near_half(after(backward, gathered), "pc")

    def solve_forward(middle_inverse_ref, last_inverse_ref, rhs_ref, sum_ref, resid_ref, solved_ref, early_ref, late_ref, out_ref,
                      first_ref, middle_ref):
        row, col = lax.axis_index("pr"), lax.axis_index("pc")
        for n, k in enumerate(row_order):
            first_ref[row ^ k] = solved_ref[2 * n]
            middle_ref[row ^ k] = solved_ref[2 * n + 1]
        first = stack(first_ref, col)
        total = dot(row_factor(late_ref, per), first)
        resid = (resid_ref[...].astype(f32) - total).astype(bf16)
        out_ref[1] = dot(middle_inverse_ref[...], resid).astype(bf16)
        total = dot(row_factor(late_ref, 0), first) + dot(row_factor(early_ref, 0), stack(middle_ref, col))
        total += sum_ref[LAST].astype(f32)
        resid = (rhs_ref[...].astype(f32) - total).astype(bf16)
        out_ref[0] = dot(last_inverse_ref[...], resid).astype(bf16)

    (ends,) = call(
        solve_forward,
        [shaped(2, width, count)],
        [inverse[MIDDLE], inverse[LAST], rhs[LAST], total, resid, gathered, early, forward],
        scratch=[pltpu.VMEM((rows, width, count), bf16)] * 2,
    )
    ends = gather(ends, "pr")

    def solve_backward(solved_ref, up_ref, sub_ref, ends_ref, early_ref, late_ref, solution_ref, result_ref, last_ref, middle_ref):
        row, col = lax.axis_index("pr"), lax.axis_index("pc")
        for n, k in enumerate(row_order):
            last_ref[row ^ k] = ends_ref[2 * n]
            middle_ref[row ^ k] = ends_ref[2 * n + 1]
        last = stack(last_ref, col)
        total = dot(row_factor(early_ref, per), stack(middle_ref, col)) + dot(row_factor(late_ref, 0), last)
        solution_ref[FIRST] = (solved_ref[0].astype(f32) - total).astype(bf16)
        total = dot(row_factor(late_ref, per), last)
        solution_ref[MIDDLE] = (ends_ref[1].astype(f32) - total).astype(bf16)
        solution_ref[LAST] = ends_ref[0]
        own = solution_ref[...].reshape(levels * width, count)
        result_ref[...] = (sub_ref[...].astype(f32) - dot(up_ref[...], own)).astype(bf16)

    own_solution, result = call(
        solve_backward,
        [shaped(levels, width, count), shaped(*sub.shape)],
        [solved, up, kept, ends, early, backward],
        scratch=[pltpu.VMEM((rows, width, count), bf16)] * 2,
    )
    return own_solution[None], result[None, None, None]


def solution(mesh):
    return jax.shard_map(
        per_device,
        mesh=mesh,
        in_specs=(
            P("pr", None, None, None),
            P("pr", None, None, None),
            P("pr", None, None, "pc", None, None),
            P(),
            P("gz", "pr", "pc", None, None),
            P("gz", "pr", "pc", None, None),
            P("gz", "pr", "pc", None, None),
        ),
        out_specs=(P("pr", None, None, None), P("gz", "pr", "pc", None, None)),
        check_vma=False,
    )
```

time: 42.5 us -> 41.3 us (0.972)
  starting transfers between devices: 17.4 us -> 24.7 us
  waiting for transfers between devices: 15.7 us -> 8.79 us
  local copies, waits for them, and re-layouts: 3.98 us -> 2.85 us
  Pallas kernels: 4.03 us -> 3.52 us
    ppermute x14 -> x16, starting transfers between devices: 17.4 us -> 24.7 us  [hop(): return lax.ppermute(x, axis, [(i, i ^ offset) for i in range(size)])]
    ppermute x14 -> x16, waiting for transfers between devices: 15.7 us -> 8.79 us  [hop(): return lax.ppermute(x, axis, [(i, i ^ offset) for i in range(size)])]
    unnamed x21 -> x17, local copies, waits for them, and re-layouts: 3.85 us -> 2.8 us
    pallas_call x5 -> x6, Pallas kernels: 4.03 us -> 3.52 us  [call(): pl.pallas_call(kernel, out_shape=outs, in_specs=in_specs or [VMEM] * len(...]
  transfers between devices with their start and end apart: 14 -> 16, of which waited for: 8 -> 8; matrix products, arithmetic and copies ran while one was open for 1% -> 1% of each run, Pallas kernels for 1% -> 4%
where the time goes in v3:
time: 41.3 us; the launch traced here: 41 us
  starting transfers between devices  24.7 us (60%)
  waiting for transfers between devices  8.79 us (21%)
  Pallas kernels  3.52 us (9%)
  local copies, waits for them, and re-layouts  2.85 us (7%)
  between operations  0.84 us (2%)
    ppermute x16, starting transfers between devices, hop(): return lax.ppermute(x, axis, [(i, i ^ offset) for i in range(size)])  24.7 us
    ppermute x16, waiting for transfers between devices, hop(): return lax.ppermute(x, axis, [(i, i ^ offset) for i in range(size)])  8.79 us
    pallas_call x6, Pallas kernels, call(): pl.pallas_call(kernel, out_shape=outs, in_specs=in_specs or [VMEM] * len(...  3.52 us
    unnamed x17, local copies, waits for them, and re-layouts  2.8 us
  transfers between devices with their start and end apart: 16, of which 8 were waited for; matrix products, arithmetic and copies ran while one was open for 1% of the time, Pallas kernels for 4%

profile of v3, /device:TPU:0, one launch (start us, length us, event | category | flops | bytes accessed | tf_op | source)
XLA Modules:
  0.0 41.0 jit_solution(9434181193391023589)
XLA Ops:
  0.6 0.0 copy-start
  0.6 1.1 %copy-done = bf16[1,1,1,384,1024]{4,3,2,1,0:T(8,128)(2,1)S(1)} copy-done((bf16[1,1,1,384,1024]{4,3,2,1,0:T(8,128)(2,1)S(1)}, bf16[1,1,1,384,1024]{4,3,2,1,0:T(8,128)(2,1)}, u32[]{:S(2)}) %copy-start) | copy-done | bytes 786456
  1.8 0.0 copy-start.3
  1.8 0.9 %copy-done.3 = bf16[1,1,1,1024,128]{4,3,2,1,0:T(8,128)(2,1)S(1)} copy-done((bf16[1,1,1,1024,128]{4,3,2,1,0:T(8,128)(2,1)S(1)}, bf16[1,1,1,1024,128]{4,3,2,1,0:T(8,128)(2,1)}, u32[]{:S(2)}) %copy-start.3) | copy-done | bytes 262168
  2.7 0.0 copy-start.6
  2.7 0.0 copy-start.2
  2.7 0.4 shard_map.86
  3.1 3.0 %collective-permute-start = (bf16[3,128,128]{2,1,0:T(8,128)(2,1)S(1)}, bf16[3,128,128]{2,1,0:T(8,128)(2,1)S(1)}, u32[]{:S(2)}, u32[]{:S(2)}) collective-permute-start(bf16[3,128,128]{2,1,0:T(8,128)(2,1)S(1)} %get-tuple-element.18), channel_id=1, source_target_pairs={{0,16},{16,0},{1,17},{17,1},{2,18},{18,2},{3,19},{19,3},{4,20},{20... | collective-permute-start | bytes 294920 | tf_op jit(solution)/shard_map/ppermute | solution.py:19
  6.1 0.0 copy-done.6
  6.1 0.0 copy-start.5
  6.1 0.0 copy-done.2
  6.1 0.7 %copy-done.5 = s32[12,12]{1,0:T(8,128)S(1)} copy-done((s32[12,12]{1,0:T(8,128)S(1)}, s32[12,12]{1,0:T(8,128)}, u32[]{:S(2)}) %copy-start.5) | copy-done | bytes 600
  6.8 0.0 copy-start.4
  6.8 0.8 %shard_map.88 = (bf16[2,128,128]{2,1,0:T(8,128)(2,1)S(1)}, bf16[4,128,128]{2,1,0:T(8,128)(2,1)S(1)}, bf16[2,128,128]{2,1,0:T(8,128)(2,1)S(1)}) custom-call(s32[12,12]{1,0:T(8,128)S(1)} %copy-done.5, bf16[128,128]{1,0:T(8,128)(2,1)S(1)} %get-tuple-element.36.middle_inverse_ref.inverse_ref, bf16[3,3,128,128]{3,2,1,0:T(8,128)(2,1)S(1)} %bitcast.17), custom_call_target="tpu_custom_call" | custom-call | tf_op jit(solution)/shard_map/pallas_call | solution.py:60
  7.7 2.6 %collective-permute-start.5 = (bf16[2,128,128]{2,1,0:T(8,128)(2,1)S(1)}, bf16[2,128,128]{2,1,0:T(8,128)(2,1)S(1)}, u32[]{:S(2)}, u32[]{:S(2)}) collective-permute-start(bf16[2,128,128]{2,1,0:T(8,128)(2,1)S(1)} %get-tuple-element.23), channel_id=1, source_target_pairs={{0,2},{1,3},{2,0},{3,1},{4,6},{5,7},{6,4},{7,5},{8,10},{9,11},{10,... | collective-permute-start | bytes 196616 | tf_op jit(solution)/shard_map/ppermute | solution.py:19
  10.3 0.0 copy-done.4
  10.3 0.0 collective-permute-done
  10.3 1.6 %collective-permute-start.7 = (bf16[2,128,128]{2,1,0:T(8,128)(2,1)S(1)}, bf16[2,128,128]{2,1,0:T(8,128)(2,1)S(1)}, u32[]{:S(2)}, u32[]{:S(2)}) collective-permute-start(bf16[2,128,128]{2,1,0:T(8,128)(2,1)S(1)} %get-tuple-element.27), channel_id=1, source_target_pairs={{0,8},{4,12},{8,0},{12,4},{1,9},{5,13},{9,1},{13,5},{2,10},{6,14},... | collective-permute-start | bytes 196616 | tf_op jit(solution)/shard_map/ppermute | solution.py:19
  11.9 1.2 %collective-permute-done.5 = bf16[2,128,128]{2,1,0:T(8,128)(2,1)S(1)} collective-permute-done((bf16[2,128,128]{2,1,0:T(8,128)(2,1)S(1)}, bf16[2,128,128]{2,1,0:T(8,128)(2,1)S(1)}, u32[]{:S(2)}, u32[]{:S(2)}) %collective-permute-start.5) | collective-permute-done | bytes 65568 | tf_op jit(solution)/shard_map/ppermute | solution.py:19
  13.2 2.4 %collective-permute-start.1 = (bf16[3,128,128]{2,1,0:T(8,128)(2,1)S(1)}, bf16[3,128,128]{2,1,0:T(8,128)(2,1)S(1)}, u32[]{:S(2)}, u32[]{:S(2)}) collective-permute-start(bf16[3,128,128]{2,1,0:T(8,128)(2,1)S(1)} %add.9), channel_id=1, source_target_pairs={{0,2},{1,3},{2,0},{3,1},{4,6},{5,7},{6,4},{7,5},{8,10},{9,11},{10,... | collective-permute-start | bytes 294920 | tf_op jit(solution)/shard_map/ppermute | solution.py:19
  15.6 2.1 %collective-permute-start.6 = (bf16[4,128,128]{2,1,0:T(8,128)(2,1)S(1)}, bf16[4,128,128]{2,1,0:T(8,128)(2,1)S(1)}, u32[]{:S(2)}, u32[]{:S(2)}) collective-permute-start(bf16[4,128,128]{2,1,0:T(8,128)(2,1)S(1)} %pad_maximum_fusion.5), channel_id=1, source_target_pairs={{0,1},{1,0},{2,3},{3,2},{4,5},{5,4},{6,7},{7,6},{8,9},{9,8},{10,11... | collective-permute-start | bytes 393224 | tf_op jit(solution)/shard_map/ppermute | solution.py:19
  17.7 0.0 collective-permute-done.7
  17.7 0.1 collective-permute-start.8
  17.8 1.1 %collective-permute-done.1 = bf16[3,128,128]{2,1,0:T(8,128)(2,1)S(1)} collective-permute-done((bf16[3,128,128]{2,1,0:T(8,128)(2,1)S(1)}, bf16[3,128,128]{2,1,0:T(8,128)(2,1)S(1)}, u32[]{:S(2)}, u32[]{:S(2)}) %collective-permute-start.1) | collective-permute-done | bytes 98336 | tf_op jit(solution)/shard_map/ppermute | solution.py:19
  18.9 1.8 %collective-permute-start.2 = (bf16[3,128,128]{2,1,0:T(8,128)(2,1)S(1)}, bf16[3,128,128]{2,1,0:T(8,128)(2,1)S(1)}, u32[]{:S(2)}, u32[]{:S(2)}) collective-permute-start(bf16[3,128,128]{2,1,0:T(8,128)(2,1)S(1)} %add.10), channel_id=1, source_target_pairs={{0,1},{1,0},{2,3},{3,2},{4,5},{5,4},{6,7},{7,6},{8,9},{9,8},{10,11... | collective-permute-start | bytes 294920 | tf_op jit(solution)/shard_map/ppermute | solution.py:19
  20.7 0.7 %collective-permute-done.6 = bf16[4,128,128]{2,1,0:T(8,128)(2,1)S(1)} collective-permute-done((bf16[4,128,128]{2,1,0:T(8,128)(2,1)S(1)}, bf16[4,128,128]{2,1,0:T(8,128)(2,1)S(1)}, u32[]{:S(2)}, u32[]{:S(2)}) %collective-permute-start.6) | collective-permute-done | bytes 131104 | tf_op jit(solution)/shard_map/ppermute | solution.py:19
  21.4 0.0 collective-permute-done.8
  21.4 0.2 shard_map.89
  21.7 2.2 %collective-permute-start.11 = (bf16[2,128,128]{2,1,0:T(8,128)(2,1)S(1)}, bf16[2,128,128]{2,1,0:T(8,128)(2,1)S(1)}, u32[]{:S(2)}, u32[]{:S(2)}) collective-permute-start(bf16[2,128,128]{2,1,0:T(8,128)(2,1)S(1)} %get-tuple-element.28), channel_id=1, source_target_pairs={{0,3},{1,2},{2,1},{3,0},{4,7},{5,6},{6,5},{7,4},{8,11},{9,10},{10,... | collective-permute-start | bytes 196616 | tf_op jit(solution)/shard_map/ppermute | solution.py:19
  23.9 1.1 %collective-permute-start.10 = (bf16[2,128,128]{2,1,0:T(8,128)(2,1)S(1)}, bf16[2,128,128]{2,1,0:T(8,128)(2,1)S(1)}, u32[]{:S(2)}, u32[]{:S(2)}) collective-permute-start(bf16[2,128,128]{2,1,0:T(8,128)(2,1)S(1)} %get-tuple-element.28), channel_id=1, source_target_pairs={{0,1},{1,0},{2,3},{3,2},{4,5},{5,4},{6,7},{7,6},{8,9},{9,8},{10,11... | collective-permute-start | bytes 196616 | tf_op jit(solution)/shard_map/ppermute | solution.py:19
  25.0 1.1 %collective-permute-start.9 = (bf16[2,128,128]{2,1,0:T(8,128)(2,1)S(1)}, bf16[2,128,128]{2,1,0:T(8,128)(2,1)S(1)}, u32[]{:S(2)}, u32[]{:S(2)}) collective-permute-start(bf16[2,128,128]{2,1,0:T(8,128)(2,1)S(1)} %get-tuple-element.28), channel_id=1, source_target_pairs={{0,2},{1,3},{2,0},{3,1},{4,6},{5,7},{6,4},{7,5},{8,10},{9,11},{10,... | collective-permute-start | bytes 196616 | tf_op jit(solution)/shard_map/ppermute | solution.py:19
  26.1 0.0 collective-permute-done.2
  26.2 0.2 shard_map.87
  26.3 1.6 %collective-permute-start.3 = (bf16[2,128,128]{2,1,0:T(8,128)(2,1)S(1)}, bf16[2,128,128]{2,1,0:T(8,128)(2,1)S(1)}, u32[]{:S(2)}, u32[]{:S(2)}) collective-permute-start(bf16[2,128,128]{2,1,0:T(8,128)(2,1)S(1)} %get-tuple-element.19.solved_ref), channel_id=1, source_target_pairs={{0,8},{4,12},{8,0},{12,4},{1,9},{5,13},{9,1},{13,5},{2,10},{6,14},... | collective-permute-start | bytes 196616 | tf_op jit(solution)/shard_map/ppermute | solution.py:19
  27.9 1.8 %collective-permute-start.14 = (bf16[2,128,128]{2,1,0:T(8,128)(2,1)S(1)}, bf16[2,128,128]{2,1,0:T(8,128)(2,1)S(1)}, u32[]{:S(2)}, u32[]{:S(2)}) collective-permute-start(bf16[2,128,128]{2,1,0:T(8,128)(2,1)S(1)} %get-tuple-element.30), channel_id=1, source_target_pairs={{0,2},{1,3},{2,0},{3,1},{4,6},{5,7},{6,4},{7,5},{8,10},{9,11},{10,... | collective-permute-start | bytes 196616 | tf_op jit(solution)/shard_map/ppermute | solution.py:19
  29.7 0.9 %collective-permute-done.3 = bf16[2,128,128]{2,1,0:T(8,128)(2,1)S(1)} collective-permute-done((bf16[2,128,128]{2,1,0:T(8,128)(2,1)S(1)}, bf16[2,128,128]{2,1,0:T(8,128)(2,1)S(1)}, u32[]{:S(2)}, u32[]{:S(2)}) %collective-permute-start.3) | collective-permute-done | bytes 65568 | tf_op jit(solution)/shard_map/ppermute | solution.py:19
  30.7 0.1 collective-permute-start.4
  30.7 0.0 collective-permute-done.11
  30.7 0.0 collective-permute-done.10
  30.8 0.6 %collective-permute-done.9 = bf16[2,128,128]{2,1,0:T(8,128)(2,1)S(1)} collective-permute-done((bf16[2,128,128]{2,1,0:T(8,128)(2,1)S(1)}, bf16[2,128,128]{2,1,0:T(8,128)(2,1)S(1)}, u32[]{:S(2)}, u32[]{:S(2)}) %collective-permute-start.9) | collective-permute-done | bytes 65568 | tf_op jit(solution)/shard_map/ppermute | solution.py:19
  31.4 0.6 %collective-permute-done.4 = bf16[4,128,128]{2,1,0:T(8,128)(2,1)S(1)} collective-permute-done((bf16[4,128,128]{2,1,0:T(8,128)(2,1)S(1)}, bf16[4,128,128]{2,1,0:T(8,128)(2,1)S(1)}, u32[]{:S(2)}, u32[]{:S(2)}) %collective-permute-start.4) | collective-permute-done | bytes 131104 | tf_op jit(solution)/shard_map/ppermute | solution.py:19
  32.1 0.5 %shard_map.90 = bf16[2,128,128]{2,1,0:T(8,128)(2,1)S(1)} custom-call(bf16[128,128]{1,0:T(8,128)(2,1)S(1)} %get-tuple-element.36.middle_inverse_ref.inverse_ref, bf16[128,128]{1,0:T(8,128)(2,1)S(1)} %get-tuple-element.34.last_inverse_ref, bf16[128,128]{1,0:T(8,128)(2,1)S(1)} %slice_bitcast_fusion.rhs_ref, bf16[3,128,128]{2,1,0:T(8,128)(2,1)S(1)} %add.11.total_ref.sum_ref, ...), custom_call_target="tpu_custom_call" | custom-call | tf_op jit(solution)/shard_map/pallas_call | solution.py:60
  32.6 0.0 copy-start.1
  32.6 1.6 %collective-permute-start.12 = (bf16[2,128,128]{2,1,0:T(8,128)(2,1)S(1)}, bf16[2,128,128]{2,1,0:T(8,128)(2,1)S(1)}, u32[]{:S(2)}, u32[]{:S(2)}) collective-permute-start(bf16[2,128,128]{2,1,0:T(8,128)(2,1)S(1)} %shard_map.90), channel_id=1, source_target_pairs={{0,8},{4,12},{8,0},{12,4},{1,9},{5,13},{9,1},{13,5},{2,10},{6,14},... | collective-permute-start | bytes 196616 | tf_op jit(solution)/shard_map/ppermute | solution.py:19
  34.2 0.0 collective-permute-done.14
  34.2 1.7 %collective-permute-start.15 = (bf16[4,128,128]{2,1,0:T(8,128)(2,1)S(1)}, bf16[4,128,128]{2,1,0:T(8,128)(2,1)S(1)}, u32[]{:S(2)}, u32[]{:S(2)}) collective-permute-start(bf16[4,128,128]{2,1,0:T(8,128)(2,1)S(1)} %pad_maximum_fusion.8), channel_id=1, source_target_pairs={{0,1},{1,0},{2,3},{3,2},{4,5},{5,4},{6,7},{7,6},{8,9},{9,8},{10,11... | collective-permute-start | bytes 393224 | tf_op jit(solution)/shard_map/ppermute | solution.py:19
  35.9 1.1 %collective-permute-done.12 = bf16[2,128,128]{2,1,0:T(8,128)(2,1)S(1)} collective-permute-done((bf16[2,128,128]{2,1,0:T(8,128)(2,1)S(1)}, bf16[2,128,128]{2,1,0:T(8,128)(2,1)S(1)}, u32[]{:S(2)}, u32[]{:S(2)}) %collective-permute-start.12) | collective-permute-done | bytes 65568 | tf_op jit(solution)/shard_map/ppermute | solution.py:19
  37.0 0.1 collective-permute-start.13
  37.1 2.5 %collective-permute-done.15 = bf16[4,128,128]{2,1,0:T(8,128)(2,1)S(1)} collective-permute-done((bf16[4,128,128]{2,1,0:T(8,128)(2,1)S(1)}, bf16[4,128,128]{2,1,0:T(8,128)(2,1)S(1)}, u32[]{:S(2)}, u32[]{:S(2)}) %collective-permute-start.15) | collective-permute-done | bytes 131104 | tf_op jit(solution)/shard_map/ppermute | solution.py:19
  39.6 0.0 collective-permute-done.13
  39.7 0.0 copy-done.1
  39.7 1.4 %shard_map.91 = (bf16[3,128,128]{2,1,0:T(8,128)(2,1)}, bf16[1024,128]{1,0:T(8,128)(2,1)}) custom-call(bf16[2,128,128]{2,1,0:T(8,128)(2,1)S(1)} %get-tuple-element.19.solved_ref, bf16[1024,384]{1,0:T(8,128)(2,1)S(1)} %bitcast.16, bf16[1024,128]{1,0:T(8,128)(2,1)S(1)} %get-tuple-element.20.sub_ref, bf16[8,128,128]{2,1,0:T(8,128)(2,1)S(1)} %pad_maximum_fusion.2.ends_ref, ...), custom_call_target="tpu_custom_call" | custom-call | tf_op jit(solution)/shard_map/pallas_call | solution.py:60
  (19 shorter events, 0.4 us)
Async XLA Ops:
  0.6 1.1 %copy-start = (bf16[1,1,1,384,1024]{4,3,2,1,0:T(8,128)(2,1)S(1)}, bf16[1,1,1,384,1024]{4,3,2,1,0:T(8,128)(2,1)}, u32[]{:S(2)}) copy-start(bf16[1,1,1,384,1024]{4,3,2,1,0:T(8,128)(2,1)} %param.12) | copy-start | bytes 2359300
  1.8 0.9 %copy-start.3 = (bf16[1,1,1,1024,128]{4,3,2,1,0:T(8,128)(2,1)S(1)}, bf16[1,1,1,1024,128]{4,3,2,1,0:T(8,128)(2,1)}, u32[]{:S(2)}) copy-start(bf16[1,1,1,1024,128]{4,3,2,1,0:T(8,128)(2,1)} %param.11) | copy-start | bytes 786436
  2.7 3.4 %copy-start.6 = (bf16[1,3,128,128]{3,2,1,0:T(8,128)(2,1)S(1)}, bf16[1,3,128,128]{3,2,1,0:T(8,128)(2,1)}, u32[]{:S(2)}) copy-start(bf16[1,3,128,128]{3,2,1,0:T(8,128)(2,1)} %param.8) | copy-start | bytes 294916
  2.7 3.4 %copy-start.2 = (bf16[1,3,3,1,128,128]{5,4,3,2,1,0:T(8,128)(2,1)S(1)}, bf16[1,3,3,1,128,128]{5,4,3,2,1,0:T(8,128)(2,1)}, u32[]{:S(2)}) copy-start(bf16[1,3,3,1,128,128]{5,4,3,2,1,0:T(8,128)(2,1)} %param.9) | copy-start | bytes 884740
  3.1 7.2 %collective-permute-start = (bf16[3,128,128]{2,1,0:T(8,128)(2,1)S(1)}, bf16[3,128,128]{2,1,0:T(8,128)(2,1)S(1)}, u32[]{:S(2)}, u32[]{:S(2)}) collective-permute-start(bf16[3,128,128]{2,1,0:T(8,128)(2,1)S(1)} %get-tuple-element.18), channel_id=1, source_target_pairs={{0,16},{16,0},{1,17},{17,1},{2,18},{18,2},{3,19},{19,3},{4,20},{20... | collective-permute-start | bytes 294920 | tf_op jit(solution)/shard_map/ppermute | solution.py:19
  6.1 0.7 %copy-start.5 = (s32[12,12]{1,0:T(8,128)S(1)}, s32[12,12]{1,0:T(8,128)}, u32[]{:S(2)}) copy-start(s32[12,12]{1,0:T(8,128)} %pattern_ref.1) | copy-start | bytes 1732
  6.8 3.4 %copy-start.4 = (bf16[1,3,128,128]{3,2,1,0:T(8,128)(2,1)S(1)}, bf16[1,3,128,128]{3,2,1,0:T(8,128)(2,1)}, u32[]{:S(2)}) copy-start(bf16[1,3,128,128]{3,2,1,0:T(8,128)(2,1)} %param.7) | copy-start | bytes 294916
  7.7 5.5 %collective-permute-start.5 = (bf16[2,128,128]{2,1,0:T(8,128)(2,1)S(1)}, bf16[2,128,128]{2,1,0:T(8,128)(2,1)S(1)}, u32[]{:S(2)}, u32[]{:S(2)}) collective-permute-start(bf16[2,128,128]{2,1,0:T(8,128)(2,1)S(1)} %get-tuple-element.23), channel_id=1, source_target_pairs={{0,2},{1,3},{2,0},{3,1},{4,6},{5,7},{6,4},{7,5},{8,10},{9,11},{10,... | collective-permute-start | bytes 196616 | tf_op jit(solution)/shard_map/ppermute | solution.py:19
  10.3 7.4 %collective-permute-start.7 = (bf16[2,128,128]{2,1,0:T(8,128)(2,1)S(1)}, bf16[2,128,128]{2,1,0:T(8,128)(2,1)S(1)}, u32[]{:S(2)}, u32[]{:S(2)}) collective-permute-start(bf16[2,128,128]{2,1,0:T(8,128)(2,1)S(1)} %get-tuple-element.27), channel_id=1, source_target_pairs={{0,8},{4,12},{8,0},{12,4},{1,9},{5,13},{9,1},{13,5},{2,10},{6,14},... | collective-permute-start | bytes 196616 | tf_op jit(solution)/shard_map/ppermute | solution.py:19
  13.2 5.7 %collective-permute-start.1 = (bf16[3,128,128]{2,1,0:T(8,128)(2,1)S(1)}, bf16[3,128,128]{2,1,0:T(8,128)(2,1)S(1)}, u32[]{:S(2)}, u32[]{:S(2)}) collective-permute-start(bf16[3,128,128]{2,1,0:T(8,128)(2,1)S(1)} %add.9), channel_id=1, source_target_pairs={{0,2},{1,3},{2,0},{3,1},{4,6},{5,7},{6,4},{7,5},{8,10},{9,11},{10,... | collective-permute-start | bytes 294920 | tf_op jit(solution)/shard_map/ppermute | solution.py:19
  15.6 5.8 %collective-permute-start.6 = (bf16[4,128,128]{2,1,0:T(8,128)(2,1)S(1)}, bf16[4,128,128]{2,1,0:T(8,128)(2,1)S(1)}, u32[]{:S(2)}, u32[]{:S(2)}) collective-permute-start(bf16[4,128,128]{2,1,0:T(8,128)(2,1)S(1)} %pad_maximum_fusion.5), channel_id=1, source_target_pairs={{0,1},{1,0},{2,3},{3,2},{4,5},{5,4},{6,7},{7,6},{8,9},{9,8},{10,11... | collective-permute-start | bytes 393224 | tf_op jit(solution)/shard_map/ppermute | solution.py:19
  17.7 3.7 %collective-permute-start.8 = (bf16[4,128,128]{2,1,0:T(8,128)(2,1)S(1)}, bf16[4,128,128]{2,1,0:T(8,128)(2,1)S(1)}, u32[]{:S(2)}, u32[]{:S(2)}) collective-permute-start(bf16[4,128,128]{2,1,0:T(8,128)(2,1)S(1)} %pad_maximum_fusion.6), channel_id=1, source_target_pairs={{0,4},{4,0},{8,12},{12,8},{1,5},{5,1},{9,13},{13,9},{2,6},{6,2},{1... | collective-permute-start | bytes 393224 | tf_op jit(solution)/shard_map/ppermute | solution.py:19
  18.9 7.2 %collective-permute-start.2 = (bf16[3,128,128]{2,1,0:T(8,128)(2,1)S(1)}, bf16[3,128,128]{2,1,0:T(8,128)(2,1)S(1)}, u32[]{:S(2)}, u32[]{:S(2)}) collective-permute-start(bf16[3,128,128]{2,1,0:T(8,128)(2,1)S(1)} %add.10), channel_id=1, source_target_pairs={{0,1},{1,0},{2,3},{3,2},{4,5},{5,4},{6,7},{7,6},{8,9},{9,8},{10,11... | collective-permute-start | bytes 294920 | tf_op jit(solution)/shard_map/ppermute | solution.py:19
  21.7 9.1 %collective-permute-start.11 = (bf16[2,128,128]{2,1,0:T(8,128)(2,1)S(1)}, bf16[2,128,128]{2,1,0:T(8,128)(2,1)S(1)}, u32[]{:S(2)}, u32[]{:S(2)}) collective-permute-start(bf16[2,128,128]{2,1,0:T(8,128)(2,1)S(1)} %get-tuple-element.28), channel_id=1, source_target_pairs={{0,3},{1,2},{2,1},{3,0},{4,7},{5,6},{6,5},{7,4},{8,11},{9,10},{10,... | collective-permute-start | bytes 196616 | tf_op jit(solution)/shard_map/ppermute | solution.py:19
  23.9 6.9 %collective-permute-start.10 = (bf16[2,128,128]{2,1,0:T(8,128)(2,1)S(1)}, bf16[2,128,128]{2,1,0:T(8,128)(2,1)S(1)}, u32[]{:S(2)}, u32[]{:S(2)}) collective-permute-start(bf16[2,128,128]{2,1,0:T(8,128)(2,1)S(1)} %get-tuple-element.28), channel_id=1, source_target_pairs={{0,1},{1,0},{2,3},{3,2},{4,5},{5,4},{6,7},{7,6},{8,9},{9,8},{10,11... | collective-permute-start | bytes 196616 | tf_op jit(solution)/shard_map/ppermute | solution.py:19
  25.0 6.4 %collective-permute-start.9 = (bf16[2,128,128]{2,1,0:T(8,128)(2,1)S(1)}, bf16[2,128,128]{2,1,0:T(8,128)(2,1)S(1)}, u32[]{:S(2)}, u32[]{:S(2)}) collective-permute-start(bf16[2,128,128]{2,1,0:T(8,128)(2,1)S(1)} %get-tuple-element.28), channel_id=1, source_target_pairs={{0,2},{1,3},{2,0},{3,1},{4,6},{5,7},{6,4},{7,5},{8,10},{9,11},{10,... | collective-permute-start | bytes 196616 | tf_op jit(solution)/shard_map/ppermute | solution.py:19
  26.3 4.3 %collective-permute-start.3 = (bf16[2,128,128]{2,1,0:T(8,128)(2,1)S(1)}, bf16[2,128,128]{2,1,0:T(8,128)(2,1)S(1)}, u32[]{:S(2)}, u32[]{:S(2)}) collective-permute-start(bf16[2,128,128]{2,1,0:T(8,128)(2,1)S(1)} %get-tuple-element.19.solved_ref), channel_id=1, source_target_pairs={{0,8},{4,12},{8,0},{12,4},{1,9},{5,13},{9,1},{13,5},{2,10},{6,14},... | collective-permute-start | bytes 196616 | tf_op jit(solution)/shard_map/ppermute | solution.py:19
  27.9 6.3 %collective-permute-start.14 = (bf16[2,128,128]{2,1,0:T(8,128)(2,1)S(1)}, bf16[2,128,128]{2,1,0:T(8,128)(2,1)S(1)}, u32[]{:S(2)}, u32[]{:S(2)}) collective-permute-start(bf16[2,128,128]{2,1,0:T(8,128)(2,1)S(1)} %get-tuple-element.30), channel_id=1, source_target_pairs={{0,2},{1,3},{2,0},{3,1},{4,6},{5,7},{6,4},{7,5},{8,10},{9,11},{10,... | collective-permute-start | bytes 196616 | tf_op jit(solution)/shard_map/ppermute | solution.py:19
  30.7 1.4 %collective-permute-start.4 = (bf16[4,128,128]{2,1,0:T(8,128)(2,1)S(1)}, bf16[4,128,128]{2,1,0:T(8,128)(2,1)S(1)}, u32[]{:S(2)}, u32[]{:S(2)}) collective-permute-start(bf16[4,128,128]{2,1,0:T(8,128)(2,1)S(1)} %pad_maximum_fusion.4), channel_id=1, source_target_pairs={{0,4},{4,0},{8,12},{12,8},{1,5},{5,1},{9,13},{13,9},{2,6},{6,2},{1... | collective-permute-start | bytes 393224 | tf_op jit(solution)/shard_map/ppermute | solution.py:19
  32.6 7.0 %copy-start.1 = (bf16[1,1,1,1024,384]{4,3,2,1,0:T(8,128)(2,1)S(1)}, bf16[1,1,1,1024,384]{4,3,2,1,0:T(8,128)(2,1)}, u32[]{:S(2)}) copy-start(bf16[1,1,1,1024,384]{4,3,2,1,0:T(8,128)(2,1)} %param.13) | copy-start | bytes 2359300
  32.6 4.3 %collective-permute-start.12 = (bf16[2,128,128]{2,1,0:T(8,128)(2,1)S(1)}, bf16[2,128,128]{2,1,0:T(8,128)(2,1)S(1)}, u32[]{:S(2)}, u32[]{:S(2)}) collective-permute-start(bf16[2,128,128]{2,1,0:T(8,128)(2,1)S(1)} %shard_map.90), channel_id=1, source_target_pairs={{0,8},{4,12},{8,0},{12,4},{1,9},{5,13},{9,1},{13,5},{2,10},{6,14},... | collective-permute-start | bytes 196616 | tf_op jit(solution)/shard_map/ppermute | solution.py:19
  34.2 5.3 %collective-permute-start.15 = (bf16[4,128,128]{2,1,0:T(8,128)(2,1)S(1)}, bf16[4,128,128]{2,1,0:T(8,128)(2,1)S(1)}, u32[]{:S(2)}, u32[]{:S(2)}) collective-permute-start(bf16[4,128,128]{2,1,0:T(8,128)(2,1)S(1)} %pad_maximum_fusion.8), channel_id=1, source_target_pairs={{0,1},{1,0},{2,3},{3,2},{4,5},{5,4},{6,7},{7,6},{8,9},{9,8},{10,11... | collective-permute-start | bytes 393224 | tf_op jit(solution)/shard_map/ppermute | solution.py:19
  37.0 2.6 %collective-permute-start.13 = (bf16[4,128,128]{2,1,0:T(8,128)(2,1)S(1)}, bf16[4,128,128]{2,1,0:T(8,128)(2,1)S(1)}, u32[]{:S(2)}, u32[]{:S(2)}) collective-permute-start(bf16[4,128,128]{2,1,0:T(8,128)(2,1)S(1)} %pad_maximum_fusion.7), channel_id=1, source_target_pairs={{0,4},{4,0},{8,12},{12,8},{1,5},{5,1},{9,13},{13,9},{2,6},{6,2},{1... | collective-permute-start | bytes 393224 | tf_op jit(solution)/shard_map/ppermute | solution.py:19

commit v4 on v3

--- a/solution.py
+++ b/solution.py
@@ -131,7 +131,7 @@
                 fill = dot(factor, stack(held_ref, col))
                 out_ref[m] = (late_ref[start + m].astype(f32) - fill).astype(bf16)
         for m in range(per):
-            backward_ref[per + m] = late_ref[2 * per + m]
+            forward_ref[2 * per + m] = late_ref[2 * per + m]
             forward_ref[per + m] = late_ref[3 * per + m]
 
     def solve_first(rhs_ref, first_inverse_ref, middle_inverse_ref, total_ref, out_ref, resid_ref):
@@ -153,7 +153,7 @@
     columns = gather(after(column, part), "pr")
     forward, backward = call(
         fill_kernel,
-        [shaped(2 * per, width, width), shaped(2 * per, width, width)],
+        [shaped(3 * per, width, width), shaped(per, width, width)],
         [early, late, columns],
         scratch=[pltpu.VMEM((rows, width, width), bf16)],
     )
@@ -190,7 +190,7 @@
     )
     ends = gather(ends, "pr")
 
-    def solve_backward(solved_ref, up_ref, sub_ref, ends_ref, early_ref, late_ref, solution_ref, result_ref, last_ref, middle_ref):
+    def solve_backward(solved_ref, up_ref, sub_ref, ends_ref, early_ref, forward_ref, late_ref, solution_ref, result_ref, last_ref, middle_ref):
         row, col = lax.axis_index("pr"), lax.axis_index("pc")
         for n, k in enumerate(row_order):
             last_ref[row ^ k] = ends_ref[2 * n]
@@ -198,7 +198,7 @@
         last = stack(last_ref, col)
         total = dot(row_factor(early_ref, per), stack(middle_ref, col)) + dot(row_factor(late_ref, 0), last)
         solution_ref[FIRST] = (solved_ref[0].astype(f32) - total).astype(bf16)
-        total = dot(row_factor(late_ref, per), last)
+        total = dot(row_factor(forward_ref, 2 * per), last)
         solution_ref[MIDDLE] = (ends_ref[1].astype(f32) - total).astype(bf16)
         solution_ref[LAST] = ends_ref[0]
         own = solution_ref[...].reshape(levels * width, count)
@@ -207,7 +207,7 @@
     own_solution, result = call(
         solve_backward,
         [shaped(levels, width, count), shaped(*sub.shape)],
-        [solved, up, kept, ends, early, backward],
+        [solved, up, kept, ends, early, forward, backward],
         scratch=[pltpu.VMEM((rows, width, count), bf16)] * 2,
     )
     return own_solution[None], result[None, None, None]

time: 41.3 us -> 40.6 us (0.983)
    unnamed x17 -> x20, local copies, waits for them, and re-layouts: 2.8 us -> 2.84 us
where the time goes in v4:
time: 40.6 us; the launch traced here: 40.4 us
  starting transfers between devices  24.4 us (60%)
  waiting for transfers between devices  8.43 us (21%)
  Pallas kernels  3.52 us (9%)
  local copies, waits for them, and re-layouts  2.9 us (7%)
  between operations  0.86 us (2%)
    ppermute x16, starting transfers between devices, hop(): return lax.ppermute(x, axis, [(i, i ^ offset) for i in range(size)])  24.4 us
    ppermute x16, waiting for transfers between devices, hop(): return lax.ppermute(x, axis, [(i, i ^ offset) for i in range(size)])  8.43 us
    pallas_call x6, Pallas kernels, call(): pl.pallas_call(kernel, out_shape=outs, in_specs=in_specs or [VMEM] * len(...  3.52 us
    unnamed x20, local copies, waits for them, and re-layouts  2.84 us
  transfers between devices with their start and end apart: 16, of which 8 were waited for; matrix products, arithmetic and copies ran while one was open for 1% of the time, Pallas kernels for 4%

profile of v4, /device:TPU:0, one launch (start us, length us, event | category | flops | bytes accessed | tf_op | source)
XLA Modules:
  0.0 40.4 jit_solution(6055148047952852179)
XLA Ops:
  0.6 0.0 copy-start.1
  0.6 1.1 %copy-done.1 = bf16[1,1,1,384,1024]{4,3,2,1,0:T(8,128)(2,1)S(1)} copy-done((bf16[1,1,1,384,1024]{4,3,2,1,0:T(8,128)(2,1)S(1)}, bf16[1,1,1,384,1024]{4,3,2,1,0:T(8,128)(2,1)}, u32[]{:S(2)}) %copy-start.1) | copy-done | bytes 786456
  1.8 0.0 copy-start.3
  1.8 0.9 %copy-done.3 = bf16[1,1,1,1024,128]{4,3,2,1,0:T(8,128)(2,1)S(1)} copy-done((bf16[1,1,1,1024,128]{4,3,2,1,0:T(8,128)(2,1)S(1)}, bf16[1,1,1,1024,128]{4,3,2,1,0:T(8,128)(2,1)}, u32[]{:S(2)}) %copy-start.3) | copy-done | bytes 262168
  2.7 0.0 copy-start.6
  2.7 0.0 copy-start.2
  2.7 0.4 shard_map.86
  3.1 3.0 %collective-permute-start = (bf16[3,128,128]{2,1,0:T(8,128)(2,1)S(1)}, bf16[3,128,128]{2,1,0:T(8,128)(2,1)S(1)}, u32[]{:S(2)}, u32[]{:S(2)}) collective-permute-start(bf16[3,128,128]{2,1,0:T(8,128)(2,1)S(1)} %get-tuple-element.18), channel_id=1, source_target_pairs={{0,16},{16,0},{1,17},{17,1},{2,18},{18,2},{3,19},{19,3},{4,20},{20... | collective-permute-start | bytes 294920 | tf_op jit(solution)/shard_map/ppermute | solution.py:19
  6.1 0.0 copy-done.6
  6.1 0.0 copy-start.5
  6.1 0.0 copy-done.2
  6.1 0.7 %copy-done.5 = s32[12,12]{1,0:T(8,128)S(1)} copy-done((s32[12,12]{1,0:T(8,128)S(1)}, s32[12,12]{1,0:T(8,128)}, u32[]{:S(2)}) %copy-start.5) | copy-done | bytes 600
  6.8 0.0 copy-start.4
  6.8 0.8 %shard_map.88 = (bf16[2,128,128]{2,1,0:T(8,128)(2,1)S(1)}, bf16[4,128,128]{2,1,0:T(8,128)(2,1)S(1)}, bf16[2,128,128]{2,1,0:T(8,128)(2,1)S(1)}) custom-call(s32[12,12]{1,0:T(8,128)S(1)} %copy-done.5, bf16[128,128]{1,0:T(8,128)(2,1)S(1)} %get-tuple-element.36.middle_inverse_ref.inverse_ref, bf16[3,3,128,128]{3,2,1,0:T(8,128)(2,1)S(1)} %bitcast.17), custom_call_target="tpu_custom_call" | custom-call | tf_op jit(solution)/shard_map/pallas_call | solution.py:60
  7.7 2.6 %collective-permute-start.5 = (bf16[2,128,128]{2,1,0:T(8,128)(2,1)S(1)}, bf16[2,128,128]{2,1,0:T(8,128)(2,1)S(1)}, u32[]{:S(2)}, u32[]{:S(2)}) collective-permute-start(bf16[2,128,128]{2,1,0:T(8,128)(2,1)S(1)} %get-tuple-element.23), channel_id=1, source_target_pairs={{0,2},{1,3},{2,0},{3,1},{4,6},{5,7},{6,4},{7,5},{8,10},{9,11},{10,... | collective-permute-start | bytes 196616 | tf_op jit(solution)/shard_map/ppermute | solution.py:19
  10.3 0.0 copy-done.4
  10.3 0.0 collective-permute-done
  10.3 1.6 %collective-permute-start.7 = (bf16[2,128,128]{2,1,0:T(8,128)(2,1)S(1)}, bf16[2,128,128]{2,1,0:T(8,128)(2,1)S(1)}, u32[]{:S(2)}, u32[]{:S(2)}) collective-permute-start(bf16[2,128,128]{2,1,0:T(8,128)(2,1)S(1)} %get-tuple-element.27), channel_id=1, source_target_pairs={{0,8},{4,12},{8,0},{12,4},{1,9},{5,13},{9,1},{13,5},{2,10},{6,14},... | collective-permute-start | bytes 196616 | tf_op jit(solution)/shard_map/ppermute | solution.py:19
  11.9 1.2 %collective-permute-done.5 = bf16[2,128,128]{2,1,0:T(8,128)(2,1)S(1)} collective-permute-done((bf16[2,128,128]{2,1,0:T(8,128)(2,1)S(1)}, bf16[2,128,128]{2,1,0:T(8,128)(2,1)S(1)}, u32[]{:S(2)}, u32[]{:S(2)}) %collective-permute-start.5) | collective-permute-done | bytes 65568 | tf_op jit(solution)/shard_map/ppermute | solution.py:19
  13.2 2.4 %collective-permute-start.1 = (bf16[3,128,128]{2,1,0:T(8,128)(2,1)S(1)}, bf16[3,128,128]{2,1,0:T(8,128)(2,1)S(1)}, u32[]{:S(2)}, u32[]{:S(2)}) collective-permute-start(bf16[3,128,128]{2,1,0:T(8,128)(2,1)S(1)} %add.9), channel_id=1, source_target_pairs={{0,2},{1,3},{2,0},{3,1},{4,6},{5,7},{6,4},{7,5},{8,10},{9,11},{10,... | collective-permute-start | bytes 294920 | tf_op jit(solution)/shard_map/ppermute | solution.py:19
  15.6 2.1 %collective-permute-start.6 = (bf16[4,128,128]{2,1,0:T(8,128)(2,1)S(1)}, bf16[4,128,128]{2,1,0:T(8,128)(2,1)S(1)}, u32[]{:S(2)}, u32[]{:S(2)}) collective-permute-start(bf16[4,128,128]{2,1,0:T(8,128)(2,1)S(1)} %pad_maximum_fusion.3), channel_id=1, source_target_pairs={{0,1},{1,0},{2,3},{3,2},{4,5},{5,4},{6,7},{7,6},{8,9},{9,8},{10,11... | collective-permute-start | bytes 393224 | tf_op jit(solution)/shard_map/ppermute | solution.py:19
  17.7 0.0 collective-permute-done.7
  17.7 0.1 collective-permute-start.8
  17.8 1.1 %collective-permute-done.1 = bf16[3,128,128]{2,1,0:T(8,128)(2,1)S(1)} collective-permute-done((bf16[3,128,128]{2,1,0:T(8,128)(2,1)S(1)}, bf16[3,128,128]{2,1,0:T(8,128)(2,1)S(1)}, u32[]{:S(2)}, u32[]{:S(2)}) %collective-permute-start.1) | collective-permute-done | bytes 98336 | tf_op jit(solution)/shard_map/ppermute | solution.py:19
  18.9 1.8 %collective-permute-start.2 = (bf16[3,128,128]{2,1,0:T(8,128)(2,1)S(1)}, bf16[3,128,128]{2,1,0:T(8,128)(2,1)S(1)}, u32[]{:S(2)}, u32[]{:S(2)}) collective-permute-start(bf16[3,128,128]{2,1,0:T(8,128)(2,1)S(1)} %add.10), channel_id=1, source_target_pairs={{0,1},{1,0},{2,3},{3,2},{4,5},{5,4},{6,7},{7,6},{8,9},{9,8},{10,11... | collective-permute-start | bytes 294920 | tf_op jit(solution)/shard_map/ppermute | solution.py:19
  20.7 0.6 %collective-permute-done.6 = bf16[4,128,128]{2,1,0:T(8,128)(2,1)S(1)} collective-permute-done((bf16[4,128,128]{2,1,0:T(8,128)(2,1)S(1)}, bf16[4,128,128]{2,1,0:T(8,128)(2,1)S(1)}, u32[]{:S(2)}, u32[]{:S(2)}) %collective-permute-start.6) | collective-permute-done | bytes 131104 | tf_op jit(solution)/shard_map/ppermute | solution.py:19
  21.2 0.0 collective-permute-done.8
  21.3 0.2 shard_map.89
  21.5 2.9 %collective-permute-start.9 = (bf16[3,128,128]{2,1,0:T(8,128)(2,1)S(1)}, bf16[3,128,128]{2,1,0:T(8,128)(2,1)S(1)}, u32[]{:S(2)}, u32[]{:S(2)}) collective-permute-start(bf16[3,128,128]{2,1,0:T(8,128)(2,1)S(1)} %get-tuple-element.28), channel_id=1, source_target_pairs={{0,2},{1,3},{2,0},{3,1},{4,6},{5,7},{6,4},{7,5},{8,10},{9,11},{10,... | collective-permute-start | bytes 294920 | tf_op jit(solution)/shard_map/ppermute | solution.py:19
  24.4 0.0 collective-permute-start.10
  24.4 2.0 %collective-permute-start.11 = (bf16[3,128,128]{2,1,0:T(8,128)(2,1)S(1)}, bf16[3,128,128]{2,1,0:T(8,128)(2,1)S(1)}, u32[]{:S(2)}, u32[]{:S(2)}) collective-permute-start(bf16[3,128,128]{2,1,0:T(8,128)(2,1)S(1)} %get-tuple-element.28), channel_id=1, source_target_pairs={{0,3},{1,2},{2,1},{3,0},{4,7},{5,6},{6,5},{7,4},{8,11},{9,10},{10,... | collective-permute-start | bytes 294920 | tf_op jit(solution)/shard_map/ppermute | solution.py:19
  26.5 0.0 collective-permute-done.2
  26.5 0.2 shard_map.87
  26.7 1.6 %collective-permute-start.3 = (bf16[2,128,128]{2,1,0:T(8,128)(2,1)S(1)}, bf16[2,128,128]{2,1,0:T(8,128)(2,1)S(1)}, u32[]{:S(2)}, u32[]{:S(2)}) collective-permute-start(bf16[2,128,128]{2,1,0:T(8,128)(2,1)S(1)} %get-tuple-element.19.solved_ref), channel_id=1, source_target_pairs={{0,8},{4,12},{8,0},{12,4},{1,9},{5,13},{9,1},{13,5},{2,10},{6,14},... | collective-permute-start | bytes 196616 | tf_op jit(solution)/shard_map/ppermute | solution.py:19
  28.2 1.5 %collective-permute-start.14 = (bf16[1,128,128]{2,1,0:T(8,128)(2,1)S(1)}, bf16[1,128,128]{2,1,0:T(8,128)(2,1)S(1)}, u32[]{:S(2)}, u32[]{:S(2)}) collective-permute-start(bf16[1,128,128]{2,1,0:T(8,128)(2,1)S(1)} %get-tuple-element.30), channel_id=1, source_target_pairs={{0,2},{1,3},{2,0},{3,1},{4,6},{5,7},{6,4},{7,5},{8,10},{9,11},{10,... | collective-permute-start | bytes 98312 | tf_op jit(solution)/shard_map/ppermute | solution.py:19
  29.7 1.3 %collective-permute-done.3 = bf16[2,128,128]{2,1,0:T(8,128)(2,1)S(1)} collective-permute-done((bf16[2,128,128]{2,1,0:T(8,128)(2,1)S(1)}, bf16[2,128,128]{2,1,0:T(8,128)(2,1)S(1)}, u32[]{:S(2)}, u32[]{:S(2)}) %collective-permute-start.3) | collective-permute-done | bytes 65568 | tf_op jit(solution)/shard_map/ppermute | solution.py:19
  31.0 0.1 collective-permute-start.4
  31.1 0.0 collective-permute-done.9
  31.1 0.0 collective-permute-done.10
  31.2 0.6 %collective-permute-done.11 = bf16[3,128,128]{2,1,0:T(8,128)(2,1)S(1)} collective-permute-done((bf16[3,128,128]{2,1,0:T(8,128)(2,1)S(1)}, bf16[3,128,128]{2,1,0:T(8,128)(2,1)S(1)}, u32[]{:S(2)}, u32[]{:S(2)}) %collective-permute-start.11) | collective-permute-done | bytes 98336 | tf_op jit(solution)/shard_map/ppermute | solution.py:19
  31.8 0.6 %collective-permute-done.4 = bf16[4,128,128]{2,1,0:T(8,128)(2,1)S(1)} collective-permute-done((bf16[4,128,128]{2,1,0:T(8,128)(2,1)S(1)}, bf16[4,128,128]{2,1,0:T(8,128)(2,1)S(1)}, u32[]{:S(2)}, u32[]{:S(2)}) %collective-permute-start.4) | collective-permute-done | bytes 131104 | tf_op jit(solution)/shard_map/ppermute | solution.py:19
  32.4 0.5 %shard_map.90 = bf16[2,128,128]{2,1,0:T(8,128)(2,1)S(1)} custom-call(bf16[128,128]{1,0:T(8,128)(2,1)S(1)} %get-tuple-element.36.middle_inverse_ref.inverse_ref, bf16[128,128]{1,0:T(8,128)(2,1)S(1)} %get-tuple-element.34.last_inverse_ref, bf16[128,128]{1,0:T(8,128)(2,1)S(1)} %slice_bitcast_fusion.rhs_ref, bf16[3,128,128]{2,1,0:T(8,128)(2,1)S(1)} %add.11.total_ref.sum_ref, ...), custom_call_target="tpu_custom_call" | custom-call | tf_op jit(solution)/shard_map/pallas_call | solution.py:60
  33.0 0.0 copy-start
  33.0 1.6 %collective-permute-start.12 = (bf16[2,128,128]{2,1,0:T(8,128)(2,1)S(1)}, bf16[2,128,128]{2,1,0:T(8,128)(2,1)S(1)}, u32[]{:S(2)}, u32[]{:S(2)}) collective-permute-start(bf16[2,128,128]{2,1,0:T(8,128)(2,1)S(1)} %shard_map.90), channel_id=1, source_target_pairs={{0,8},{4,12},{8,0},{12,4},{1,9},{5,13},{9,1},{13,5},{2,10},{6,14},... | collective-permute-start | bytes 196616 | tf_op jit(solution)/shard_map/ppermute | solution.py:19
  34.6 0.0 collective-permute-done.14
  34.6 1.2 %collective-permute-start.15 = (bf16[2,128,128]{2,1,0:T(8,128)(2,1)S(1)}, bf16[2,128,128]{2,1,0:T(8,128)(2,1)S(1)}, u32[]{:S(2)}, u32[]{:S(2)}) collective-permute-start(bf16[2,128,128]{2,1,0:T(8,128)(2,1)S(1)} %pad_maximum_fusion.7), channel_id=1, source_target_pairs={{0,1},{1,0},{2,3},{3,2},{4,5},{5,4},{6,7},{7,6},{8,9},{9,8},{10,11... | collective-permute-start | bytes 196616 | tf_op jit(solution)/shard_map/ppermute | solution.py:19
  35.8 1.5 %collective-permute-done.12 = bf16[2,128,128]{2,1,0:T(8,128)(2,1)S(1)} collective-permute-done((bf16[2,128,128]{2,1,0:T(8,128)(2,1)S(1)}, bf16[2,128,128]{2,1,0:T(8,128)(2,1)S(1)}, u32[]{:S(2)}, u32[]{:S(2)}) %collective-permute-start.12) | collective-permute-done | bytes 65568 | tf_op jit(solution)/shard_map/ppermute | solution.py:19
  37.4 0.1 collective-permute-start.13
  37.4 1.5 %collective-permute-done.15 = bf16[2,128,128]{2,1,0:T(8,128)(2,1)S(1)} collective-permute-done((bf16[2,128,128]{2,1,0:T(8,128)(2,1)S(1)}, bf16[2,128,128]{2,1,0:T(8,128)(2,1)S(1)}, u32[]{:S(2)}, u32[]{:S(2)}) %collective-permute-start.15) | collective-permute-done | bytes 65568 | tf_op jit(solution)/shard_map/ppermute | solution.py:19
  39.0 0.0 collective-permute-done.13
  39.0 0.0 copy-done
  39.0 1.4 %shard_map.91 = (bf16[3,128,128]{2,1,0:T(8,128)(2,1)}, bf16[1024,128]{1,0:T(8,128)(2,1)}) custom-call(bf16[2,128,128]{2,1,0:T(8,128)(2,1)S(1)} %get-tuple-element.19.solved_ref, bf16[1024,384]{1,0:T(8,128)(2,1)S(1)} %bitcast.15, bf16[1024,128]{1,0:T(8,128)(2,1)S(1)} %get-tuple-element.20.sub_ref, bf16[8,128,128]{2,1,0:T(8,128)(2,1)S(1)} %pad_maximum_fusion.1.ends_ref, ...), custom_call_target="tpu_custom_call" | custom-call | tf_op jit(solution)/shard_map/pallas_call | solution.py:60
  (22 shorter events, 0.4 us)
Async XLA Ops:
  0.6 1.1 %copy-start.1 = (bf16[1,1,1,384,1024]{4,3,2,1,0:T(8,128)(2,1)S(1)}, bf16[1,1,1,384,1024]{4,3,2,1,0:T(8,128)(2,1)}, u32[]{:S(2)}) copy-start(bf16[1,1,1,384,1024]{4,3,2,1,0:T(8,128)(2,1)} %param.12) | copy-start | bytes 2359300
  1.8 0.9 %copy-start.3 = (bf16[1,1,1,1024,128]{4,3,2,1,0:T(8,128)(2,1)S(1)}, bf16[1,1,1,1024,128]{4,3,2,1,0:T(8,128)(2,1)}, u32[]{:S(2)}) copy-start(bf16[1,1,1,1024,128]{4,3,2,1,0:T(8,128)(2,1)} %param.11) | copy-start | bytes 786436
  2.7 3.4 %copy-start.6 = (bf16[1,3,128,128]{3,2,1,0:T(8,128)(2,1)S(1)}, bf16[1,3,128,128]{3,2,1,0:T(8,128)(2,1)}, u32[]{:S(2)}) copy-start(bf16[1,3,128,128]{3,2,1,0:T(8,128)(2,1)} %param.8) | copy-start | bytes 294916
  2.7 3.4 %copy-start.2 = (bf16[1,3,3,1,128,128]{5,4,3,2,1,0:T(8,128)(2,1)S(1)}, bf16[1,3,3,1,128,128]{5,4,3,2,1,0:T(8,128)(2,1)}, u32[]{:S(2)}) copy-start(bf16[1,3,3,1,128,128]{5,4,3,2,1,0:T(8,128)(2,1)} %param.9) | copy-start | bytes 884740
  3.1 7.2 %collective-permute-start = (bf16[3,128,128]{2,1,0:T(8,128)(2,1)S(1)}, bf16[3,128,128]{2,1,0:T(8,128)(2,1)S(1)}, u32[]{:S(2)}, u32[]{:S(2)}) collective-permute-start(bf16[3,128,128]{2,1,0:T(8,128)(2,1)S(1)} %get-tuple-element.18), channel_id=1, source_target_pairs={{0,16},{16,0},{1,17},{17,1},{2,18},{18,2},{3,19},{19,3},{4,20},{20... | collective-permute-start | bytes 294920 | tf_op jit(solution)/shard_map/ppermute | solution.py:19
  6.1 0.7 %copy-start.5 = (s32[12,12]{1,0:T(8,128)S(1)}, s32[12,12]{1,0:T(8,128)}, u32[]{:S(2)}) copy-start(s32[12,12]{1,0:T(8,128)} %pattern_ref.1) | copy-start | bytes 1732
  6.8 3.4 %copy-start.4 = (bf16[1,3,128,128]{3,2,1,0:T(8,128)(2,1)S(1)}, bf16[1,3,128,128]{3,2,1,0:T(8,128)(2,1)}, u32[]{:S(2)}) copy-start(bf16[1,3,128,128]{3,2,1,0:T(8,128)(2,1)} %param.7) | copy-start | bytes 294916
  7.7 5.5 %collective-permute-start.5 = (bf16[2,128,128]{2,1,0:T(8,128)(2,1)S(1)}, bf16[2,128,128]{2,1,0:T(8,128)(2,1)S(1)}, u32[]{:S(2)}, u32[]{:S(2)}) collective-permute-start(bf16[2,128,128]{2,1,0:T(8,128)(2,1)S(1)} %get-tuple-element.23), channel_id=1, source_target_pairs={{0,2},{1,3},{2,0},{3,1},{4,6},{5,7},{6,4},{7,5},{8,10},{9,11},{10,... | collective-permute-start | bytes 196616 | tf_op jit(solution)/shard_map/ppermute | solution.py:19
  10.3 7.4 %collective-permute-start.7 = (bf16[2,128,128]{2,1,0:T(8,128)(2,1)S(1)}, bf16[2,128,128]{2,1,0:T(8,128)(2,1)S(1)}, u32[]{:S(2)}, u32[]{:S(2)}) collective-permute-start(bf16[2,128,128]{2,1,0:T(8,128)(2,1)S(1)} %get-tuple-element.27), channel_id=1, source_target_pairs={{0,8},{4,12},{8,0},{12,4},{1,9},{5,13},{9,1},{13,5},{2,10},{6,14},... | collective-permute-start | bytes 196616 | tf_op jit(solution)/shard_map/ppermute | solution.py:19
  13.2 5.7 %collective-permute-start.1 = (bf16[3,128,128]{2,1,0:T(8,128)(2,1)S(1)}, bf16[3,128,128]{2,1,0:T(8,128)(2,1)S(1)}, u32[]{:S(2)}, u32[]{:S(2)}) collective-permute-start(bf16[3,128,128]{2,1,0:T(8,128)(2,1)S(1)} %add.9), channel_id=1, source_target_pairs={{0,2},{1,3},{2,0},{3,1},{4,6},{5,7},{6,4},{7,5},{8,10},{9,11},{10,... | collective-permute-start | bytes 294920 | tf_op jit(solution)/shard_map/ppermute | solution.py:19
  15.6 5.6 %collective-permute-start.6 = (bf16[4,128,128]{2,1,0:T(8,128)(2,1)S(1)}, bf16[4,128,128]{2,1,0:T(8,128)(2,1)S(1)}, u32[]{:S(2)}, u32[]{:S(2)}) collective-permute-start(bf16[4,128,128]{2,1,0:T(8,128)(2,1)S(1)} %pad_maximum_fusion.3), channel_id=1, source_target_pairs={{0,1},{1,0},{2,3},{3,2},{4,5},{5,4},{6,7},{7,6},{8,9},{9,8},{10,11... | collective-permute-start | bytes 393224 | tf_op jit(solution)/shard_map/ppermute | solution.py:19
  17.7 3.5 %collective-permute-start.8 = (bf16[4,128,128]{2,1,0:T(8,128)(2,1)S(1)}, bf16[4,128,128]{2,1,0:T(8,128)(2,1)S(1)}, u32[]{:S(2)}, u32[]{:S(2)}) collective-permute-start(bf16[4,128,128]{2,1,0:T(8,128)(2,1)S(1)} %pad_maximum_fusion.4), channel_id=1, source_target_pairs={{0,4},{4,0},{8,12},{12,8},{1,5},{5,1},{9,13},{13,9},{2,6},{6,2},{1... | collective-permute-start | bytes 393224 | tf_op jit(solution)/shard_map/ppermute | solution.py:19
  18.9 7.6 %collective-permute-start.2 = (bf16[3,128,128]{2,1,0:T(8,128)(2,1)S(1)}, bf16[3,128,128]{2,1,0:T(8,128)(2,1)S(1)}, u32[]{:S(2)}, u32[]{:S(2)}) collective-permute-start(bf16[3,128,128]{2,1,0:T(8,128)(2,1)S(1)} %add.10), channel_id=1, source_target_pairs={{0,1},{1,0},{2,3},{3,2},{4,5},{5,4},{6,7},{7,6},{8,9},{9,8},{10,11... | collective-permute-start | bytes 294920 | tf_op jit(solution)/shard_map/ppermute | solution.py:19
  21.5 9.6 %collective-permute-start.9 = (bf16[3,128,128]{2,1,0:T(8,128)(2,1)S(1)}, bf16[3,128,128]{2,1,0:T(8,128)(2,1)S(1)}, u32[]{:S(2)}, u32[]{:S(2)}) collective-permute-start(bf16[3,128,128]{2,1,0:T(8,128)(2,1)S(1)} %get-tuple-element.28), channel_id=1, source_target_pairs={{0,2},{1,3},{2,0},{3,1},{4,6},{5,7},{6,4},{7,5},{8,10},{9,11},{10,... | collective-permute-start | bytes 294920 | tf_op jit(solution)/shard_map/ppermute | solution.py:19
  24.4 6.7 %collective-permute-start.10 = (bf16[3,128,128]{2,1,0:T(8,128)(2,1)S(1)}, bf16[3,128,128]{2,1,0:T(8,128)(2,1)S(1)}, u32[]{:S(2)}, u32[]{:S(2)}) collective-permute-start(bf16[3,128,128]{2,1,0:T(8,128)(2,1)S(1)} %get-tuple-element.28), channel_id=1, source_target_pairs={{0,1},{1,0},{2,3},{3,2},{4,5},{5,4},{6,7},{7,6},{8,9},{9,8},{10,11... | collective-permute-start | bytes 294920 | tf_op jit(solution)/shard_map/ppermute | solution.py:19
  24.4 7.3 %collective-permute-start.11 = (bf16[3,128,128]{2,1,0:T(8,128)(2,1)S(1)}, bf16[3,128,128]{2,1,0:T(8,128)(2,1)S(1)}, u32[]{:S(2)}, u32[]{:S(2)}) collective-permute-start(bf16[3,128,128]{2,1,0:T(8,128)(2,1)S(1)} %get-tuple-element.28), channel_id=1, source_target_pairs={{0,3},{1,2},{2,1},{3,0},{4,7},{5,6},{6,5},{7,4},{8,11},{9,10},{10,... | collective-permute-start | bytes 294920 | tf_op jit(solution)/shard_map/ppermute | solution.py:19
  26.7 4.3 %collective-permute-start.3 = (bf16[2,128,128]{2,1,0:T(8,128)(2,1)S(1)}, bf16[2,128,128]{2,1,0:T(8,128)(2,1)S(1)}, u32[]{:S(2)}, u32[]{:S(2)}) collective-permute-start(bf16[2,128,128]{2,1,0:T(8,128)(2,1)S(1)} %get-tuple-element.19.solved_ref), channel_id=1, source_target_pairs={{0,8},{4,12},{8,0},{12,4},{1,9},{5,13},{9,1},{13,5},{2,10},{6,14},... | collective-permute-start | bytes 196616 | tf_op jit(solution)/shard_map/ppermute | solution.py:19
  28.2 6.3 %collective-permute-start.14 = (bf16[1,128,128]{2,1,0:T(8,128)(2,1)S(1)}, bf16[1,128,128]{2,1,0:T(8,128)(2,1)S(1)}, u32[]{:S(2)}, u32[]{:S(2)}) collective-permute-start(bf16[1,128,128]{2,1,0:T(8,128)(2,1)S(1)} %get-tuple-element.30), channel_id=1, source_target_pairs={{0,2},{1,3},{2,0},{3,1},{4,6},{5,7},{6,4},{7,5},{8,10},{9,11},{10,... | collective-permute-start | bytes 98312 | tf_op jit(solution)/shard_map/ppermute | solution.py:19
  31.0 1.4 %collective-permute-start.4 = (bf16[4,128,128]{2,1,0:T(8,128)(2,1)S(1)}, bf16[4,128,128]{2,1,0:T(8,128)(2,1)S(1)}, u32[]{:S(2)}, u32[]{:S(2)}) collective-permute-start(bf16[4,128,128]{2,1,0:T(8,128)(2,1)S(1)} %pad_maximum_fusion.2), channel_id=1, source_target_pairs={{0,4},{4,0},{8,12},{12,8},{1,5},{5,1},{9,13},{13,9},{2,6},{6,2},{1... | collective-permute-start | bytes 393224 | tf_op jit(solution)/shard_map/ppermute | solution.py:19
  33.0 6.0 %copy-start = (bf16[1,1,1,1024,384]{4,3,2,1,0:T(8,128)(2,1)S(1)}, bf16[1,1,1,1024,384]{4,3,2,1,0:T(8,128)(2,1)}, u32[]{:S(2)}) copy-start(bf16[1,1,1,1024,384]{4,3,2,1,0:T(8,128)(2,1)} %param.13) | copy-start | bytes 2359300
  33.0 4.3 %collective-permute-start.12 = (bf16[2,128,128]{2,1,0:T(8,128)(2,1)S(1)}, bf16[2,128,128]{2,1,0:T(8,128)(2,1)S(1)}, u32[]{:S(2)}, u32[]{:S(2)}) collective-permute-start(bf16[2,128,128]{2,1,0:T(8,128)(2,1)S(1)} %shard_map.90), channel_id=1, source_target_pairs={{0,8},{4,12},{8,0},{12,4},{1,9},{5,13},{9,1},{13,5},{2,10},{6,14},... | collective-permute-start | bytes 196616 | tf_op jit(solution)/shard_map/ppermute | solution.py:19
  34.6 4.3 %collective-permute-start.15 = (bf16[2,128,128]{2,1,0:T(8,128)(2,1)S(1)}, bf16[2,128,128]{2,1,0:T(8,128)(2,1)S(1)}, u32[]{:S(2)}, u32[]{:S(2)}) collective-permute-start(bf16[2,128,128]{2,1,0:T(8,128)(2,1)S(1)} %pad_maximum_fusion.7), channel_id=1, source_target_pairs={{0,1},{1,0},{2,3},{3,2},{4,5},{5,4},{6,7},{7,6},{8,9},{9,8},{10,11... | collective-permute-start | bytes 196616 | tf_op jit(solution)/shard_map/ppermute | solution.py:19
  37.4 1.6 %collective-permute-start.13 = (bf16[4,128,128]{2,1,0:T(8,128)(2,1)S(1)}, bf16[4,128,128]{2,1,0:T(8,128)(2,1)S(1)}, u32[]{:S(2)}, u32[]{:S(2)}) collective-permute-start(bf16[4,128,128]{2,1,0:T(8,128)(2,1)S(1)} %pad_maximum_fusion.5), channel_id=1, source_target_pairs={{0,4},{4,0},{8,12},{12,8},{1,5},{5,1},{9,13},{13,9},{2,6},{6,2},{1... | collective-permute-start | bytes 393224 | tf_op jit(solution)/shard_map/ppermute | solution.py:19

commit v5 on v4

--- a/solution.py
+++ b/solution.py
@@ -88,30 +88,36 @@
 
     part, kept = call(couple_kernel, [shaped(levels, width, count), shaped(*sub.shape)], [low, sub])
 
-    def mask_kernel(pattern_ref, inverse_ref, blocks_ref, early_ref, late_ref, column_ref):
-        row, col = lax.axis_index("pr"), lax.axis_index("pc")
-
-        def masked(level, b):
-            i, j = level * rows + row, b * cols + col
-            mark = pattern_ref[i, j] if b // per < level else pattern_ref[j, i]
-            return jnp.where(mark == 1, blocks_ref[level, b], jnp.zeros((width, width), bf16))
-
+    def masked(pattern_ref, block, level, b):
+        i, j = level * rows + lax.axis_index("pr"), b * cols + lax.axis_index("pc")
+        if b // per > level:
+            i, j = j, i
+        spot = [lax.broadcasted_iota(jnp.int32, pattern_ref.shape, axis) == at for axis, at in ((0, i), (1, j))]
+        marks = jnp.where(spot[0] & spot[1] & (pattern_ref[...] == 1), 1.0, 0.0)
+        return (block.astype(f32) * jnp.max(marks, axis=(0, 1), keepdims=True)).astype(bf16)
+
+    def early_kernel(pattern_ref, blocks_ref, early_ref):
         for m in range(per):
-            to_first, to_last = masked(MIDDLE, m), masked(MIDDLE, LAST * per + m)
-            early_ref[m] = masked(LAST, MIDDLE * per + m)
-            early_ref[per + m] = masked(FIRST, MIDDLE * per + m)
-            late_ref[m] = masked(LAST, m)
-            late_ref[per + m] = masked(FIRST, LAST * per + m)
+            early_ref[m] = masked(pattern_ref, blocks_ref[LAST, MIDDLE * per + m], LAST, MIDDLE * per + m)
+            early_ref[per + m] = masked(pattern_ref, blocks_ref[FIRST, MIDDLE * per + m], FIRST, MIDDLE * per + m)
+
+    def mask_kernel(pattern_ref, inverse_ref, blocks_ref, late_ref, column_ref):
+        for m in range(per):
+            to_first = masked(pattern_ref, blocks_ref[MIDDLE, m], MIDDLE, m)
+            to_last = masked(pattern_ref, blocks_ref[MIDDLE, LAST * per + m], MIDDLE, LAST * per + m)
+            late_ref[m] = masked(pattern_ref, blocks_ref[LAST, m], LAST, m)
+            late_ref[per + m] = masked(pattern_ref, blocks_ref[FIRST, LAST * per + m], FIRST, LAST * per + m)
             late_ref[2 * per + m] = to_last
             late_ref[3 * per + m] = to_first
             column_ref[m] = dot(inverse_ref[...], to_first).astype(bf16)
             column_ref[per + m] = to_last
 
-    early, late, column = call(
+    blocks = after(blocks, part)
+    (early,) = call(early_kernel, [shaped(2 * per, width, width)], [pattern, blocks])
+    late, column = call(
         mask_kernel,
-        [shaped(2 * per, width, width), shaped(4 * per, width, width), shaped(2 * per, width, width)],
-        [pattern, inverse[MIDDLE], after(blocks, part)],
-        in_specs=[SMEM, VMEM, VMEM],
+        [shaped(4 * per, width, width), shaped(2 * per, width, width)],
+        [pattern, inverse[MIDDLE], blocks],
     )
 
     def row_factor(ref, start):

time: 40.6 us -> 39.2 us (0.966)
  local copies, waits for them, and re-layouts: 2.9 us -> 2.23 us
  Pallas kernels: 3.52 us -> 3.08 us
    unnamed x20, local copies, waits for them, and re-layouts: 2.84 us -> 2.17 us
    pallas_call x6 -> x7, Pallas kernels: 3.52 us -> 3.08 us  [call(): pl.pallas_call(kernel, out_shape=outs, in_specs=in_specs or [VMEM] * len(...]
  transfers between devices with their start and end apart: 16 -> 16, of which waited for: 8 -> 8; matrix products, arithmetic and copies ran while one was open for 1% -> 1% of each run, Pallas kernels for 4% -> 3%
where the time goes in v5:
time: 39.2 us; the launch traced here: 39 us
  starting transfers between devices  24.5 us (62%)
  waiting for transfers between devices  8.14 us (21%)
  Pallas kernels  3.08 us (8%)
  local copies, waits for them, and re-layouts  2.23 us (6%)
  between operations  0.89 us (2%)
    ppermute x16, starting transfers between devices, hop(): return lax.ppermute(x, axis, [(i, i ^ offset) for i in range(size)])  24.5 us
    ppermute x16, waiting for transfers between devices, hop(): return lax.ppermute(x, axis, [(i, i ^ offset) for i in range(size)])  8.14 us
    pallas_call x7, Pallas kernels, call(): pl.pallas_call(kernel, out_shape=outs, in_specs=in_specs or [VMEM] * len(...  3.08 us
    unnamed x20, local copies, waits for them, and re-layouts  2.17 us
  transfers between devices with their start and end apart: 16, of which 8 were waited for; matrix products, arithmetic and copies ran while one was open for 1% of the time, Pallas kernels for 3%

profile of v5, /device:TPU:0, one launch (start us, length us, event | category | flops | bytes accessed | tf_op | source)
XLA Modules:
  0.0 39.0 jit_solution(10515807248958600494)
XLA Ops:
  0.6 0.0 copy-start.2
  0.6 1.1 %copy-done.2 = bf16[1,1,1,384,1024]{4,3,2,1,0:T(8,128)(2,1)S(1)} copy-done((bf16[1,1,1,384,1024]{4,3,2,1,0:T(8,128)(2,1)S(1)}, bf16[1,1,1,384,1024]{4,3,2,1,0:T(8,128)(2,1)}, u32[]{:S(2)}) %copy-start.2) | copy-done | bytes 786456
  1.8 0.0 copy-start.3
  1.8 0.9 %copy-done.3 = bf16[1,1,1,1024,128]{4,3,2,1,0:T(8,128)(2,1)S(1)} copy-done((bf16[1,1,1,1024,128]{4,3,2,1,0:T(8,128)(2,1)S(1)}, bf16[1,1,1,1024,128]{4,3,2,1,0:T(8,128)(2,1)}, u32[]{:S(2)}) %copy-start.3) | copy-done | bytes 262168
  2.7 0.0 copy-start
  2.7 0.0 copy-start.5
  2.7 0.4 %shard_map.86 = (bf16[3,128,128]{2,1,0:T(8,128)(2,1)S(1)}, bf16[1024,128]{1,0:T(8,128)(2,1)S(1)}) custom-call(bf16[384,1024]{1,0:T(8,128)(2,1)S(1)} %bitcast.18, bf16[1024,128]{1,0:T(8,128)(2,1)S(1)} %bitcast.19), custom_call_target="tpu_custom_call" | custom-call | tf_op jit(solution)/shard_map/pallas_call | solution.py:60
  3.1 3.0 %collective-permute-start = (bf16[3,128,128]{2,1,0:T(8,128)(2,1)S(1)}, bf16[3,128,128]{2,1,0:T(8,128)(2,1)S(1)}, u32[]{:S(2)}, u32[]{:S(2)}) collective-permute-start(bf16[3,128,128]{2,1,0:T(8,128)(2,1)S(1)} %get-tuple-element.17), channel_id=1, source_target_pairs={{0,16},{16,0},{1,17},{17,1},{2,18},{18,2},{3,19},{19,3},{4,20},{20... | collective-permute-start | bytes 294920 | tf_op jit(solution)/shard_map/ppermute | solution.py:19
  6.1 0.0 copy-done
  6.1 0.0 copy-done.5
  6.1 0.0 copy-start.6
  6.1 0.1 shard_map.88
  6.3 0.0 copy-start.4
  6.3 2.7 %collective-permute-start.5 = (bf16[2,128,128]{2,1,0:T(8,128)(2,1)S(1)}, bf16[2,128,128]{2,1,0:T(8,128)(2,1)S(1)}, u32[]{:S(2)}, u32[]{:S(2)}) collective-permute-start(bf16[2,128,128]{2,1,0:T(8,128)(2,1)S(1)} %shard_map.88), channel_id=1, source_target_pairs={{0,2},{1,3},{2,0},{3,1},{4,6},{5,7},{6,4},{7,5},{8,10},{9,11},{10,... | collective-permute-start | bytes 196616 | tf_op jit(solution)/shard_map/ppermute | solution.py:19
  8.9 0.0 copy-done.6
  9.0 0.0 copy-done.4
  9.0 0.3 shard_map.89
  9.2 0.0 collective-permute-done
  9.3 1.6 %collective-permute-start.7 = (bf16[2,128,128]{2,1,0:T(8,128)(2,1)S(1)}, bf16[2,128,128]{2,1,0:T(8,128)(2,1)S(1)}, u32[]{:S(2)}, u32[]{:S(2)}) collective-permute-start(bf16[2,128,128]{2,1,0:T(8,128)(2,1)S(1)} %get-tuple-element.25), channel_id=1, source_target_pairs={{0,8},{4,12},{8,0},{12,4},{1,9},{5,13},{9,1},{13,5},{2,10},{6,14},... | collective-permute-start | bytes 196616 | tf_op jit(solution)/shard_map/ppermute | solution.py:19
  10.9 0.9 %collective-permute-done.5 = bf16[2,128,128]{2,1,0:T(8,128)(2,1)S(1)} collective-permute-done((bf16[2,128,128]{2,1,0:T(8,128)(2,1)S(1)}, bf16[2,128,128]{2,1,0:T(8,128)(2,1)S(1)}, u32[]{:S(2)}, u32[]{:S(2)}) %collective-permute-start.5) | collective-permute-done | bytes 65568 | tf_op jit(solution)/shard_map/ppermute | solution.py:19
  11.8 2.4 %collective-permute-start.1 = (bf16[3,128,128]{2,1,0:T(8,128)(2,1)S(1)}, bf16[3,128,128]{2,1,0:T(8,128)(2,1)S(1)}, u32[]{:S(2)}, u32[]{:S(2)}) collective-permute-start(bf16[3,128,128]{2,1,0:T(8,128)(2,1)S(1)} %add.9), channel_id=1, source_target_pairs={{0,2},{1,3},{2,0},{3,1},{4,6},{5,7},{6,4},{7,5},{8,10},{9,11},{10,... | collective-permute-start | bytes 294920 | tf_op jit(solution)/shard_map/ppermute | solution.py:19
  14.2 2.1 %collective-permute-start.6 = (bf16[4,128,128]{2,1,0:T(8,128)(2,1)S(1)}, bf16[4,128,128]{2,1,0:T(8,128)(2,1)S(1)}, u32[]{:S(2)}, u32[]{:S(2)}) collective-permute-start(bf16[4,128,128]{2,1,0:T(8,128)(2,1)S(1)} %pad_maximum_fusion.3), channel_id=1, source_target_pairs={{0,1},{1,0},{2,3},{3,2},{4,5},{5,4},{6,7},{7,6},{8,9},{9,8},{10,11... | collective-permute-start | bytes 393224 | tf_op jit(solution)/shard_map/ppermute | solution.py:19
  16.4 0.0 collective-permute-done.7
  16.4 0.1 collective-permute-start.8
  16.5 1.1 %collective-permute-done.1 = bf16[3,128,128]{2,1,0:T(8,128)(2,1)S(1)} collective-permute-done((bf16[3,128,128]{2,1,0:T(8,128)(2,1)S(1)}, bf16[3,128,128]{2,1,0:T(8,128)(2,1)S(1)}, u32[]{:S(2)}, u32[]{:S(2)}) %collective-permute-start.1) | collective-permute-done | bytes 98336 | tf_op jit(solution)/shard_map/ppermute | solution.py:19
  17.6 1.8 %collective-permute-start.2 = (bf16[3,128,128]{2,1,0:T(8,128)(2,1)S(1)}, bf16[3,128,128]{2,1,0:T(8,128)(2,1)S(1)}, u32[]{:S(2)}, u32[]{:S(2)}) collective-permute-start(bf16[3,128,128]{2,1,0:T(8,128)(2,1)S(1)} %add.10), channel_id=1, source_target_pairs={{0,1},{1,0},{2,3},{3,2},{4,5},{5,4},{6,7},{7,6},{8,9},{9,8},{10,11... | collective-permute-start | bytes 294920 | tf_op jit(solution)/shard_map/ppermute | solution.py:19
  19.3 0.6 %collective-permute-done.6 = bf16[4,128,128]{2,1,0:T(8,128)(2,1)S(1)} collective-permute-done((bf16[4,128,128]{2,1,0:T(8,128)(2,1)S(1)}, bf16[4,128,128]{2,1,0:T(8,128)(2,1)S(1)}, u32[]{:S(2)}, u32[]{:S(2)}) %collective-permute-start.6) | collective-permute-done | bytes 131104 | tf_op jit(solution)/shard_map/ppermute | solution.py:19
  19.9 0.0 collective-permute-done.8
  20.0 0.2 shard_map.90
  20.2 2.9 %collective-permute-start.9 = (bf16[3,128,128]{2,1,0:T(8,128)(2,1)S(1)}, bf16[3,128,128]{2,1,0:T(8,128)(2,1)S(1)}, u32[]{:S(2)}, u32[]{:S(2)}) collective-permute-start(bf16[3,128,128]{2,1,0:T(8,128)(2,1)S(1)} %get-tuple-element.26), channel_id=1, source_target_pairs={{0,2},{1,3},{2,0},{3,1},{4,6},{5,7},{6,4},{7,5},{8,10},{9,11},{10,... | collective-permute-start | bytes 294920 | tf_op jit(solution)/shard_map/ppermute | solution.py:19
  23.1 0.0 collective-permute-start.10
  23.1 2.0 %collective-permute-start.11 = (bf16[3,128,128]{2,1,0:T(8,128)(2,1)S(1)}, bf16[3,128,128]{2,1,0:T(8,128)(2,1)S(1)}, u32[]{:S(2)}, u32[]{:S(2)}) collective-permute-start(bf16[3,128,128]{2,1,0:T(8,128)(2,1)S(1)} %get-tuple-element.26), channel_id=1, source_target_pairs={{0,3},{1,2},{2,1},{3,0},{4,7},{5,6},{6,5},{7,4},{8,11},{9,10},{10,... | collective-permute-start | bytes 294920 | tf_op jit(solution)/shard_map/ppermute | solution.py:19
  25.1 0.0 collective-permute-done.2
  25.2 0.2 shard_map.87
  25.3 1.6 %collective-permute-start.3 = (bf16[2,128,128]{2,1,0:T(8,128)(2,1)S(1)}, bf16[2,128,128]{2,1,0:T(8,128)(2,1)S(1)}, u32[]{:S(2)}, u32[]{:S(2)}) collective-permute-start(bf16[2,128,128]{2,1,0:T(8,128)(2,1)S(1)} %get-tuple-element.18.solved_ref), channel_id=1, source_target_pairs={{0,8},{4,12},{8,0},{12,4},{1,9},{5,13},{9,1},{13,5},{2,10},{6,14},... | collective-permute-start | bytes 196616 | tf_op jit(solution)/shard_map/ppermute | solution.py:19
  26.9 1.5 %collective-permute-start.14 = (bf16[1,128,128]{2,1,0:T(8,128)(2,1)S(1)}, bf16[1,128,128]{2,1,0:T(8,128)(2,1)S(1)}, u32[]{:S(2)}, u32[]{:S(2)}) collective-permute-start(bf16[1,128,128]{2,1,0:T(8,128)(2,1)S(1)} %get-tuple-element.28), channel_id=1, source_target_pairs={{0,2},{1,3},{2,0},{3,1},{4,6},{5,7},{6,4},{7,5},{8,10},{9,11},{10,... | collective-permute-start | bytes 98312 | tf_op jit(solution)/shard_map/ppermute | solution.py:19
  28.4 1.3 %collective-permute-done.3 = bf16[2,128,128]{2,1,0:T(8,128)(2,1)S(1)} collective-permute-done((bf16[2,128,128]{2,1,0:T(8,128)(2,1)S(1)}, bf16[2,128,128]{2,1,0:T(8,128)(2,1)S(1)}, u32[]{:S(2)}, u32[]{:S(2)}) %collective-permute-start.3) | collective-permute-done | bytes 65568 | tf_op jit(solution)/shard_map/ppermute | solution.py:19
  29.7 0.1 collective-permute-start.4
  29.8 0.0 collective-permute-done.9
  29.8 0.0 collective-permute-done.10
  29.8 0.6 %collective-permute-done.11 = bf16[3,128,128]{2,1,0:T(8,128)(2,1)S(1)} collective-permute-done((bf16[3,128,128]{2,1,0:T(8,128)(2,1)S(1)}, bf16[3,128,128]{2,1,0:T(8,128)(2,1)S(1)}, u32[]{:S(2)}, u32[]{:S(2)}) %collective-permute-start.11) | collective-permute-done | bytes 98336 | tf_op jit(solution)/shard_map/ppermute | solution.py:19
  30.5 0.6 %collective-permute-done.4 = bf16[4,128,128]{2,1,0:T(8,128)(2,1)S(1)} collective-permute-done((bf16[4,128,128]{2,1,0:T(8,128)(2,1)S(1)}, bf16[4,128,128]{2,1,0:T(8,128)(2,1)S(1)}, u32[]{:S(2)}, u32[]{:S(2)}) %collective-permute-start.4) | collective-permute-done | bytes 131104 | tf_op jit(solution)/shard_map/ppermute | solution.py:19
  31.1 0.5 %shard_map.91 = bf16[2,128,128]{2,1,0:T(8,128)(2,1)S(1)} custom-call(bf16[128,128]{1,0:T(8,128)(2,1)S(1)} %get-tuple-element.34.middle_inverse_ref.inverse_ref, bf16[128,128]{1,0:T(8,128)(2,1)S(1)} %get-tuple-element.32.last_inverse_ref, bf16[128,128]{1,0:T(8,128)(2,1)S(1)} %slice_bitcast_fusion.rhs_ref, bf16[3,128,128]{2,1,0:T(8,128)(2,1)S(1)} %add.11.total_ref.sum_ref, ...), custom_call_target="tpu_custom_call" | custom-call | tf_op jit(solution)/shard_map/pallas_call | solution.py:60
  31.7 0.0 copy-start.1
  31.7 1.6 %collective-permute-start.12 = (bf16[2,128,128]{2,1,0:T(8,128)(2,1)S(1)}, bf16[2,128,128]{2,1,0:T(8,128)(2,1)S(1)}, u32[]{:S(2)}, u32[]{:S(2)}) collective-permute-start(bf16[2,128,128]{2,1,0:T(8,128)(2,1)S(1)} %shard_map.91), channel_id=1, source_target_pairs={{0,8},{4,12},{8,0},{12,4},{1,9},{5,13},{9,1},{13,5},{2,10},{6,14},... | collective-permute-start | bytes 196616 | tf_op jit(solution)/shard_map/ppermute | solution.py:19
  33.3 0.0 collective-permute-done.14
  33.3 1.2 %collective-permute-start.15 = (bf16[2,128,128]{2,1,0:T(8,128)(2,1)S(1)}, bf16[2,128,128]{2,1,0:T(8,128)(2,1)S(1)}, u32[]{:S(2)}, u32[]{:S(2)}) collective-permute-start(bf16[2,128,128]{2,1,0:T(8,128)(2,1)S(1)} %pad_maximum_fusion.7), channel_id=1, source_target_pairs={{0,1},{1,0},{2,3},{3,2},{4,5},{5,4},{6,7},{7,6},{8,9},{9,8},{10,11... | collective-permute-start | bytes 196616 | tf_op jit(solution)/shard_map/ppermute | solution.py:19
  34.5 1.5 %collective-permute-done.12 = bf16[2,128,128]{2,1,0:T(8,128)(2,1)S(1)} collective-permute-done((bf16[2,128,128]{2,1,0:T(8,128)(2,1)S(1)}, bf16[2,128,128]{2,1,0:T(8,128)(2,1)S(1)}, u32[]{:S(2)}, u32[]{:S(2)}) %collective-permute-start.12) | collective-permute-done | bytes 65568 | tf_op jit(solution)/shard_map/ppermute | solution.py:19
  36.0 0.1 collective-permute-start.13
  36.1 1.5 %collective-permute-done.15 = bf16[2,128,128]{2,1,0:T(8,128)(2,1)S(1)} collective-permute-done((bf16[2,128,128]{2,1,0:T(8,128)(2,1)S(1)}, bf16[2,128,128]{2,1,0:T(8,128)(2,1)S(1)}, u32[]{:S(2)}, u32[]{:S(2)}) %collective-permute-start.15) | collective-permute-done | bytes 65568 | tf_op jit(solution)/shard_map/ppermute | solution.py:19
  37.6 0.0 collective-permute-done.13
  37.7 0.0 copy-done.1
  37.7 1.4 %shard_map.92 = (bf16[3,128,128]{2,1,0:T(8,128)(2,1)}, bf16[1024,128]{1,0:T(8,128)(2,1)}) custom-call(bf16[2,128,128]{2,1,0:T(8,128)(2,1)S(1)} %get-tuple-element.18.solved_ref, bf16[1024,384]{1,0:T(8,128)(2,1)S(1)} %bitcast.17, bf16[1024,128]{1,0:T(8,128)(2,1)S(1)} %get-tuple-element.19.sub_ref, bf16[8,128,128]{2,1,0:T(8,128)(2,1)S(1)} %pad_maximum_fusion.1.ends_ref, ...), custom_call_target="tpu_custom_call" | custom-call | tf_op jit(solution)/shard_map/pallas_call | solution.py:60
  (22 shorter events, 0.4 us)
Async XLA Ops:
  0.6 1.1 %copy-start.2 = (bf16[1,1,1,384,1024]{4,3,2,1,0:T(8,128)(2,1)S(1)}, bf16[1,1,1,384,1024]{4,3,2,1,0:T(8,128)(2,1)}, u32[]{:S(2)}) copy-start(bf16[1,1,1,384,1024]{4,3,2,1,0:T(8,128)(2,1)} %param.12) | copy-start | bytes 2359300
  1.8 0.9 %copy-start.3 = (bf16[1,1,1,1024,128]{4,3,2,1,0:T(8,128)(2,1)S(1)}, bf16[1,1,1,1024,128]{4,3,2,1,0:T(8,128)(2,1)}, u32[]{:S(2)}) copy-start(bf16[1,1,1,1024,128]{4,3,2,1,0:T(8,128)(2,1)} %param.11) | copy-start | bytes 786436
  2.7 3.4 %copy-start = (bf16[1,3,3,1,128,128]{5,4,3,2,1,0:T(8,128)(2,1)S(1)}, bf16[1,3,3,1,128,128]{5,4,3,2,1,0:T(8,128)(2,1)}, u32[]{:S(2)}) copy-start(bf16[1,3,3,1,128,128]{5,4,3,2,1,0:T(8,128)(2,1)} %param.9) | copy-start | bytes 884740
  2.7 3.4 %copy-start.5 = (s32[12,12]{1,0:T(8,128)S(1)}, s32[12,12]{1,0:T(8,128)}, u32[]{:S(2)}) copy-start(s32[12,12]{1,0:T(8,128)} %pattern_ref.3) | copy-start | bytes 1732
  3.1 6.1 %collective-permute-start = (bf16[3,128,128]{2,1,0:T(8,128)(2,1)S(1)}, bf16[3,128,128]{2,1,0:T(8,128)(2,1)S(1)}, u32[]{:S(2)}, u32[]{:S(2)}) collective-permute-start(bf16[3,128,128]{2,1,0:T(8,128)(2,1)S(1)} %get-tuple-element.17), channel_id=1, source_target_pairs={{0,16},{16,0},{1,17},{17,1},{2,18},{18,2},{3,19},{19,3},{4,20},{20... | collective-permute-start | bytes 294920 | tf_op jit(solution)/shard_map/ppermute | solution.py:19
  6.1 2.8 %copy-start.6 = (bf16[1,3,128,128]{3,2,1,0:T(8,128)(2,1)S(1)}, bf16[1,3,128,128]{3,2,1,0:T(8,128)(2,1)}, u32[]{:S(2)}) copy-start(bf16[1,3,128,128]{3,2,1,0:T(8,128)(2,1)} %param.8) | copy-start | bytes 294916
  6.3 2.7 %copy-start.4 = (bf16[1,3,128,128]{3,2,1,0:T(8,128)(2,1)S(1)}, bf16[1,3,128,128]{3,2,1,0:T(8,128)(2,1)}, u32[]{:S(2)}) copy-start(bf16[1,3,128,128]{3,2,1,0:T(8,128)(2,1)} %param.7) | copy-start | bytes 294916
  6.3 5.5 %collective-permute-start.5 = (bf16[2,128,128]{2,1,0:T(8,128)(2,1)S(1)}, bf16[2,128,128]{2,1,0:T(8,128)(2,1)S(1)}, u32[]{:S(2)}, u32[]{:S(2)}) collective-permute-start(bf16[2,128,128]{2,1,0:T(8,128)(2,1)S(1)} %shard_map.88), channel_id=1, source_target_pairs={{0,2},{1,3},{2,0},{3,1},{4,6},{5,7},{6,4},{7,5},{8,10},{9,11},{10,... | collective-permute-start | bytes 196616 | tf_op jit(solution)/shard_map/ppermute | solution.py:19
  9.3 7.1 %collective-permute-start.7 = (bf16[2,128,128]{2,1,0:T(8,128)(2,1)S(1)}, bf16[2,128,128]{2,1,0:T(8,128)(2,1)S(1)}, u32[]{:S(2)}, u32[]{:S(2)}) collective-permute-start(bf16[2,128,128]{2,1,0:T(8,128)(2,1)S(1)} %get-tuple-element.25), channel_id=1, source_target_pairs={{0,8},{4,12},{8,0},{12,4},{1,9},{5,13},{9,1},{13,5},{2,10},{6,14},... | collective-permute-start | bytes 196616 | tf_op jit(solution)/shard_map/ppermute | solution.py:19
  11.8 5.7 %collective-permute-start.1 = (bf16[3,128,128]{2,1,0:T(8,128)(2,1)S(1)}, bf16[3,128,128]{2,1,0:T(8,128)(2,1)S(1)}, u32[]{:S(2)}, u32[]{:S(2)}) collective-permute-start(bf16[3,128,128]{2,1,0:T(8,128)(2,1)S(1)} %add.9), channel_id=1, source_target_pairs={{0,2},{1,3},{2,0},{3,1},{4,6},{5,7},{6,4},{7,5},{8,10},{9,11},{10,... | collective-permute-start | bytes 294920 | tf_op jit(solution)/shard_map/ppermute | solution.py:19
  14.2 5.6 %collective-permute-start.6 = (bf16[4,128,128]{2,1,0:T(8,128)(2,1)S(1)}, bf16[4,128,128]{2,1,0:T(8,128)(2,1)S(1)}, u32[]{:S(2)}, u32[]{:S(2)}) collective-permute-start(bf16[4,128,128]{2,1,0:T(8,128)(2,1)S(1)} %pad_maximum_fusion.3), channel_id=1, source_target_pairs={{0,1},{1,0},{2,3},{3,2},{4,5},{5,4},{6,7},{7,6},{8,9},{9,8},{10,11... | collective-permute-start | bytes 393224 | tf_op jit(solution)/shard_map/ppermute | solution.py:19
  16.4 3.5 %collective-permute-start.8 = (bf16[4,128,128]{2,1,0:T(8,128)(2,1)S(1)}, bf16[4,128,128]{2,1,0:T(8,128)(2,1)S(1)}, u32[]{:S(2)}, u32[]{:S(2)}) collective-permute-start(bf16[4,128,128]{2,1,0:T(8,128)(2,1)S(1)} %pad_maximum_fusion.4), channel_id=1, source_target_pairs={{0,4},{4,0},{8,12},{12,8},{1,5},{5,1},{9,13},{13,9},{2,6},{6,2},{1... | collective-permute-start | bytes 393224 | tf_op jit(solution)/shard_map/ppermute | solution.py:19
  17.6 7.6 %collective-permute-start.2 = (bf16[3,128,128]{2,1,0:T(8,128)(2,1)S(1)}, bf16[3,128,128]{2,1,0:T(8,128)(2,1)S(1)}, u32[]{:S(2)}, u32[]{:S(2)}) collective-permute-start(bf16[3,128,128]{2,1,0:T(8,128)(2,1)S(1)} %add.10), channel_id=1, source_target_pairs={{0,1},{1,0},{2,3},{3,2},{4,5},{5,4},{6,7},{7,6},{8,9},{9,8},{10,11... | collective-permute-start | bytes 294920 | tf_op jit(solution)/shard_map/ppermute | solution.py:19
  20.2 9.6 %collective-permute-start.9 = (bf16[3,128,128]{2,1,0:T(8,128)(2,1)S(1)}, bf16[3,128,128]{2,1,0:T(8,128)(2,1)S(1)}, u32[]{:S(2)}, u32[]{:S(2)}) collective-permute-start(bf16[3,128,128]{2,1,0:T(8,128)(2,1)S(1)} %get-tuple-element.26), channel_id=1, source_target_pairs={{0,2},{1,3},{2,0},{3,1},{4,6},{5,7},{6,4},{7,5},{8,10},{9,11},{10,... | collective-permute-start | bytes 294920 | tf_op jit(solution)/shard_map/ppermute | solution.py:19
  23.1 6.7 %collective-permute-start.10 = (bf16[3,128,128]{2,1,0:T(8,128)(2,1)S(1)}, bf16[3,128,128]{2,1,0:T(8,128)(2,1)S(1)}, u32[]{:S(2)}, u32[]{:S(2)}) collective-permute-start(bf16[3,128,128]{2,1,0:T(8,128)(2,1)S(1)} %get-tuple-element.26), channel_id=1, source_target_pairs={{0,1},{1,0},{2,3},{3,2},{4,5},{5,4},{6,7},{7,6},{8,9},{9,8},{10,11... | collective-permute-start | bytes 294920 | tf_op jit(solution)/shard_map/ppermute | solution.py:19
  23.1 7.3 %collective-permute-start.11 = (bf16[3,128,128]{2,1,0:T(8,128)(2,1)S(1)}, bf16[3,128,128]{2,1,0:T(8,128)(2,1)S(1)}, u32[]{:S(2)}, u32[]{:S(2)}) collective-permute-start(bf16[3,128,128]{2,1,0:T(8,128)(2,1)S(1)} %get-tuple-element.26), channel_id=1, source_target_pairs={{0,3},{1,2},{2,1},{3,0},{4,7},{5,6},{6,5},{7,4},{8,11},{9,10},{10,... | collective-permute-start | bytes 294920 | tf_op jit(solution)/shard_map/ppermute | solution.py:19
  25.3 4.3 %collective-permute-start.3 = (bf16[2,128,128]{2,1,0:T(8,128)(2,1)S(1)}, bf16[2,128,128]{2,1,0:T(8,128)(2,1)S(1)}, u32[]{:S(2)}, u32[]{:S(2)}) collective-permute-start(bf16[2,128,128]{2,1,0:T(8,128)(2,1)S(1)} %get-tuple-element.18.solved_ref), channel_id=1, source_target_pairs={{0,8},{4,12},{8,0},{12,4},{1,9},{5,13},{9,1},{13,5},{2,10},{6,14},... | collective-permute-start | bytes 196616 | tf_op jit(solution)/shard_map/ppermute | solution.py:19
  26.9 6.3 %collective-permute-start.14 = (bf16[1,128,128]{2,1,0:T(8,128)(2,1)S(1)}, bf16[1,128,128]{2,1,0:T(8,128)(2,1)S(1)}, u32[]{:S(2)}, u32[]{:S(2)}) collective-permute-start(bf16[1,128,128]{2,1,0:T(8,128)(2,1)S(1)} %get-tuple-element.28), channel_id=1, source_target_pairs={{0,2},{1,3},{2,0},{3,1},{4,6},{5,7},{6,4},{7,5},{8,10},{9,11},{10,... | collective-permute-start | bytes 98312 | tf_op jit(solution)/shard_map/ppermute | solution.py:19
  29.7 1.4 %collective-permute-start.4 = (bf16[4,128,128]{2,1,0:T(8,128)(2,1)S(1)}, bf16[4,128,128]{2,1,0:T(8,128)(2,1)S(1)}, u32[]{:S(2)}, u32[]{:S(2)}) collective-permute-start(bf16[4,128,128]{2,1,0:T(8,128)(2,1)S(1)} %pad_maximum_fusion.2), channel_id=1, source_target_pairs={{0,4},{4,0},{8,12},{12,8},{1,5},{5,1},{9,13},{13,9},{2,6},{6,2},{1... | collective-permute-start | bytes 393224 | tf_op jit(solution)/shard_map/ppermute | solution.py:19
  31.7 6.0 %copy-start.1 = (bf16[1,1,1,1024,384]{4,3,2,1,0:T(8,128)(2,1)S(1)}, bf16[1,1,1,1024,384]{4,3,2,1,0:T(8,128)(2,1)}, u32[]{:S(2)}) copy-start(bf16[1,1,1,1024,384]{4,3,2,1,0:T(8,128)(2,1)} %param.13) | copy-start | bytes 2359300
  31.7 4.3 %collective-permute-start.12 = (bf16[2,128,128]{2,1,0:T(8,128)(2,1)S(1)}, bf16[2,128,128]{2,1,0:T(8,128)(2,1)S(1)}, u32[]{:S(2)}, u32[]{:S(2)}) collective-permute-start(bf16[2,128,128]{2,1,0:T(8,128)(2,1)S(1)} %shard_map.91), channel_id=1, source_target_pairs={{0,8},{4,12},{8,0},{12,4},{1,9},{5,13},{9,1},{13,5},{2,10},{6,14},... | collective-permute-start | bytes 196616 | tf_op jit(solution)/shard_map/ppermute | solution.py:19
  33.3 4.3 %collective-permute-start.15 = (bf16[2,128,128]{2,1,0:T(8,128)(2,1)S(1)}, bf16[2,128,128]{2,1,0:T(8,128)(2,1)S(1)}, u32[]{:S(2)}, u32[]{:S(2)}) collective-permute-start(bf16[2,128,128]{2,1,0:T(8,128)(2,1)S(1)} %pad_maximum_fusion.7), channel_id=1, source_target_pairs={{0,1},{1,0},{2,3},{3,2},{4,5},{5,4},{6,7},{7,6},{8,9},{9,8},{10,11... | collective-permute-start | bytes 196616 | tf_op jit(solution)/shard_map/ppermute | solution.py:19
  36.0 1.6 %collective-permute-start.13 = (bf16[4,128,128]{2,1,0:T(8,128)(2,1)S(1)}, bf16[4,128,128]{2,1,0:T(8,128)(2,1)S(1)}, u32[]{:S(2)}, u32[]{:S(2)}) collective-permute-start(bf16[4,128,128]{2,1,0:T(8,128)(2,1)S(1)} %pad_maximum_fusion.5), channel_id=1, source_target_pairs={{0,4},{4,0},{8,12},{12,8},{1,5},{5,1},{9,13},{13,9},{2,6},{6,2},{1... | collective-permute-start | bytes 393224 | tf_op jit(solution)/shard_map/ppermute | solution.py:19

commit v6 on v5

--- a/solution.py
+++ b/solution.py
@@ -82,11 +82,7 @@
     row_order, col_order = offsets("pr"), offsets("pc")
 
 
-    def couple_kernel(low_ref, sub_ref, part_ref, kept_ref):
-        kept_ref[...] = sub_ref[...]
-        part_ref[...] = dot(low_ref[...], sub_ref[...]).astype(bf16).reshape(levels, width, count)
-
-    part, kept = call(couple_kernel, [shaped(levels, width, count), shaped(*sub.shape)], [low, sub])
+    part = dot(low, sub).astype(bf16).reshape(levels, width, count)
 
     def masked(pattern_ref, block, level, b):
         i, j = level * rows + lax.axis_index("pr"), b * cols + lax.axis_index("pc")
@@ -101,7 +97,8 @@
             early_ref[m] = masked(pattern_ref, blocks_ref[LAST, MIDDLE * per + m], LAST, MIDDLE * per + m)
             early_ref[per + m] = masked(pattern_ref, blocks_ref[FIRST, MIDDLE * per + m], FIRST, MIDDLE * per + m)
 
-    def mask_kernel(pattern_ref, inverse_ref, blocks_ref, late_ref, column_ref):
+    def mask_kernel(pattern_ref, inverse_ref, blocks_ref, sub_ref, late_ref, column_ref, kept_ref):
+        kept_ref[...] = sub_ref[...]
         for m in range(per):
             to_first = masked(pattern_ref, blocks_ref[MIDDLE, m], MIDDLE, m)
             to_last = masked(pattern_ref, blocks_ref[MIDDLE, LAST * per + m], MIDDLE, LAST * per + m)
@@ -114,10 +111,10 @@
 
     blocks = after(blocks, part)
     (early,) = call(early_kernel, [shaped(2 * per, width, width)], [pattern, blocks])
-    late, column = call(
+    late, column, kept = call(
         mask_kernel,
-        [shaped(4 * per, width, width), shaped(2 * per, width, width)],
-        [pattern, inverse[MIDDLE], blocks],
+        [shaped(4 * per, width, width), shaped(2 * per, width, width), shaped(*sub.shape)],
+        [pattern, inverse[MIDDLE], blocks, sub],
     )
 
     def row_factor(ref, start):

time: 39.2 us -> 39.2 us (level)
  matrix products: 0 us -> 1.33 us
  local copies, waits for them, and re-layouts: 2.23 us -> 1.28 us
    dot_general x0 -> x1, matrix products: none -> 1.33 us  [dot(): return jnp.dot(a, b, preferred_element_type=jnp.float32)]
    unnamed x20, local copies, waits for them, and re-layouts: 2.17 us -> 1.22 us
    pallas_call x7 -> x6, Pallas kernels: 3.08 us -> 2.69 us  [call(): pl.pallas_call(kernel, out_shape=outs, in_specs=in_specs or [VMEM] * len(...]
where the time goes in v6:
time: 39.2 us; the launch traced here: 39 us
  starting transfers between devices  24.5 us (62%)
  waiting for transfers between devices  8.12 us (21%)
  Pallas kernels  2.69 us (7%)
  matrix products  1.33 us (3%)
  local copies, waits for them, and re-layouts  1.28 us (3%)
  between operations  0.91 us (2%)
    ppermute x16, starting transfers between devices, hop(): return lax.ppermute(x, axis, [(i, i ^ offset) for i in range(size)])  24.5 us
    ppermute x16, waiting for transfers between devices, hop(): return lax.ppermute(x, axis, [(i, i ^ offset) for i in range(size)])  8.12 us
    pallas_call x6, Pallas kernels, call(): pl.pallas_call(kernel, out_shape=outs, in_specs=in_specs or [VMEM] * len(...  2.69 us
    dot_general x1, matrix products, dot(): return jnp.dot(a, b, preferred_element_type=jnp.float32)  1.33 us
    unnamed x20, local copies, waits for them, and re-layouts  1.22 us
  transfers between devices with their start and end apart: 16, of which 8 were waited for; matrix products, arithmetic and copies ran while one was open for 1% of the time, Pallas kernels for 3%

profile of v6, /device:TPU:0, one launch (start us, length us, event | category | flops | bytes accessed | tf_op | source)
XLA Modules:
  0.0 39.0 jit_solution(401323109463075171)
XLA Ops:
  0.6 0.0 copy-start
  0.6 0.0 copy-start.1
  0.7 1.1 %copy-done = bf16[1,1,1,384,1024]{4,3,2,1,0:T(8,128)(2,1)S(1)} copy-done((bf16[1,1,1,384,1024]{4,3,2,1,0:T(8,128)(2,1)S(1)}, bf16[1,1,1,384,1024]{4,3,2,1,0:T(8,128)(2,1)}, u32[]{:S(2)}) %copy-start) | copy-done | bytes 786456
  1.8 0.0 copy-start.5
  1.8 1.3 %convolution_convert_fusion = bf16[384,128]{1,0:T(8,128)(2,1)S(1)} fusion(bf16[1,1,1,384,1024]{4,3,2,1,0:T(8,128)(2,1)S(1)} %copy-done, bf16[1,1,1,1024,128]{4,3,2,1,0:T(8,128)(2,1)} %param.11), kind=kOutput, calls=%fused_computation | convolution fusion | flops 100712448 | bytes 1146880 | tf_op jit(solution)/shard_map/dot_general | solution.py:14
  3.1 3.0 %collective-permute-start = (bf16[3,128,128]{2,1,0:T(8,128)(2,1)S(1)}, bf16[3,128,128]{2,1,0:T(8,128)(2,1)S(1)}, u32[]{:S(2)}, u32[]{:S(2)}) collective-permute-start(bf16[3,128,128]{2,1,0:T(8,128)(2,1)S(1)} %bitcast.25), channel_id=1, source_target_pairs={{0,16},{16,0},{1,17},{17,1},{2,18},{18,2},{3,19},{19,3},{4,20},{20... | collective-permute-start | bytes 294920 | tf_op jit(solution)/shard_map/ppermute | solution.py:19
  6.1 0.0 copy-done.1
  6.1 0.0 copy-done.5
  6.1 0.0 copy-start.6
  6.1 0.0 copy-start.2
  6.1 0.1 shard_map.88
  6.3 0.0 copy-start.4
  6.3 2.7 %collective-permute-start.5 = (bf16[2,128,128]{2,1,0:T(8,128)(2,1)S(1)}, bf16[2,128,128]{2,1,0:T(8,128)(2,1)S(1)}, u32[]{:S(2)}, u32[]{:S(2)}) collective-permute-start(bf16[2,128,128]{2,1,0:T(8,128)(2,1)S(1)} %shard_map.88), channel_id=1, source_target_pairs={{0,2},{1,3},{2,0},{3,1},{4,6},{5,7},{6,4},{7,5},{8,10},{9,11},{10,... | collective-permute-start | bytes 196616 | tf_op jit(solution)/shard_map/ppermute | solution.py:19
  8.9 0.0 copy-done.6
  9.0 0.0 copy-done.4
  9.0 0.0 copy-done.2
  9.0 0.3 shard_map.87
  9.2 0.0 collective-permute-done
  9.3 1.6 %collective-permute-start.7 = (bf16[2,128,128]{2,1,0:T(8,128)(2,1)S(1)}, bf16[2,128,128]{2,1,0:T(8,128)(2,1)S(1)}, u32[]{:S(2)}, u32[]{:S(2)}) collective-permute-start(bf16[2,128,128]{2,1,0:T(8,128)(2,1)S(1)} %get-tuple-element.23), channel_id=1, source_target_pairs={{0,8},{4,12},{8,0},{12,4},{1,9},{5,13},{9,1},{13,5},{2,10},{6,14},... | collective-permute-start | bytes 196616 | tf_op jit(solution)/shard_map/ppermute | solution.py:19
  10.9 0.9 %collective-permute-done.5 = bf16[2,128,128]{2,1,0:T(8,128)(2,1)S(1)} collective-permute-done((bf16[2,128,128]{2,1,0:T(8,128)(2,1)S(1)}, bf16[2,128,128]{2,1,0:T(8,128)(2,1)S(1)}, u32[]{:S(2)}, u32[]{:S(2)}) %collective-permute-start.5) | collective-permute-done | bytes 65568 | tf_op jit(solution)/shard_map/ppermute | solution.py:19
  11.8 2.4 %collective-permute-start.1 = (bf16[3,128,128]{2,1,0:T(8,128)(2,1)S(1)}, bf16[3,128,128]{2,1,0:T(8,128)(2,1)S(1)}, u32[]{:S(2)}, u32[]{:S(2)}) collective-permute-start(bf16[3,128,128]{2,1,0:T(8,128)(2,1)S(1)} %add.9), channel_id=1, source_target_pairs={{0,2},{1,3},{2,0},{3,1},{4,6},{5,7},{6,4},{7,5},{8,10},{9,11},{10,... | collective-permute-start | bytes 294920 | tf_op jit(solution)/shard_map/ppermute | solution.py:19
  14.2 2.1 %collective-permute-start.6 = (bf16[4,128,128]{2,1,0:T(8,128)(2,1)S(1)}, bf16[4,128,128]{2,1,0:T(8,128)(2,1)S(1)}, u32[]{:S(2)}, u32[]{:S(2)}) collective-permute-start(bf16[4,128,128]{2,1,0:T(8,128)(2,1)S(1)} %pad_maximum_fusion.3), channel_id=1, source_target_pairs={{0,1},{1,0},{2,3},{3,2},{4,5},{5,4},{6,7},{7,6},{8,9},{9,8},{10,11... | collective-permute-start | bytes 393224 | tf_op jit(solution)/shard_map/ppermute | solution.py:19
  16.4 0.0 collective-permute-done.7
  16.4 0.1 collective-permute-start.8
  16.5 1.1 %collective-permute-done.1 = bf16[3,128,128]{2,1,0:T(8,128)(2,1)S(1)} collective-permute-done((bf16[3,128,128]{2,1,0:T(8,128)(2,1)S(1)}, bf16[3,128,128]{2,1,0:T(8,128)(2,1)S(1)}, u32[]{:S(2)}, u32[]{:S(2)}) %collective-permute-start.1) | collective-permute-done | bytes 98336 | tf_op jit(solution)/shard_map/ppermute | solution.py:19
  17.6 1.8 %collective-permute-start.2 = (bf16[3,128,128]{2,1,0:T(8,128)(2,1)S(1)}, bf16[3,128,128]{2,1,0:T(8,128)(2,1)S(1)}, u32[]{:S(2)}, u32[]{:S(2)}) collective-permute-start(bf16[3,128,128]{2,1,0:T(8,128)(2,1)S(1)} %add.10), channel_id=1, source_target_pairs={{0,1},{1,0},{2,3},{3,2},{4,5},{5,4},{6,7},{7,6},{8,9},{9,8},{10,11... | collective-permute-start | bytes 294920 | tf_op jit(solution)/shard_map/ppermute | solution.py:19
  19.3 0.6 %collective-permute-done.6 = bf16[4,128,128]{2,1,0:T(8,128)(2,1)S(1)} collective-permute-done((bf16[4,128,128]{2,1,0:T(8,128)(2,1)S(1)}, bf16[4,128,128]{2,1,0:T(8,128)(2,1)S(1)}, u32[]{:S(2)}, u32[]{:S(2)}) %collective-permute-start.6) | collective-permute-done | bytes 131104 | tf_op jit(solution)/shard_map/ppermute | solution.py:19
  19.9 0.0 collective-permute-done.8
  20.0 0.2 shard_map.89
  20.2 2.9 %collective-permute-start.9 = (bf16[3,128,128]{2,1,0:T(8,128)(2,1)S(1)}, bf16[3,128,128]{2,1,0:T(8,128)(2,1)S(1)}, u32[]{:S(2)}, u32[]{:S(2)}) collective-permute-start(bf16[3,128,128]{2,1,0:T(8,128)(2,1)S(1)} %get-tuple-element.24), channel_id=1, source_target_pairs={{0,2},{1,3},{2,0},{3,1},{4,6},{5,7},{6,4},{7,5},{8,10},{9,11},{10,... | collective-permute-start | bytes 294920 | tf_op jit(solution)/shard_map/ppermute | solution.py:19
  23.1 0.0 collective-permute-start.10
  23.1 2.0 %collective-permute-start.11 = (bf16[3,128,128]{2,1,0:T(8,128)(2,1)S(1)}, bf16[3,128,128]{2,1,0:T(8,128)(2,1)S(1)}, u32[]{:S(2)}, u32[]{:S(2)}) collective-permute-start(bf16[3,128,128]{2,1,0:T(8,128)(2,1)S(1)} %get-tuple-element.24), channel_id=1, source_target_pairs={{0,3},{1,2},{2,1},{3,0},{4,7},{5,6},{6,5},{7,4},{8,11},{9,10},{10,... | collective-permute-start | bytes 294920 | tf_op jit(solution)/shard_map/ppermute | solution.py:19
  25.1 0.0 collective-permute-done.2
  25.2 0.2 shard_map.86
  25.3 1.6 %collective-permute-start.3 = (bf16[2,128,128]{2,1,0:T(8,128)(2,1)S(1)}, bf16[2,128,128]{2,1,0:T(8,128)(2,1)S(1)}, u32[]{:S(2)}, u32[]{:S(2)}) collective-permute-start(bf16[2,128,128]{2,1,0:T(8,128)(2,1)S(1)} %get-tuple-element.16.solved_ref), channel_id=1, source_target_pairs={{0,8},{4,12},{8,0},{12,4},{1,9},{5,13},{9,1},{13,5},{2,10},{6,14},... | collective-permute-start | bytes 196616 | tf_op jit(solution)/shard_map/ppermute | solution.py:19
  26.9 1.5 %collective-permute-start.14 = (bf16[1,128,128]{2,1,0:T(8,128)(2,1)S(1)}, bf16[1,128,128]{2,1,0:T(8,128)(2,1)S(1)}, u32[]{:S(2)}, u32[]{:S(2)}) collective-permute-start(bf16[1,128,128]{2,1,0:T(8,128)(2,1)S(1)} %get-tuple-element.26), channel_id=1, source_target_pairs={{0,2},{1,3},{2,0},{3,1},{4,6},{5,7},{6,4},{7,5},{8,10},{9,11},{10,... | collective-permute-start | bytes 98312 | tf_op jit(solution)/shard_map/ppermute | solution.py:19
  28.4 1.3 %collective-permute-done.3 = bf16[2,128,128]{2,1,0:T(8,128)(2,1)S(1)} collective-permute-done((bf16[2,128,128]{2,1,0:T(8,128)(2,1)S(1)}, bf16[2,128,128]{2,1,0:T(8,128)(2,1)S(1)}, u32[]{:S(2)}, u32[]{:S(2)}) %collective-permute-start.3) | collective-permute-done | bytes 65568 | tf_op jit(solution)/shard_map/ppermute | solution.py:19
  29.7 0.1 collective-permute-start.4
  29.8 0.0 collective-permute-done.9
  29.8 0.0 collective-permute-done.10
  29.8 0.6 %collective-permute-done.11 = bf16[3,128,128]{2,1,0:T(8,128)(2,1)S(1)} collective-permute-done((bf16[3,128,128]{2,1,0:T(8,128)(2,1)S(1)}, bf16[3,128,128]{2,1,0:T(8,128)(2,1)S(1)}, u32[]{:S(2)}, u32[]{:S(2)}) %collective-permute-start.11) | collective-permute-done | bytes 98336 | tf_op jit(solution)/shard_map/ppermute | solution.py:19
  30.5 0.6 %collective-permute-done.4 = bf16[4,128,128]{2,1,0:T(8,128)(2,1)S(1)} collective-permute-done((bf16[4,128,128]{2,1,0:T(8,128)(2,1)S(1)}, bf16[4,128,128]{2,1,0:T(8,128)(2,1)S(1)}, u32[]{:S(2)}, u32[]{:S(2)}) %collective-permute-start.4) | collective-permute-done | bytes 131104 | tf_op jit(solution)/shard_map/ppermute | solution.py:19
  31.1 0.5 %shard_map.90 = bf16[2,128,128]{2,1,0:T(8,128)(2,1)S(1)} custom-call(bf16[128,128]{1,0:T(8,128)(2,1)S(1)} %get-tuple-element.32.middle_inverse_ref.inverse_ref, bf16[128,128]{1,0:T(8,128)(2,1)S(1)} %get-tuple-element.30.last_inverse_ref, bf16[128,128]{1,0:T(8,128)(2,1)S(1)} %slice_bitcast_fusion.rhs_ref, bf16[3,128,128]{2,1,0:T(8,128)(2,1)S(1)} %add.11.total_ref.sum_ref, ...), custom_call_target="tpu_custom_call" | custom-call | tf_op jit(solution)/shard_map/pallas_call | solution.py:60
  31.7 0.0 copy-start.3
  31.7 1.6 %collective-permute-start.12 = (bf16[2,128,128]{2,1,0:T(8,128)(2,1)S(1)}, bf16[2,128,128]{2,1,0:T(8,128)(2,1)S(1)}, u32[]{:S(2)}, u32[]{:S(2)}) collective-permute-start(bf16[2,128,128]{2,1,0:T(8,128)(2,1)S(1)} %shard_map.90), channel_id=1, source_target_pairs={{0,8},{4,12},{8,0},{12,4},{1,9},{5,13},{9,1},{13,5},{2,10},{6,14},... | collective-permute-start | bytes 196616 | tf_op jit(solution)/shard_map/ppermute | solution.py:19
  33.3 0.0 collective-permute-done.14
  33.3 1.2 %collective-permute-start.15 = (bf16[2,128,128]{2,1,0:T(8,128)(2,1)S(1)}, bf16[2,128,128]{2,1,0:T(8,128)(2,1)S(1)}, u32[]{:S(2)}, u32[]{:S(2)}) collective-permute-start(bf16[2,128,128]{2,1,0:T(8,128)(2,1)S(1)} %pad_maximum_fusion.7), channel_id=1, source_target_pairs={{0,1},{1,0},{2,3},{3,2},{4,5},{5,4},{6,7},{7,6},{8,9},{9,8},{10,11... | collective-permute-start | bytes 196616 | tf_op jit(solution)/shard_map/ppermute | solution.py:19
  34.5 1.5 %collective-permute-done.12 = bf16[2,128,128]{2,1,0:T(8,128)(2,1)S(1)} collective-permute-done((bf16[2,128,128]{2,1,0:T(8,128)(2,1)S(1)}, bf16[2,128,128]{2,1,0:T(8,128)(2,1)S(1)}, u32[]{:S(2)}, u32[]{:S(2)}) %collective-permute-start.12) | collective-permute-done | bytes 65568 | tf_op jit(solution)/shard_map/ppermute | solution.py:19
  36.0 0.1 collective-permute-start.13
  36.1 1.5 %collective-permute-done.15 = bf16[2,128,128]{2,1,0:T(8,128)(2,1)S(1)} collective-permute-done((bf16[2,128,128]{2,1,0:T(8,128)(2,1)S(1)}, bf16[2,128,128]{2,1,0:T(8,128)(2,1)S(1)}, u32[]{:S(2)}, u32[]{:S(2)}) %collective-permute-start.15) | collective-permute-done | bytes 65568 | tf_op jit(solution)/shard_map/ppermute | solution.py:19
  37.6 0.0 collective-permute-done.13
  37.7 0.0 copy-done.3
  37.7 1.4 %shard_map.91 = (bf16[3,128,128]{2,1,0:T(8,128)(2,1)}, bf16[1024,128]{1,0:T(8,128)(2,1)}) custom-call(bf16[2,128,128]{2,1,0:T(8,128)(2,1)S(1)} %get-tuple-element.16.solved_ref, bf16[1024,384]{1,0:T(8,128)(2,1)S(1)} %bitcast.23, bf16[1024,128]{1,0:T(8,128)(2,1)S(1)} %get-tuple-element.18.sub_ref, bf16[8,128,128]{2,1,0:T(8,128)(2,1)S(1)} %pad_maximum_fusion.1.ends_ref, ...), custom_call_target="tpu_custom_call" | custom-call | tf_op jit(solution)/shard_map/pallas_call | solution.py:60
  (22 shorter events, 0.4 us)
Async XLA Ops:
  0.6 1.1 %copy-start = (bf16[1,1,1,384,1024]{4,3,2,1,0:T(8,128)(2,1)S(1)}, bf16[1,1,1,384,1024]{4,3,2,1,0:T(8,128)(2,1)}, u32[]{:S(2)}) copy-start(bf16[1,1,1,384,1024]{4,3,2,1,0:T(8,128)(2,1)} %param.12) | copy-start | bytes 2359300
  0.6 5.5 %copy-start.1 = (bf16[1,3,3,1,128,128]{5,4,3,2,1,0:T(8,128)(2,1)S(1)}, bf16[1,3,3,1,128,128]{5,4,3,2,1,0:T(8,128)(2,1)}, u32[]{:S(2)}) copy-start(bf16[1,3,3,1,128,128]{5,4,3,2,1,0:T(8,128)(2,1)} %param.9) | copy-start | bytes 884740
  1.8 4.3 %copy-start.5 = (s32[12,12]{1,0:T(8,128)S(1)}, s32[12,12]{1,0:T(8,128)}, u32[]{:S(2)}) copy-start(s32[12,12]{1,0:T(8,128)} %pattern_ref.3) | copy-start | bytes 1732
  3.1 6.1 %collective-permute-start = (bf16[3,128,128]{2,1,0:T(8,128)(2,1)S(1)}, bf16[3,128,128]{2,1,0:T(8,128)(2,1)S(1)}, u32[]{:S(2)}, u32[]{:S(2)}) collective-permute-start(bf16[3,128,128]{2,1,0:T(8,128)(2,1)S(1)} %bitcast.25), channel_id=1, source_target_pairs={{0,16},{16,0},{1,17},{17,1},{2,18},{18,2},{3,19},{19,3},{4,20},{20... | collective-permute-start | bytes 294920 | tf_op jit(solution)/shard_map/ppermute | solution.py:19
  6.1 2.8 %copy-start.6 = (bf16[1,3,128,128]{3,2,1,0:T(8,128)(2,1)S(1)}, bf16[1,3,128,128]{3,2,1,0:T(8,128)(2,1)}, u32[]{:S(2)}) copy-start(bf16[1,3,128,128]{3,2,1,0:T(8,128)(2,1)} %param.8) | copy-start | bytes 294916
  6.1 2.9 %copy-start.2 = (bf16[1,1,1,1024,128]{4,3,2,1,0:T(8,128)(2,1)S(1)}, bf16[1,1,1,1024,128]{4,3,2,1,0:T(8,128)(2,1)}, u32[]{:S(2)}) copy-start(bf16[1,1,1,1024,128]{4,3,2,1,0:T(8,128)(2,1)} %param.11) | copy-start | bytes 786436
  6.3 2.7 %copy-start.4 = (bf16[1,3,128,128]{3,2,1,0:T(8,128)(2,1)S(1)}, bf16[1,3,128,128]{3,2,1,0:T(8,128)(2,1)}, u32[]{:S(2)}) copy-start(bf16[1,3,128,128]{3,2,1,0:T(8,128)(2,1)} %param.7) | copy-start | bytes 294916
  6.3 5.5 %collective-permute-start.5 = (bf16[2,128,128]{2,1,0:T(8,128)(2,1)S(1)}, bf16[2,128,128]{2,1,0:T(8,128)(2,1)S(1)}, u32[]{:S(2)}, u32[]{:S(2)}) collective-permute-start(bf16[2,128,128]{2,1,0:T(8,128)(2,1)S(1)} %shard_map.88), channel_id=1, source_target_pairs={{0,2},{1,3},{2,0},{3,1},{4,6},{5,7},{6,4},{7,5},{8,10},{9,11},{10,... | collective-permute-start | bytes 196616 | tf_op jit(solution)/shard_map/ppermute | solution.py:19
  9.3 7.1 %collective-permute-start.7 = (bf16[2,128,128]{2,1,0:T(8,128)(2,1)S(1)}, bf16[2,128,128]{2,1,0:T(8,128)(2,1)S(1)}, u32[]{:S(2)}, u32[]{:S(2)}) collective-permute-start(bf16[2,128,128]{2,1,0:T(8,128)(2,1)S(1)} %get-tuple-element.23), channel_id=1, source_target_pairs={{0,8},{4,12},{8,0},{12,4},{1,9},{5,13},{9,1},{13,5},{2,10},{6,14},... | collective-permute-start | bytes 196616 | tf_op jit(solution)/shard_map/ppermute | solution.py:19
  11.8 5.7 %collective-permute-start.1 = (bf16[3,128,128]{2,1,0:T(8,128)(2,1)S(1)}, bf16[3,128,128]{2,1,0:T(8,128)(2,1)S(1)}, u32[]{:S(2)}, u32[]{:S(2)}) collective-permute-start(bf16[3,128,128]{2,1,0:T(8,128)(2,1)S(1)} %add.9), channel_id=1, source_target_pairs={{0,2},{1,3},{2,0},{3,1},{4,6},{5,7},{6,4},{7,5},{8,10},{9,11},{10,... | collective-permute-start | bytes 294920 | tf_op jit(solution)/shard_map/ppermute | solution.py:19
  14.2 5.6 %collective-permute-start.6 = (bf16[4,128,128]{2,1,0:T(8,128)(2,1)S(1)}, bf16[4,128,128]{2,1,0:T(8,128)(2,1)S(1)}, u32[]{:S(2)}, u32[]{:S(2)}) collective-permute-start(bf16[4,128,128]{2,1,0:T(8,128)(2,1)S(1)} %pad_maximum_fusion.3), channel_id=1, source_target_pairs={{0,1},{1,0},{2,3},{3,2},{4,5},{5,4},{6,7},{7,6},{8,9},{9,8},{10,11... | collective-permute-start | bytes 393224 | tf_op jit(solution)/shard_map/ppermute | solution.py:19
  16.4 3.5 %collective-permute-start.8 = (bf16[4,128,128]{2,1,0:T(8,128)(2,1)S(1)}, bf16[4,128,128]{2,1,0:T(8,128)(2,1)S(1)}, u32[]{:S(2)}, u32[]{:S(2)}) collective-permute-start(bf16[4,128,128]{2,1,0:T(8,128)(2,1)S(1)} %pad_maximum_fusion.4), channel_id=1, source_target_pairs={{0,4},{4,0},{8,12},{12,8},{1,5},{5,1},{9,13},{13,9},{2,6},{6,2},{1... | collective-permute-start | bytes 393224 | tf_op jit(solution)/shard_map/ppermute | solution.py:19
  17.6 7.6 %collective-permute-start.2 = (bf16[3,128,128]{2,1,0:T(8,128)(2,1)S(1)}, bf16[3,128,128]{2,1,0:T(8,128)(2,1)S(1)}, u32[]{:S(2)}, u32[]{:S(2)}) collective-permute-start(bf16[3,128,128]{2,1,0:T(8,128)(2,1)S(1)} %add.10), channel_id=1, source_target_pairs={{0,1},{1,0},{2,3},{3,2},{4,5},{5,4},{6,7},{7,6},{8,9},{9,8},{10,11... | collective-permute-start | bytes 294920 | tf_op jit(solution)/shard_map/ppermute | solution.py:19
  20.2 9.6 %collective-permute-start.9 = (bf16[3,128,128]{2,1,0:T(8,128)(2,1)S(1)}, bf16[3,128,128]{2,1,0:T(8,128)(2,1)S(1)}, u32[]{:S(2)}, u32[]{:S(2)}) collective-permute-start(bf16[3,128,128]{2,1,0:T(8,128)(2,1)S(1)} %get-tuple-element.24), channel_id=1, source_target_pairs={{0,2},{1,3},{2,0},{3,1},{4,6},{5,7},{6,4},{7,5},{8,10},{9,11},{10,... | collective-permute-start | bytes 294920 | tf_op jit(solution)/shard_map/ppermute | solution.py:19
  23.1 6.7 %collective-permute-start.10 = (bf16[3,128,128]{2,1,0:T(8,128)(2,1)S(1)}, bf16[3,128,128]{2,1,0:T(8,128)(2,1)S(1)}, u32[]{:S(2)}, u32[]{:S(2)}) collective-permute-start(bf16[3,128,128]{2,1,0:T(8,128)(2,1)S(1)} %get-tuple-element.24), channel_id=1, source_target_pairs={{0,1},{1,0},{2,3},{3,2},{4,5},{5,4},{6,7},{7,6},{8,9},{9,8},{10,11... | collective-permute-start | bytes 294920 | tf_op jit(solution)/shard_map/ppermute | solution.py:19
  23.1 7.4 %collective-permute-start.11 = (bf16[3,128,128]{2,1,0:T(8,128)(2,1)S(1)}, bf16[3,128,128]{2,1,0:T(8,128)(2,1)S(1)}, u32[]{:S(2)}, u32[]{:S(2)}) collective-permute-start(bf16[3,128,128]{2,1,0:T(8,128)(2,1)S(1)} %get-tuple-element.24), channel_id=1, source_target_pairs={{0,3},{1,2},{2,1},{3,0},{4,7},{5,6},{6,5},{7,4},{8,11},{9,10},{10,... | collective-permute-start | bytes 294920 | tf_op jit(solution)/shard_map/ppermute | solution.py:19
  25.3 4.3 %collective-permute-start.3 = (bf16[2,128,128]{2,1,0:T(8,128)(2,1)S(1)}, bf16[2,128,128]{2,1,0:T(8,128)(2,1)S(1)}, u32[]{:S(2)}, u32[]{:S(2)}) collective-permute-start(bf16[2,128,128]{2,1,0:T(8,128)(2,1)S(1)} %get-tuple-element.16.solved_ref), channel_id=1, source_target_pairs={{0,8},{4,12},{8,0},{12,4},{1,9},{5,13},{9,1},{13,5},{2,10},{6,14},... | collective-permute-start | bytes 196616 | tf_op jit(solution)/shard_map/ppermute | solution.py:19
  26.9 6.3 %collective-permute-start.14 = (bf16[1,128,128]{2,1,0:T(8,128)(2,1)S(1)}, bf16[1,128,128]{2,1,0:T(8,128)(2,1)S(1)}, u32[]{:S(2)}, u32[]{:S(2)}) collective-permute-start(bf16[1,128,128]{2,1,0:T(8,128)(2,1)S(1)} %get-tuple-element.26), channel_id=1, source_target_pairs={{0,2},{1,3},{2,0},{3,1},{4,6},{5,7},{6,4},{7,5},{8,10},{9,11},{10,... | collective-permute-start | bytes 98312 | tf_op jit(solution)/shard_map/ppermute | solution.py:19
  29.7 1.4 %collective-permute-start.4 = (bf16[4,128,128]{2,1,0:T(8,128)(2,1)S(1)}, bf16[4,128,128]{2,1,0:T(8,128)(2,1)S(1)}, u32[]{:S(2)}, u32[]{:S(2)}) collective-permute-start(bf16[4,128,128]{2,1,0:T(8,128)(2,1)S(1)} %pad_maximum_fusion.2), channel_id=1, source_target_pairs={{0,4},{4,0},{8,12},{12,8},{1,5},{5,1},{9,13},{13,9},{2,6},{6,2},{1... | collective-permute-start | bytes 393224 | tf_op jit(solution)/shard_map/ppermute | solution.py:19
  31.7 6.0 %copy-start.3 = (bf16[1,1,1,1024,384]{4,3,2,1,0:T(8,128)(2,1)S(1)}, bf16[1,1,1,1024,384]{4,3,2,1,0:T(8,128)(2,1)}, u32[]{:S(2)}) copy-start(bf16[1,1,1,1024,384]{4,3,2,1,0:T(8,128)(2,1)} %param.13) | copy-start | bytes 2359300
  31.7 4.3 %collective-permute-start.12 = (bf16[2,128,128]{2,1,0:T(8,128)(2,1)S(1)}, bf16[2,128,128]{2,1,0:T(8,128)(2,1)S(1)}, u32[]{:S(2)}, u32[]{:S(2)}) collective-permute-start(bf16[2,128,128]{2,1,0:T(8,128)(2,1)S(1)} %shard_map.90), channel_id=1, source_target_pairs={{0,8},{4,12},{8,0},{12,4},{1,9},{5,13},{9,1},{13,5},{2,10},{6,14},... | collective-permute-start | bytes 196616 | tf_op jit(solution)/shard_map/ppermute | solution.py:19
  33.3 4.3 %collective-permute-start.15 = (bf16[2,128,128]{2,1,0:T(8,128)(2,1)S(1)}, bf16[2,128,128]{2,1,0:T(8,128)(2,1)S(1)}, u32[]{:S(2)}, u32[]{:S(2)}) collective-permute-start(bf16[2,128,128]{2,1,0:T(8,128)(2,1)S(1)} %pad_maximum_fusion.7), channel_id=1, source_target_pairs={{0,1},{1,0},{2,3},{3,2},{4,5},{5,4},{6,7},{7,6},{8,9},{9,8},{10,11... | collective-permute-start | bytes 196616 | tf_op jit(solution)/shard_map/ppermute | solution.py:19
  36.0 1.6 %collective-permute-start.13 = (bf16[4,128,128]{2,1,0:T(8,128)(2,1)S(1)}, bf16[4,128,128]{2,1,0:T(8,128)(2,1)S(1)}, u32[]{:S(2)}, u32[]{:S(2)}) collective-permute-start(bf16[4,128,128]{2,1,0:T(8,128)(2,1)S(1)} %pad_maximum_fusion.5), channel_id=1, source_target_pairs={{0,4},{4,0},{8,12},{12,8},{1,5},{5,1},{9,13},{13,9},{2,6},{6,2},{1... | collective-permute-start | bytes 393224 | tf_op jit(solution)/shard_map/ppermute | solution.py:19

commit v7 on v6

--- a/solution.py
+++ b/solution.py
@@ -82,7 +82,7 @@
     row_order, col_order = offsets("pr"), offsets("pc")
 
 
-    part = dot(low, sub).astype(bf16).reshape(levels, width, count)
+    part = dot(after(low, sub), sub).astype(bf16).reshape(levels, width, count)
 
     def masked(pattern_ref, block, level, b):
         i, j = level * rows + lax.axis_index("pr"), b * cols + lax.axis_index("pc")

time: 39.2 us -> 39.2 us (level)
  no operation moved by 1% of the time
where the time goes in v7:
time: 39.2 us; the launch traced here: 39.1 us
  starting transfers between devices  24.5 us (62%)
  waiting for transfers between devices  8.11 us (21%)
  Pallas kernels  2.68 us (7%)
  matrix products  1.36 us (3%)
  local copies, waits for them, and re-layouts  1.29 us (3%)
  between operations  0.9 us (2%)
    ppermute x16, starting transfers between devices, hop(): return lax.ppermute(x, axis, [(i, i ^ offset) for i in range(size)])  24.5 us
    ppermute x16, waiting for transfers between devices, hop(): return lax.ppermute(x, axis, [(i, i ^ offset) for i in range(size)])  8.11 us
    pallas_call x6, Pallas kernels, call(): pl.pallas_call(kernel, out_shape=outs, in_specs=in_specs or [VMEM] * len(...  2.68 us
    dot_general x1, matrix products, dot(): return jnp.dot(a, b, preferred_element_type=jnp.float32)  1.36 us
    unnamed x20, local copies, waits for them, and re-layouts  1.23 us
  transfers between devices with their start and end apart: 16, of which 8 were waited for; matrix products, arithmetic and copies ran while one was open for 1% of the time, Pallas kernels for 3%

profile of v7, /device:TPU:0, one launch (start us, length us, event | category | flops | bytes accessed | tf_op | source)
XLA Modules:
  0.0 39.1 jit_solution(9828915297720689204)
XLA Ops:
  0.6 0.0 copy-start
  0.6 1.1 %copy-done = bf16[1,1,1,384,1024]{4,3,2,1,0:T(8,128)(2,1)S(1)} copy-done((bf16[1,1,1,384,1024]{4,3,2,1,0:T(8,128)(2,1)S(1)}, bf16[1,1,1,384,1024]{4,3,2,1,0:T(8,128)(2,1)}, u32[]{:S(2)}) %copy-start) | copy-done | bytes 786456
  1.8 0.0 copy-start.1
  1.8 0.0 copy-start.5
  1.8 1.4 %convolution_convert_fusion = bf16[384,128]{1,0:T(8,128)(2,1)S(1)} fusion(bf16[384,1024]{1,0:T(8,128)(2,1)S(1)} %bitcast.19, bf16[1,1,1,1024,128]{4,3,2,1,0:T(8,128)(2,1)} %param.11), kind=kOutput, calls=%fused_computation | convolution fusion | flops 100712448 | bytes 1146880 | tf_op jit(solution)/shard_map/dot_general | solution.py:14
  3.1 3.0 %collective-permute-start = (bf16[3,128,128]{2,1,0:T(8,128)(2,1)S(1)}, bf16[3,128,128]{2,1,0:T(8,128)(2,1)S(1)}, u32[]{:S(2)}, u32[]{:S(2)}) collective-permute-start(bf16[3,128,128]{2,1,0:T(8,128)(2,1)S(1)} %bitcast.25), channel_id=1, source_target_pairs={{0,16},{16,0},{1,17},{17,1},{2,18},{18,2},{3,19},{19,3},{4,20},{20... | collective-permute-start | bytes 294920 | tf_op jit(solution)/shard_map/ppermute | solution.py:19
  6.1 0.0 copy-done.1
  6.1 0.0 copy-done.5
  6.1 0.0 copy-start.6
  6.2 0.0 copy-start.2
  6.2 0.1 shard_map.88
  6.3 0.0 copy-start.4
  6.3 2.7 %collective-permute-start.5 = (bf16[2,128,128]{2,1,0:T(8,128)(2,1)S(1)}, bf16[2,128,128]{2,1,0:T(8,128)(2,1)S(1)}, u32[]{:S(2)}, u32[]{:S(2)}) collective-permute-start(bf16[2,128,128]{2,1,0:T(8,128)(2,1)S(1)} %shard_map.88), channel_id=1, source_target_pairs={{0,2},{1,3},{2,0},{3,1},{4,6},{5,7},{6,4},{7,5},{8,10},{9,11},{10,... | collective-permute-start | bytes 196616 | tf_op jit(solution)/shard_map/ppermute | solution.py:19
  9.0 0.0 copy-done.6
  9.0 0.0 copy-done.4
  9.0 0.0 copy-done.2
  9.0 0.3 shard_map.87
  9.3 0.0 collective-permute-done
  9.3 1.6 %collective-permute-start.7 = (bf16[2,128,128]{2,1,0:T(8,128)(2,1)S(1)}, bf16[2,128,128]{2,1,0:T(8,128)(2,1)S(1)}, u32[]{:S(2)}, u32[]{:S(2)}) collective-permute-start(bf16[2,128,128]{2,1,0:T(8,128)(2,1)S(1)} %get-tuple-element.25), channel_id=1, source_target_pairs={{0,8},{4,12},{8,0},{12,4},{1,9},{5,13},{9,1},{13,5},{2,10},{6,14},... | collective-permute-start | bytes 196616 | tf_op jit(solution)/shard_map/ppermute | solution.py:19
  10.9 0.9 %collective-permute-done.5 = bf16[2,128,128]{2,1,0:T(8,128)(2,1)S(1)} collective-permute-done((bf16[2,128,128]{2,1,0:T(8,128)(2,1)S(1)}, bf16[2,128,128]{2,1,0:T(8,128)(2,1)S(1)}, u32[]{:S(2)}, u32[]{:S(2)}) %collective-permute-start.5) | collective-permute-done | bytes 65568 | tf_op jit(solution)/shard_map/ppermute | solution.py:19
  11.9 2.4 %collective-permute-start.1 = (bf16[3,128,128]{2,1,0:T(8,128)(2,1)S(1)}, bf16[3,128,128]{2,1,0:T(8,128)(2,1)S(1)}, u32[]{:S(2)}, u32[]{:S(2)}) collective-permute-start(bf16[3,128,128]{2,1,0:T(8,128)(2,1)S(1)} %add.9), channel_id=1, source_target_pairs={{0,2},{1,3},{2,0},{3,1},{4,6},{5,7},{6,4},{7,5},{8,10},{9,11},{10,... | collective-permute-start | bytes 294920 | tf_op jit(solution)/shard_map/ppermute | solution.py:19
  14.3 2.1 %collective-permute-start.6 = (bf16[4,128,128]{2,1,0:T(8,128)(2,1)S(1)}, bf16[4,128,128]{2,1,0:T(8,128)(2,1)S(1)}, u32[]{:S(2)}, u32[]{:S(2)}) collective-permute-start(bf16[4,128,128]{2,1,0:T(8,128)(2,1)S(1)} %pad_maximum_fusion.3), channel_id=1, source_target_pairs={{0,1},{1,0},{2,3},{3,2},{4,5},{5,4},{6,7},{7,6},{8,9},{9,8},{10,11... | collective-permute-start | bytes 393224 | tf_op jit(solution)/shard_map/ppermute | solution.py:19
  16.4 0.0 collective-permute-done.7
  16.4 0.1 collective-permute-start.8
  16.5 1.1 %collective-permute-done.1 = bf16[3,128,128]{2,1,0:T(8,128)(2,1)S(1)} collective-permute-done((bf16[3,128,128]{2,1,0:T(8,128)(2,1)S(1)}, bf16[3,128,128]{2,1,0:T(8,128)(2,1)S(1)}, u32[]{:S(2)}, u32[]{:S(2)}) %collective-permute-start.1) | collective-permute-done | bytes 98336 | tf_op jit(solution)/shard_map/ppermute | solution.py:19
  17.6 1.8 %collective-permute-start.2 = (bf16[3,128,128]{2,1,0:T(8,128)(2,1)S(1)}, bf16[3,128,128]{2,1,0:T(8,128)(2,1)S(1)}, u32[]{:S(2)}, u32[]{:S(2)}) collective-permute-start(bf16[3,128,128]{2,1,0:T(8,128)(2,1)S(1)} %add.10), channel_id=1, source_target_pairs={{0,1},{1,0},{2,3},{3,2},{4,5},{5,4},{6,7},{7,6},{8,9},{9,8},{10,11... | collective-permute-start | bytes 294920 | tf_op jit(solution)/shard_map/ppermute | solution.py:19
  19.4 0.6 %collective-permute-done.6 = bf16[4,128,128]{2,1,0:T(8,128)(2,1)S(1)} collective-permute-done((bf16[4,128,128]{2,1,0:T(8,128)(2,1)S(1)}, bf16[4,128,128]{2,1,0:T(8,128)(2,1)S(1)}, u32[]{:S(2)}, u32[]{:S(2)}) %collective-permute-start.6) | collective-permute-done | bytes 131104 | tf_op jit(solution)/shard_map/ppermute | solution.py:19
  19.9 0.0 collective-permute-done.8
  20.0 0.2 shard_map.89
  20.2 2.9 %collective-permute-start.9 = (bf16[3,128,128]{2,1,0:T(8,128)(2,1)S(1)}, bf16[3,128,128]{2,1,0:T(8,128)(2,1)S(1)}, u32[]{:S(2)}, u32[]{:S(2)}) collective-permute-start(bf16[3,128,128]{2,1,0:T(8,128)(2,1)S(1)} %get-tuple-element.26), channel_id=1, source_target_pairs={{0,2},{1,3},{2,0},{3,1},{4,6},{5,7},{6,4},{7,5},{8,10},{9,11},{10,... | collective-permute-start | bytes 294920 | tf_op jit(solution)/shard_map/ppermute | solution.py:19
  23.1 0.0 collective-permute-start.10
  23.1 2.0 %collective-permute-start.11 = (bf16[3,128,128]{2,1,0:T(8,128)(2,1)S(1)}, bf16[3,128,128]{2,1,0:T(8,128)(2,1)S(1)}, u32[]{:S(2)}, u32[]{:S(2)}) collective-permute-start(bf16[3,128,128]{2,1,0:T(8,128)(2,1)S(1)} %get-tuple-element.26), channel_id=1, source_target_pairs={{0,3},{1,2},{2,1},{3,0},{4,7},{5,6},{6,5},{7,4},{8,11},{9,10},{10,... | collective-permute-start | bytes 294920 | tf_op jit(solution)/shard_map/ppermute | solution.py:19
  25.2 0.0 collective-permute-done.2
  25.2 0.2 shard_map.86
  25.4 1.6 %collective-permute-start.3 = (bf16[2,128,128]{2,1,0:T(8,128)(2,1)S(1)}, bf16[2,128,128]{2,1,0:T(8,128)(2,1)S(1)}, u32[]{:S(2)}, u32[]{:S(2)}) collective-permute-start(bf16[2,128,128]{2,1,0:T(8,128)(2,1)S(1)} %get-tuple-element.18.solved_ref), channel_id=1, source_target_pairs={{0,8},{4,12},{8,0},{12,4},{1,9},{5,13},{9,1},{13,5},{2,10},{6,14},... | collective-permute-start | bytes 196616 | tf_op jit(solution)/shard_map/ppermute | solution.py:19
  26.9 1.5 %collective-permute-start.14 = (bf16[1,128,128]{2,1,0:T(8,128)(2,1)S(1)}, bf16[1,128,128]{2,1,0:T(8,128)(2,1)S(1)}, u32[]{:S(2)}, u32[]{:S(2)}) collective-permute-start(bf16[1,128,128]{2,1,0:T(8,128)(2,1)S(1)} %get-tuple-element.28), channel_id=1, source_target_pairs={{0,2},{1,3},{2,0},{3,1},{4,6},{5,7},{6,4},{7,5},{8,10},{9,11},{10,... | collective-permute-start | bytes 98312 | tf_op jit(solution)/shard_map/ppermute | solution.py:19
  28.4 1.3 %collective-permute-done.3 = bf16[2,128,128]{2,1,0:T(8,128)(2,1)S(1)} collective-permute-done((bf16[2,128,128]{2,1,0:T(8,128)(2,1)S(1)}, bf16[2,128,128]{2,1,0:T(8,128)(2,1)S(1)}, u32[]{:S(2)}, u32[]{:S(2)}) %collective-permute-start.3) | collective-permute-done | bytes 65568 | tf_op jit(solution)/shard_map/ppermute | solution.py:19
  29.7 0.1 collective-permute-start.4
  29.8 0.0 collective-permute-done.9
  29.8 0.0 collective-permute-done.10
  29.9 0.6 %collective-permute-done.11 = bf16[3,128,128]{2,1,0:T(8,128)(2,1)S(1)} collective-permute-done((bf16[3,128,128]{2,1,0:T(8,128)(2,1)S(1)}, bf16[3,128,128]{2,1,0:T(8,128)(2,1)S(1)}, u32[]{:S(2)}, u32[]{:S(2)}) %collective-permute-start.11) | collective-permute-done | bytes 98336 | tf_op jit(solution)/shard_map/ppermute | solution.py:19
  30.5 0.6 %collective-permute-done.4 = bf16[4,128,128]{2,1,0:T(8,128)(2,1)S(1)} collective-permute-done((bf16[4,128,128]{2,1,0:T(8,128)(2,1)S(1)}, bf16[4,128,128]{2,1,0:T(8,128)(2,1)S(1)}, u32[]{:S(2)}, u32[]{:S(2)}) %collective-permute-start.4) | collective-permute-done | bytes 131104 | tf_op jit(solution)/shard_map/ppermute | solution.py:19
  31.1 0.5 %shard_map.90 = bf16[2,128,128]{2,1,0:T(8,128)(2,1)S(1)} custom-call(bf16[128,128]{1,0:T(8,128)(2,1)S(1)} %get-tuple-element.34.middle_inverse_ref.inverse_ref, bf16[128,128]{1,0:T(8,128)(2,1)S(1)} %get-tuple-element.32.last_inverse_ref, bf16[128,128]{1,0:T(8,128)(2,1)S(1)} %slice_bitcast_fusion.rhs_ref, bf16[3,128,128]{2,1,0:T(8,128)(2,1)S(1)} %add.11.total_ref.sum_ref, ...), custom_call_target="tpu_custom_call" | custom-call | tf_op jit(solution)/shard_map/pallas_call | solution.py:60
  31.7 0.0 copy-start.3
  31.7 1.6 %collective-permute-start.12 = (bf16[2,128,128]{2,1,0:T(8,128)(2,1)S(1)}, bf16[2,128,128]{2,1,0:T(8,128)(2,1)S(1)}, u32[]{:S(2)}, u32[]{:S(2)}) collective-permute-start(bf16[2,128,128]{2,1,0:T(8,128)(2,1)S(1)} %shard_map.90), channel_id=1, source_target_pairs={{0,8},{4,12},{8,0},{12,4},{1,9},{5,13},{9,1},{13,5},{2,10},{6,14},... | collective-permute-start | bytes 196616 | tf_op jit(solution)/shard_map/ppermute | solution.py:19
  33.3 0.0 collective-permute-done.14
  33.3 1.2 %collective-permute-start.15 = (bf16[2,128,128]{2,1,0:T(8,128)(2,1)S(1)}, bf16[2,128,128]{2,1,0:T(8,128)(2,1)S(1)}, u32[]{:S(2)}, u32[]{:S(2)}) collective-permute-start(bf16[2,128,128]{2,1,0:T(8,128)(2,1)S(1)} %pad_maximum_fusion.7), channel_id=1, source_target_pairs={{0,1},{1,0},{2,3},{3,2},{4,5},{5,4},{6,7},{7,6},{8,9},{9,8},{10,11... | collective-permute-start | bytes 196616 | tf_op jit(solution)/shard_map/ppermute | solution.py:19
  34.5 1.5 %collective-permute-done.12 = bf16[2,128,128]{2,1,0:T(8,128)(2,1)S(1)} collective-permute-done((bf16[2,128,128]{2,1,0:T(8,128)(2,1)S(1)}, bf16[2,128,128]{2,1,0:T(8,128)(2,1)S(1)}, u32[]{:S(2)}, u32[]{:S(2)}) %collective-permute-start.12) | collective-permute-done | bytes 65568 | tf_op jit(solution)/shard_map/ppermute | solution.py:19
  36.0 0.1 collective-permute-start.13
  36.1 1.5 %collective-permute-done.15 = bf16[2,128,128]{2,1,0:T(8,128)(2,1)S(1)} collective-permute-done((bf16[2,128,128]{2,1,0:T(8,128)(2,1)S(1)}, bf16[2,128,128]{2,1,0:T(8,128)(2,1)S(1)}, u32[]{:S(2)}, u32[]{:S(2)}) %collective-permute-start.15) | collective-permute-done | bytes 65568 | tf_op jit(solution)/shard_map/ppermute | solution.py:19
  37.6 0.0 collective-permute-done.13
  37.7 0.0 copy-done.3
  37.7 1.4 %shard_map.91 = (bf16[3,128,128]{2,1,0:T(8,128)(2,1)}, bf16[1024,128]{1,0:T(8,128)(2,1)}) custom-call(bf16[2,128,128]{2,1,0:T(8,128)(2,1)S(1)} %get-tuple-element.18.solved_ref, bf16[1024,384]{1,0:T(8,128)(2,1)S(1)} %bitcast.23, bf16[1024,128]{1,0:T(8,128)(2,1)S(1)} %get-tuple-element.20.sub_ref, bf16[8,128,128]{2,1,0:T(8,128)(2,1)S(1)} %pad_maximum_fusion.1.ends_ref, ...), custom_call_target="tpu_custom_call" | custom-call | tf_op jit(solution)/shard_map/pallas_call | solution.py:60
  (22 shorter events, 0.4 us)
Async XLA Ops:
  0.6 1.1 %copy-start = (bf16[1,1,1,384,1024]{4,3,2,1,0:T(8,128)(2,1)S(1)}, bf16[1,1,1,384,1024]{4,3,2,1,0:T(8,128)(2,1)}, u32[]{:S(2)}) copy-start(bf16[1,1,1,384,1024]{4,3,2,1,0:T(8,128)(2,1)} %param.12) | copy-start | bytes 2359300
  1.8 4.4 %copy-start.1 = (bf16[1,3,3,1,128,128]{5,4,3,2,1,0:T(8,128)(2,1)S(1)}, bf16[1,3,3,1,128,128]{5,4,3,2,1,0:T(8,128)(2,1)}, u32[]{:S(2)}) copy-start(bf16[1,3,3,1,128,128]{5,4,3,2,1,0:T(8,128)(2,1)} %param.9) | copy-start | bytes 884740
  1.8 4.4 %copy-start.5 = (s32[12,12]{1,0:T(8,128)S(1)}, s32[12,12]{1,0:T(8,128)}, u32[]{:S(2)}) copy-start(s32[12,12]{1,0:T(8,128)} %pattern_ref.3) | copy-start | bytes 1732
  3.1 6.1 %collective-permute-start = (bf16[3,128,128]{2,1,0:T(8,128)(2,1)S(1)}, bf16[3,128,128]{2,1,0:T(8,128)(2,1)S(1)}, u32[]{:S(2)}, u32[]{:S(2)}) collective-permute-start(bf16[3,128,128]{2,1,0:T(8,128)(2,1)S(1)} %bitcast.25), channel_id=1, source_target_pairs={{0,16},{16,0},{1,17},{17,1},{2,18},{18,2},{3,19},{19,3},{4,20},{20... | collective-permute-start | bytes 294920 | tf_op jit(solution)/shard_map/ppermute | solution.py:19
  6.1 2.8 %copy-start.6 = (bf16[1,3,128,128]{3,2,1,0:T(8,128)(2,1)S(1)}, bf16[1,3,128,128]{3,2,1,0:T(8,128)(2,1)}, u32[]{:S(2)}) copy-start(bf16[1,3,128,128]{3,2,1,0:T(8,128)(2,1)} %param.8) | copy-start | bytes 294916
  6.2 2.9 %copy-start.2 = (bf16[1,1,1,1024,128]{4,3,2,1,0:T(8,128)(2,1)S(1)}, bf16[1,1,1,1024,128]{4,3,2,1,0:T(8,128)(2,1)}, u32[]{:S(2)}) copy-start(bf16[1,1,1,1024,128]{4,3,2,1,0:T(8,128)(2,1)} %param.11) | copy-start | bytes 786436
  6.3 2.7 %copy-start.4 = (bf16[1,3,128,128]{3,2,1,0:T(8,128)(2,1)S(1)}, bf16[1,3,128,128]{3,2,1,0:T(8,128)(2,1)}, u32[]{:S(2)}) copy-start(bf16[1,3,128,128]{3,2,1,0:T(8,128)(2,1)} %param.7) | copy-start | bytes 294916
  6.3 5.5 %collective-permute-start.5 = (bf16[2,128,128]{2,1,0:T(8,128)(2,1)S(1)}, bf16[2,128,128]{2,1,0:T(8,128)(2,1)S(1)}, u32[]{:S(2)}, u32[]{:S(2)}) collective-permute-start(bf16[2,128,128]{2,1,0:T(8,128)(2,1)S(1)} %shard_map.88), channel_id=1, source_target_pairs={{0,2},{1,3},{2,0},{3,1},{4,6},{5,7},{6,4},{7,5},{8,10},{9,11},{10,... | collective-permute-start | bytes 196616 | tf_op jit(solution)/shard_map/ppermute | solution.py:19
  9.3 7.1 %collective-permute-start.7 = (bf16[2,128,128]{2,1,0:T(8,128)(2,1)S(1)}, bf16[2,128,128]{2,1,0:T(8,128)(2,1)S(1)}, u32[]{:S(2)}, u32[]{:S(2)}) collective-permute-start(bf16[2,128,128]{2,1,0:T(8,128)(2,1)S(1)} %get-tuple-element.25), channel_id=1, source_target_pairs={{0,8},{4,12},{8,0},{12,4},{1,9},{5,13},{9,1},{13,5},{2,10},{6,14},... | collective-permute-start | bytes 196616 | tf_op jit(solution)/shard_map/ppermute | solution.py:19
  11.9 5.7 %collective-permute-start.1 = (bf16[3,128,128]{2,1,0:T(8,128)(2,1)S(1)}, bf16[3,128,128]{2,1,0:T(8,128)(2,1)S(1)}, u32[]{:S(2)}, u32[]{:S(2)}) collective-permute-start(bf16[3,128,128]{2,1,0:T(8,128)(2,1)S(1)} %add.9), channel_id=1, source_target_pairs={{0,2},{1,3},{2,0},{3,1},{4,6},{5,7},{6,4},{7,5},{8,10},{9,11},{10,... | collective-permute-start | bytes 294920 | tf_op jit(solution)/shard_map/ppermute | solution.py:19
  14.3 5.6 %collective-permute-start.6 = (bf16[4,128,128]{2,1,0:T(8,128)(2,1)S(1)}, bf16[4,128,128]{2,1,0:T(8,128)(2,1)S(1)}, u32[]{:S(2)}, u32[]{:S(2)}) collective-permute-start(bf16[4,128,128]{2,1,0:T(8,128)(2,1)S(1)} %pad_maximum_fusion.3), channel_id=1, source_target_pairs={{0,1},{1,0},{2,3},{3,2},{4,5},{5,4},{6,7},{7,6},{8,9},{9,8},{10,11... | collective-permute-start | bytes 393224 | tf_op jit(solution)/shard_map/ppermute | solution.py:19
  16.4 3.5 %collective-permute-start.8 = (bf16[4,128,128]{2,1,0:T(8,128)(2,1)S(1)}, bf16[4,128,128]{2,1,0:T(8,128)(2,1)S(1)}, u32[]{:S(2)}, u32[]{:S(2)}) collective-permute-start(bf16[4,128,128]{2,1,0:T(8,128)(2,1)S(1)} %pad_maximum_fusion.4), channel_id=1, source_target_pairs={{0,4},{4,0},{8,12},{12,8},{1,5},{5,1},{9,13},{13,9},{2,6},{6,2},{1... | collective-permute-start | bytes 393224 | tf_op jit(solution)/shard_map/ppermute | solution.py:19
  17.6 7.6 %collective-permute-start.2 = (bf16[3,128,128]{2,1,0:T(8,128)(2,1)S(1)}, bf16[3,128,128]{2,1,0:T(8,128)(2,1)S(1)}, u32[]{:S(2)}, u32[]{:S(2)}) collective-permute-start(bf16[3,128,128]{2,1,0:T(8,128)(2,1)S(1)} %add.10), channel_id=1, source_target_pairs={{0,1},{1,0},{2,3},{3,2},{4,5},{5,4},{6,7},{7,6},{8,9},{9,8},{10,11... | collective-permute-start | bytes 294920 | tf_op jit(solution)/shard_map/ppermute | solution.py:19
  20.2 9.6 %collective-permute-start.9 = (bf16[3,128,128]{2,1,0:T(8,128)(2,1)S(1)}, bf16[3,128,128]{2,1,0:T(8,128)(2,1)S(1)}, u32[]{:S(2)}, u32[]{:S(2)}) collective-permute-start(bf16[3,128,128]{2,1,0:T(8,128)(2,1)S(1)} %get-tuple-element.26), channel_id=1, source_target_pairs={{0,2},{1,3},{2,0},{3,1},{4,6},{5,7},{6,4},{7,5},{8,10},{9,11},{10,... | collective-permute-start | bytes 294920 | tf_op jit(solution)/shard_map/ppermute | solution.py:19
  23.1 6.7 %collective-permute-start.10 = (bf16[3,128,128]{2,1,0:T(8,128)(2,1)S(1)}, bf16[3,128,128]{2,1,0:T(8,128)(2,1)S(1)}, u32[]{:S(2)}, u32[]{:S(2)}) collective-permute-start(bf16[3,128,128]{2,1,0:T(8,128)(2,1)S(1)} %get-tuple-element.26), channel_id=1, source_target_pairs={{0,1},{1,0},{2,3},{3,2},{4,5},{5,4},{6,7},{7,6},{8,9},{9,8},{10,11... | collective-permute-start | bytes 294920 | tf_op jit(solution)/shard_map/ppermute | solution.py:19
  23.1 7.4 %collective-permute-start.11 = (bf16[3,128,128]{2,1,0:T(8,128)(2,1)S(1)}, bf16[3,128,128]{2,1,0:T(8,128)(2,1)S(1)}, u32[]{:S(2)}, u32[]{:S(2)}) collective-permute-start(bf16[3,128,128]{2,1,0:T(8,128)(2,1)S(1)} %get-tuple-element.26), channel_id=1, source_target_pairs={{0,3},{1,2},{2,1},{3,0},{4,7},{5,6},{6,5},{7,4},{8,11},{9,10},{10,... | collective-permute-start | bytes 294920 | tf_op jit(solution)/shard_map/ppermute | solution.py:19
  25.4 4.3 %collective-permute-start.3 = (bf16[2,128,128]{2,1,0:T(8,128)(2,1)S(1)}, bf16[2,128,128]{2,1,0:T(8,128)(2,1)S(1)}, u32[]{:S(2)}, u32[]{:S(2)}) collective-permute-start(bf16[2,128,128]{2,1,0:T(8,128)(2,1)S(1)} %get-tuple-element.18.solved_ref), channel_id=1, source_target_pairs={{0,8},{4,12},{8,0},{12,4},{1,9},{5,13},{9,1},{13,5},{2,10},{6,14},... | collective-permute-start | bytes 196616 | tf_op jit(solution)/shard_map/ppermute | solution.py:19
  26.9 6.3 %collective-permute-start.14 = (bf16[1,128,128]{2,1,0:T(8,128)(2,1)S(1)}, bf16[1,128,128]{2,1,0:T(8,128)(2,1)S(1)}, u32[]{:S(2)}, u32[]{:S(2)}) collective-permute-start(bf16[1,128,128]{2,1,0:T(8,128)(2,1)S(1)} %get-tuple-element.28), channel_id=1, source_target_pairs={{0,2},{1,3},{2,0},{3,1},{4,6},{5,7},{6,4},{7,5},{8,10},{9,11},{10,... | collective-permute-start | bytes 98312 | tf_op jit(solution)/shard_map/ppermute | solution.py:19
  29.7 1.4 %collective-permute-start.4 = (bf16[4,128,128]{2,1,0:T(8,128)(2,1)S(1)}, bf16[4,128,128]{2,1,0:T(8,128)(2,1)S(1)}, u32[]{:S(2)}, u32[]{:S(2)}) collective-permute-start(bf16[4,128,128]{2,1,0:T(8,128)(2,1)S(1)} %pad_maximum_fusion.2), channel_id=1, source_target_pairs={{0,4},{4,0},{8,12},{12,8},{1,5},{5,1},{9,13},{13,9},{2,6},{6,2},{1... | collective-permute-start | bytes 393224 | tf_op jit(solution)/shard_map/ppermute | solution.py:19
  31.7 6.0 %copy-start.3 = (bf16[1,1,1,1024,384]{4,3,2,1,0:T(8,128)(2,1)S(1)}, bf16[1,1,1,1024,384]{4,3,2,1,0:T(8,128)(2,1)}, u32[]{:S(2)}) copy-start(bf16[1,1,1,1024,384]{4,3,2,1,0:T(8,128)(2,1)} %param.13) | copy-start | bytes 2359300
  31.7 4.3 %collective-permute-start.12 = (bf16[2,128,128]{2,1,0:T(8,128)(2,1)S(1)}, bf16[2,128,128]{2,1,0:T(8,128)(2,1)S(1)}, u32[]{:S(2)}, u32[]{:S(2)}) collective-permute-start(bf16[2,128,128]{2,1,0:T(8,128)(2,1)S(1)} %shard_map.90), channel_id=1, source_target_pairs={{0,8},{4,12},{8,0},{12,4},{1,9},{5,13},{9,1},{13,5},{2,10},{6,14},... | collective-permute-start | bytes 196616 | tf_op jit(solution)/shard_map/ppermute | solution.py:19
  33.3 4.3 %collective-permute-start.15 = (bf16[2,128,128]{2,1,0:T(8,128)(2,1)S(1)}, bf16[2,128,128]{2,1,0:T(8,128)(2,1)S(1)}, u32[]{:S(2)}, u32[]{:S(2)}) collective-permute-start(bf16[2,128,128]{2,1,0:T(8,128)(2,1)S(1)} %pad_maximum_fusion.7), channel_id=1, source_target_pairs={{0,1},{1,0},{2,3},{3,2},{4,5},{5,4},{6,7},{7,6},{8,9},{9,8},{10,11... | collective-permute-start | bytes 196616 | tf_op jit(solution)/shard_map/ppermute | solution.py:19
  36.0 1.6 %collective-permute-start.13 = (bf16[4,128,128]{2,1,0:T(8,128)(2,1)S(1)}, bf16[4,128,128]{2,1,0:T(8,128)(2,1)S(1)}, u32[]{:S(2)}, u32[]{:S(2)}) collective-permute-start(bf16[4,128,128]{2,1,0:T(8,128)(2,1)S(1)} %pad_maximum_fusion.5), channel_id=1, source_target_pairs={{0,4},{4,0},{8,12},{12,8},{1,5},{5,1},{9,13},{13,9},{2,6},{6,2},{1... | collective-permute-start | bytes 393224 | tf_op jit(solution)/shard_map/ppermute | solution.py:19
